TPU v7x, 32 devices: a whole 2x2x4 slice. The times are simulated.
32 devices in a mesh: shell: 4 (over x, core), blk: 8 (over z, y).
Axes of the slice: x: 2, y: 2, z: 4, core: 2. Of those that a mesh axis runs over, the one named last changes fastest.
Arguments:
- strain_spec: bfloat16 [6, 4, 1024, 2, 1024], P(None, 'shell', 'blk'), may hold values from -6 to 6
- order_map: int32 [1024], replicated, may hold values from 0 to 1023, as said below
- viscosity: float32 [4, 1024, 2048], P('shell', 'blk'), may hold values from 0.2 to 5
- radial_weight: float32 [4], P('shell'), may hold values from 0.3 to 3
Outputs:
- stress_spec: bfloat16 [6, 4, 1024, 2, 1024], P(None, 'shell', 'blk')
- integrated: float32 [6, 1024, 2, 1024], P(None, 'blk', None, 'shell')
Inputs may be any that keep to these rules, and one draw needn't show every extreme that they name: order_map is a permutation of the orders 0 to 1023; the entries 2i and 2i + 1 hold two orders m and 1023 - m, in either order, so each device's 128 slots hold 64 such pairs.
All inputs are finite; a program needn't handle non-finite values.
Results may differ from a plain program's by a relative error of at most 0.014.
Values may be sent and summed in bfloat16 or wider, within the bound.
No kernel may reach another device: no remote copies, remote signals or barrier semaphores. Data moves between devices by JAX's collectives and lax.ppermute only.
A program may use at most 256 MiB of HBM per device.

v0:
```python
import math

import jax
import jax.numpy as jnp
from jax import lax
from jax.sharding import PartitionSpec as P

two_power = 1099511627776.0
inverse_power = 1.0 / 1099511627776.0
log_jump = 40.0 * math.log(2.0)


def cycle_geometry(cycle_count):
    cycle_index = jnp.arange(cycle_count // 2, dtype=jnp.float32)
    colatitude = math.pi * (2.0 * cycle_index + 1.0) / (2.0 * cycle_count)
    return (jnp.cos(colatitude), jnp.log(jnp.sin(colatitude)))


def fejer_weights(cycle_count):
    half_count = cycle_count // 2
    cycle_index = jnp.arange(half_count, dtype=jnp.int32)
    wave_number = jnp.arange(1, half_count + 1, dtype=jnp.int32)
    phase_index = wave_number[:, None] * (2 * cycle_index[None, :] + 1) % (2 * cycle_count)
    angles = phase_index.astype(jnp.float32) * (math.pi / cycle_count)
    wave_float = wave_number.astype(jnp.float32)
    divisor = 4.0 * wave_float * wave_float - 1.0
    series = jnp.sum(jnp.cos(angles) / divisor[:, None], axis=0)
    return 2.0 / cycle_count * (1.0 - 2.0 * series)


def legendre_tables(orders, cycle_count, degree_count):
    cosine, log_sine = cycle_geometry(cycle_count)
    order_int = orders[:, None]
    order_float = orders.astype(jnp.float32)[:, None]
    counter = jnp.arange(1, degree_count, dtype=jnp.int32)
    counter_float = counter.astype(jnp.float32)
    factors = jnp.where(
        counter[None, :] <= order_int, jnp.log(1.0 - 0.5 / counter_float)[None, :], 0.0
    )
    log_start = (
        0.5 * jnp.log((2.0 * order_float + 1.0) / (4.0 * math.pi))
        + 0.5 * jnp.sum(factors, axis=1, keepdims=True)
        + order_float * log_sine[None, :]
    )
    even_first = order_int % 2 == 0

    def advance(carry_state, degree):
        previous, latest, log_scale = carry_state
        degree_float = degree.astype(jnp.float32)
        below_float = degree_float - 1.0
        coef_first = jnp.sqrt(
            jnp.maximum(4.0 * degree_float * degree_float - 1.0, 0.0)
            / jnp.maximum(degree_float * degree_float - order_float * order_float, 1.0)
        )
        coef_second = jnp.sqrt(
            jnp.maximum(below_float * below_float - order_float * order_float, 0.0)
            / jnp.maximum(4.0 * below_float * below_float - 1.0, 1.0)
        )
        current = coef_first * (cosine[None, :] * latest - coef_second * previous)
        current = jnp.where(
            degree == order_int + 1,
            jnp.sqrt(2.0 * order_float + 3.0) * cosine[None, :] * latest,
            current,
        )
        current = jnp.where(degree == order_int, 1.0, current)
        current = jnp.where(degree < order_int, 0.0, current)
        result = current * jnp.exp(log_scale)
        too_large = jnp.abs(current) > two_power
        factor = jnp.where(too_large, inverse_power, 1.0)
        next_state = (
            latest * factor,
            current * factor,
            log_scale + jnp.where(too_large, log_jump, 0.0),
        )
        return (next_state, result)

    def pair_step(carry_state, half_degree):
        carry_state, lower_row = advance(carry_state, 2 * half_degree)
        carry_state, upper_row = advance(carry_state, 2 * half_degree + 1)
        even_row = jnp.where(even_first, lower_row, upper_row).astype(jnp.bfloat16)
        odd_row = jnp.where(even_first, upper_row, lower_row).astype(jnp.bfloat16)
        return (carry_state, (even_row, odd_row))

    zero_rows = jnp.zeros((orders.shape[0], cycle_count // 2), jnp.float32)
    initial = (zero_rows, zero_rows, log_start)
    final_state, tables = lax.scan(
        pair_step, initial, jnp.arange(degree_count // 2, dtype=jnp.int32), unroll=32
    )
    return tables


def fourier_table(orders_all, point_count):
    longitudes = jnp.arange(point_count, dtype=jnp.int32)
    phase_index = orders_all[:, None] * longitudes[None, :] % point_count
    angles = phase_index.astype(jnp.float32) * (2.0 * math.pi / point_count)
    return jnp.stack([jnp.cos(angles), -jnp.sin(angles)], axis=1).astype(jnp.bfloat16)


def synthesize(spectra, tables, orders):
    even_first = (orders % 2 == 0)[None, None, :, None, None]
    paired = spectra.reshape(spectra.shape[:-1] + (spectra.shape[-1] // 2, 2))
    even_part = jnp.where(even_first, paired[..., 0], paired[..., 1])
    odd_part = jnp.where(even_first, paired[..., 1], paired[..., 0])
    symmetric = jnp.einsum(
        "csmri,imj->csmrj", even_part, tables[0], preferred_element_type=jnp.float32
    )
    antisymmetric = jnp.einsum(
        "csmri,imj->csmrj", odd_part, tables[1], preferred_element_type=jnp.float32
    )
    north_side = symmetric + antisymmetric
    south_side = symmetric - antisymmetric
    return jnp.concatenate([north_side, jnp.flip(south_side, axis=-1)], axis=-1).astype(
        jnp.bfloat16
    )


def analyze(gridded, tables, orders, weights):
    half_count = gridded.shape[-1] // 2
    north_side = gridded[..., :half_count].astype(jnp.float32)
    south_side = jnp.flip(gridded[..., half_count:], axis=-1).astype(jnp.float32)
    even_side = (weights * (north_side + south_side)).astype(jnp.bfloat16)
    odd_side = (weights * (north_side - south_side)).astype(jnp.bfloat16)
    even_part = jnp.einsum(
        "csmrj,imj->csmri", even_side, tables[0], preferred_element_type=jnp.float32
    )
    odd_part = jnp.einsum(
        "csmrj,imj->csmri", odd_side, tables[1], preferred_element_type=jnp.float32
    )
    even_first = (orders % 2 == 0)[None, None, :, None, None]
    low_side = jnp.where(even_first, even_part, odd_part)
    high_side = jnp.where(even_first, odd_part, even_part)
    stacked = jnp.stack([low_side, high_side], axis=-1)
    return stacked.reshape(stacked.shape[:-2] + (2 * stacked.shape[-2],))


def shards(strain_spec, order_map, viscosity, radial_weight):
    component_count, shell_count, order_count, complex_parts, degree_count = strain_spec.shape
    block_count = lax.axis_size("blk")
    cycle_local = viscosity.shape[1]
    cycle_count = cycle_local * block_count
    point_count = viscosity.shape[2]
    my_orders = lax.dynamic_slice_in_dim(
        order_map, lax.axis_index("blk") * order_count, order_count
    )
    tables = legendre_tables(my_orders, cycle_count, degree_count)
    weights = fejer_weights(cycle_count)
    wave_table = fourier_table(order_map, point_count).reshape(
        block_count, order_count, 2, point_count
    )
    doubling = (
        jnp.where(order_map == 0, 1.0, 2.0).astype(jnp.bfloat16).reshape(block_count, order_count)
    )
    norm_factor = 2.0 * math.pi / point_count
    gridded = synthesize(strain_spec, tables, my_orders)
    item_count = gridded.shape[0]
    pieces = gridded.reshape(item_count, shell_count, order_count, 2, block_count, cycle_local)
    outgoing = pieces.transpose(0, 1, 4, 2, 3, 5).reshape(
        item_count, shell_count, block_count, order_count * 2 * cycle_local
    )
    received = lax.all_to_all(outgoing, "blk", split_axis=2, concat_axis=2, tiled=True)
    item_count = received.shape[0]
    blocks = received.reshape(item_count, shell_count, block_count, order_count, 2, cycle_local)
    blocks = blocks * doubling[None, None, :, :, None, None]
    grid_field = jnp.einsum(
        "csdxrj,dxrk->csjk", blocks, wave_table, preferred_element_type=jnp.float32
    )
    stress = (viscosity[None] * grid_field).astype(jnp.bfloat16)
    spectra = jnp.einsum(
        "csjk,dxrk->csdxrj", stress, wave_table, preferred_element_type=jnp.float32
    )
    spectra = (spectra * norm_factor).astype(jnp.bfloat16)
    returned = lax.all_to_all(
        spectra.reshape(item_count, shell_count, block_count, order_count * 2 * cycle_local),
        "blk",
        split_axis=2,
        concat_axis=2,
        tiled=True,
    )
    item_count = returned.shape[0]
    pieces = returned.reshape(item_count, shell_count, block_count, order_count, 2, cycle_local)
    coefficient = analyze(
        pieces.transpose(0, 1, 3, 4, 2, 5).reshape(
            item_count, shell_count, order_count, 2, cycle_count
        ),
        tables,
        my_orders,
        weights,
    )
    stress_spec = coefficient.astype(jnp.bfloat16)
    weighted = jnp.sum(coefficient * radial_weight[None, :, None, None, None], axis=1)
    summed = lax.psum(weighted.astype(jnp.bfloat16), "shell").astype(jnp.float32)
    share_size = degree_count // lax.axis_size("shell")
    integrated = lax.dynamic_slice_in_dim(
        summed, lax.axis_index("shell") * share_size, share_size, 3
    )
    return (stress_spec, integrated)


def solution(mesh):
    return jax.shard_map(
        shards,
        mesh=mesh,
        in_specs=(P(None, "shell", "blk", None, None), P(), P("shell", "blk", None), P("shell")),
        out_specs=(P(None, "shell", "blk", None, None), P(None, "blk", None, "shell")),
        check_vma=False,
    )
```

profile of v0, /device:TPU:0, one launch (start us, length us, event | category | flops | bytes accessed | tf_op | source)
XLA Modules:
  0.0 1825.7 jit_solution(7984311997705848446)
XLA Ops:
  8.4 1116.1 %while.23 = (s32[]{:T(128)}, f32[128,512]{1,0:T(8,128)S(1)}, f32[128,512]{1,0:T(8,128)S(1)}, f32[128,512]{1,0:T(8,128)S(1)}, bf16[16,32,128,512]{3,2,1,0:T(8,128...) while((s32[]{:T(128)}, f32[128,512]{1,0:T(8,128)S(1)}, ...), condition=%wide.region_2.3_spmd.clone.clone, body=%wide.region_1.2_spmd.clone.clone.sunk | while | flops 94841296 | bytes 77886000 | solution.py:86
  140.0 7.7 bitcast_dynamic-update-slice_fusion.3
  209.7 7.8 bitcast_dynamic-update-slice_fusion.3
  349.2 7.7 bitcast_dynamic-update-slice_fusion.3
  418.9 7.7 bitcast_dynamic-update-slice_fusion.3
  488.7 7.8 bitcast_dynamic-update-slice_fusion.3
  628.1 7.8 bitcast_dynamic-update-slice_fusion.3
  767.6 7.8 bitcast_dynamic-update-slice_fusion.3
  907.1 7.8 bitcast_dynamic-update-slice_fusion.3
  1046.5 7.8 bitcast_dynamic-update-slice_fusion.3
  1137.6 8.3 copy.163
  1153.1 60.0 %fusion.453 = f32[128,512,6,2]{1,2,3,0:T(8,128)S(1)} fusion(bf16[512,128,512,1]{2,1,0,3:T(8,128)(2,1)} %bitcast.5, bf16[6,128,2,512]{3,1,2,0:T(8,128)(2,1)S(1)} %get-tuple-element.1375), kind=kOutput, calls=%fused_computation.1291 | convolution fusion | flops 805306368 | bytes 71827456 | tf_op jit(solution)/shard_map/csmri,imj->csmrj/dot_general | solution.py:104
  1213.0 60.1 %fusion.451 = f32[128,512,6,2]{1,2,3,0:T(8,128)S(1)} fusion(bf16[512,128,512,1]{2,1,0,3:T(8,128)(2,1)} %bitcast.14, bf16[6,128,2,512]{3,1,2,0:T(8,128)(2,1)S(1)} %get-tuple-element.1376), kind=kOutput, calls=%fused_computation.1289 | convolution fusion | flops 805306368 | bytes 71827456 | tf_op jit(solution)/shard_map/csmri,imj->csmrj/dot_general | solution.py:107
  1281.8 20.7 %rev.8 = bf16[6,1,128,2,512]{4,2,3,1,0:T(8,128)(2,1)S(1)} reverse(bf16[6,1,128,2,512]{4,2,3,1,0:T(8,128)(2,1)} %fusion.476), dimensions={4} | reverse | bytes 3145728 | tf_op jit(solution)/shard_map/jit(_flip)/rev | solution.py:112
  1325.5 35.4 %cosine_convert_fusion = (bf16[8,128,1,2048]{3,0,1,2:T(8,128)(2,1)S(1)}, bf16[8,128,1,2048]{3,0,1,2:T(8,128)(2,1)}) fusion(s32[8,128]{0,1:T(8,128)S(1)} %copy.161), kind=kLoop, calls=%fused_computation.1305 | loop fusion | flops 35651584 | bytes 8392704 | tf_op jit(solution)/shard_map/convert.6
  1369.3 49.4 %all-to-all-done = bf16[6,1,8,32768]{3,0,1,2:T(8,128)(2,1)} async-done(((bf16[6,1,8,32768]{3,0,1,2:T(8,128)(2,1)}), bf16[6,1,8,32768]{3,0,1,2:T(8,128)(2,1)}, u32[]{:S(2)}, u32[]{:S(2)}) %all-to-all-start) | async-done | bytes 3145760 | tf_op jit(solution)/shard_map/all_to_all | solution.py:160
  1429.0 14.6 fusion.465
  1443.7 16.4 fusion.471
  1476.9 87.2 %all-to-all-done.1 = bf16[6,1,8,32768]{3,0,1,2:T(8,128)(2,1)} async-done(((bf16[6,1,8,32768]{3,0,1,2:T(8,128)(2,1)}), bf16[6,1,8,32768]{3,0,1,2:T(8,128)(2,1)}, u32[]{:S(2)}, u32[]{:S(2)}) %all-to-all-start.1) | async-done | bytes 3145760 | tf_op jit(solution)/shard_map/all_to_all | solution.py:172
  1582.7 23.0 %rev.9 = bf16[6,1,128,2,512]{2,4,3,0,1:T(8,128)(2,1)} reverse(bf16[6,1,128,2,512]{2,4,3,0,1:T(8,128)(2,1)} %slice.341), dimensions={4} | reverse | bytes 3145728 | tf_op jit(solution)/shard_map/jit(_flip)/rev | solution.py:120
  1614.2 57.3 %fusion.455 = f32[128,512,6,2]{1,2,3,0:T(8,128)} fusion(bf16[6,128,2,512]{3,0,2,1:T(8,128)(2,1)} %copy.183, bf16[512,128,512,1]{2,1,0,3:T(8,128)(2,1)} %bitcast.5), kind=kOutput, calls=%fused_computation.1293 | convolution fusion | flops 805306368 | bytes 71827456 | tf_op jit(solution)/shard_map/csmrj,imj->csmri/dot_general | solution.py:123
  1674.4 56.7 %fusion.449 = f32[128,512,6,2]{1,2,3,0:T(8,128)S(1)} fusion(bf16[6,128,2,512]{3,0,2,1:T(8,128)(2,1)} %copy.186, bf16[512,128,512,1]{2,1,0,3:T(8,128)(2,1)} %bitcast.14), kind=kOutput, calls=%fused_computation.1287 | convolution fusion | flops 805306368 | bytes 71827456 | tf_op jit(solution)/shard_map/csmrj,imj->csmri/dot_general | solution.py:126
  1738.8 8.7 copy.190
  1764.1 51.0 %all-reduce.2.cloned.1.call-done = bf16[6,128,2,1024]{1,3,2,0:T(8,128)(2,1)} async-done(((bf16[6,128,2,1024]{1,3,2,0:T(8,128)(2,1)}), bf16[6,128,2,1024]{1,3,2,0:T(8,128)(2,1)}) %all-reduce.2.cloned.1.call-update) | async-done | bytes 3145744 | tf_op jit(solution)/shard_map/psum | solution.py:191
  (1013 shorter events, 864.7 us)
Async XLA Ops:
  1124.5 26.4 %copy-start.3 = (pred[128,1]{0,1:T(4,128)(4,1)}, pred[128,1]{0,1:T(4,128)(4,1)S(1)}, u32[]{:S(2)}) copy-start(pred[128,1]{0,1:T(4,128)(4,1)S(1)} %get-tuple-element.2543) | copy-start | bytes 388
  1137.6 8.3 copy-start.5
  1281.8 22.3 %copy-start.7 = (bf16[6,1,128,2,512]{2,4,3,0,1:T(8,128)(2,1)S(1)}, bf16[6,1,128,2,512]{2,4,3,0,1:T(8,128)(2,1)}, u32[]{:S(2)}) copy-start(bf16[6,1,128,2,512]{2,4,3,0,1:T(8,128)(2,1)} %copy.169) | copy-start | bytes 4718596
  1318.0 7.4 copy-start.9
  1318.0 100.7 %all-to-all-start = ((bf16[6,1,8,32768]{3,0,1,2:T(8,128)(2,1)}), bf16[6,1,8,32768]{3,0,1,2:T(8,128)(2,1)}, u32[]{:S(2)}, u32[]{:S(2)}) async-start(bf16[6,1,8,32768]{3,0,1,2:T(8,128)(2,1)} %reshape.4510), calls=%async_computation | async-start | bytes 8388608 | tf_op jit(solution)/shard_map/all_to_all | solution.py:160
  1361.0 2.0 copy-start.1
  1424.5 4.5 copy-start.2
  1424.5 19.2 %slice-start = ((s8[8388608]{0:T(1024)(128)(4,1)}), s8[4194304]{0:T(1024)(128)(4,1)S(1)}, s32[]{:S(2)}) async-start(s8[8388608]{0:T(1024)(128)(4,1)} %bitcast.1251), calls=%async_computation.3 | async-start | bytes 8388608
  1429.0 14.7 slice-start.1
  1467.0 97.1 %all-to-all-start.1 = ((bf16[6,1,8,32768]{3,0,1,2:T(8,128)(2,1)}), bf16[6,1,8,32768]{3,0,1,2:T(8,128)(2,1)}, u32[]{:S(2)}, u32[]{:S(2)}) async-start(bf16[6,1,8,32768]{3,0,1,2:T(8,128)(2,1)} %reshape.4512), calls=%async_computation.1 | async-start | bytes 8388608 | tf_op jit(solution)/shard_map/all_to_all | solution.py:172
  1471.6 343.6 %all-reduce.2.cloned.1.call-start = ((), (), s32[]{:S(2)}) async-start(), calls=%async_computation.2 | async-start | bytes 6291456 | tf_op jit(solution)/shard_map/psum | solution.py:191
  1614.2 57.3 %copy-start.6 = (bf16[6,128,2,512]{1,3,2,0:T(8,128)(2,1)S(1)}, bf16[6,128,2,512]{1,3,2,0:T(8,128)(2,1)}, u32[]{:S(2)}) copy-start(bf16[6,128,2,512]{1,3,2,0:T(8,128)(2,1)} %get-tuple-element.1374) | copy-start | bytes 4718596
  1674.4 56.7 %copy-start.4 = (pred[128,1]{0,1:T(4,128)(4,1)S(1)}, pred[128,1]{0,1:T(4,128)(4,1)}, u32[]{:S(2)}) copy-start(pred[128,1]{0,1:T(4,128)(4,1)} %copy-done.3) | copy-start | bytes 388
  1674.4 56.7 %copy-start.8 = (f32[128,512,6,2]{1,2,3,0:T(8,128)S(1)}, f32[128,512,6,2]{1,2,3,0:T(8,128)}, u32[]{:S(2)}) copy-start(f32[128,512,6,2]{1,2,3,0:T(8,128)} %fusion.455) | copy-start | bytes 9437188
  1734.5 1.7 copy-start
Sparse Core Ops, SparseCore 0:
  1747.6 67.4 all-reduce.1
where the time goes:
time: 1850 us; the launch traced here: 1830 us
  other arithmetic  721 us (39%)
  loops' own time  327 us (18%)
  local copies, waits for them, and re-layouts  298 us (16%)
  matrix products  265 us (14%)
  waiting for transfers between devices  188 us (10%)
    while x496, other arithmetic  597 us
    another operation x1, loops' own time, legendre_tables(): lax.scan(pair_step, initial, jnp.arange(degree_count // 2, dtype=jnp.int3...  327 us
    dynamic_update_slice x16, local copies, waits for them, and re-layouts, legendre_tables(): lax.scan(pair_step, initial, jnp.arange(degree_count // 2, dtype=jnp.int3...  124 us
    all_to_all x1, waiting for transfers between devices, shards(): lax.all_to_all(spectra.reshape(item_count, shell_count, block_count, orde...  87.2 us
    dot_general x1, matrix products, synthesize(): jnp.einsum('csmri,imj->csmrj', odd_part, tables[1], preferred_element_typ...  60.1 us
    dot_general x1, matrix products, synthesize(): jnp.einsum('csmri,imj->csmrj', even_part, tables[0], preferred_element_ty...  60 us
    dot_general x1, matrix products, analyze(): jnp.einsum('csmrj,imj->csmri', even_side, tables[0], preferred_element_ty...  57.3 us
    dot_general x1, matrix products, analyze(): jnp.einsum('csmrj,imj->csmri', odd_side, tables[1], preferred_element_typ...  56.7 us
  transfers between devices with their start and end apart: 3, of which 3 were waited for; matrix products, arithmetic and copies ran while one was open for 3% of the time, Pallas kernels for 0%

commit v1 on v0

v1 whole, which is shorter than its diff:
```python
import functools
import math

import jax
import jax.numpy as jnp
from jax import lax
from jax.experimental import pallas as pl
from jax.experimental.pallas import tpu as pltpu
from jax.sharding import PartitionSpec as P

two_power = 1099511627776.0
inverse_power = 1.0 / 1099511627776.0
log_jump = 40.0 * math.log(2.0)

ORD = 8
CHUNK = 64
BLOCK = 16
LANES = 128
VMEM_LIMIT = 56 * 1024 * 1024


def fejer_weights(cycle_count):
    half_count = cycle_count // 2
    cycle_index = jnp.arange(half_count, dtype=jnp.int32)
    wave_number = jnp.arange(1, half_count + 1, dtype=jnp.int32)
    phase_index = wave_number[:, None] * (2 * cycle_index[None, :] + 1) % (2 * cycle_count)
    angles = phase_index.astype(jnp.float32) * (math.pi / cycle_count)
    wave_float = wave_number.astype(jnp.float32)
    divisor = 4.0 * wave_float * wave_float - 1.0
    series = jnp.sum(jnp.cos(angles) / divisor[:, None], axis=0)
    return 2.0 / cycle_count * (1.0 - 2.0 * series)


def rank_orders(orders):
    top = orders.shape[-1]
    key = orders + (orders % 2) * (1 << 20)
    return jnp.sum((key[..., None, :] < key[..., :, None]).astype(jnp.int32), axis=-1)


def apply_rank(values, rank):
    count = rank.shape[-1]
    place = jnp.arange(count, dtype=jnp.int32)
    hit = rank[..., :, None] == place
    return jnp.sum(jnp.where(hit, values[..., :, None], 0), axis=-2)


def recursion_coefficients(sorted_orders, degree_count):
    groups = sorted_orders.shape[0] // ORD
    chunks = degree_count // CHUNK
    order = sorted_orders.astype(jnp.float32).reshape(groups, ORD, 1)
    degree = jnp.arange(degree_count, dtype=jnp.float32)[None, None, :]
    below = degree - 1.0
    coef = 4.0 * (below * below - order * order) / (4.0 * below * below - 1.0)
    coef = coef.reshape(groups, ORD, chunks, CHUNK).transpose(0, 2, 1, 3)
    gap = jnp.maximum(degree * degree - order * order, 1.0)
    ratio = jnp.where(degree > order, jnp.sqrt((degree * degree - 0.25) / gap), 1.0)
    kappa = ratio.reshape(groups, ORD, degree_count // BLOCK, BLOCK)
    step = 1
    while step < BLOCK:
        shifted = jnp.pad(kappa[..., :-step], ((0, 0),) * 3 + ((step, 0),), constant_values=1.0)
        kappa = kappa * shifted
        step *= 2
    ends = kappa[..., -1].reshape(groups, ORD, chunks, CHUNK // BLOCK).transpose(0, 2, 1, 3)
    lanes = kappa.reshape(groups, ORD, chunks, CHUNK // 2, 2).transpose(0, 2, 4, 3, 1)
    lanes = lanes.reshape(groups * chunks, CHUNK * ORD)
    counter = jnp.arange(1, degree_count, dtype=jnp.float32)
    logs = jnp.where(counter <= order, jnp.log(1.0 - 0.5 / counter), 0.0)
    start = 0.5 * jnp.log((2.0 * order + 1.0) / (4.0 * math.pi)) + 0.5 * jnp.sum(
        logs, axis=-1, keepdims=True
    )
    extra = jnp.concatenate([order, start], axis=-1)[:, None]
    extra = jnp.broadcast_to(extra, (groups, chunks, ORD, 2))
    used = CHUNK + CHUNK // BLOCK + 2
    fill = jnp.zeros((groups, chunks, ORD, LANES - used), jnp.float32)
    table = jnp.concatenate([coef, ends, extra, fill], axis=-1)
    return table.reshape(groups * chunks, ORD, LANES), lanes


def work_items(sorted_orders, degree_count):
    groups = sorted_orders.shape[0] // ORD
    chunks = degree_count // CHUNK
    first = sorted_orders.reshape(groups, ORD)[:, 0] // CHUNK
    count = chunks - first
    index = jnp.arange(groups, dtype=jnp.int32)
    upto = jnp.sum(jnp.where(index[None, :] <= index[:, None], count[None, :], 0), axis=1)
    item = jnp.arange(groups * chunks, dtype=jnp.int32)
    group = jnp.sum((item[:, None] >= upto[None, :]).astype(jnp.int32), axis=1)
    group = jnp.minimum(group, groups - 1)
    hit = group[:, None] == index[None, :]
    offset = jnp.sum(jnp.where(hit, (upto - count)[None, :], 0), axis=1)
    begin = jnp.sum(jnp.where(hit, first[None, :], 0), axis=1)
    chunk = item - offset + begin
    start = (chunk == begin).astype(jnp.int32)
    return group, jnp.minimum(chunk, chunks - 1), start, upto[-1:]


def spread_matrix():
    place = jnp.arange(CHUNK * ORD, dtype=jnp.int32)
    parity = place // (CHUNK * ORD // 2)
    degree = 2 * (place % (CHUNK * ORD // 2) // ORD) + parity
    half = jnp.arange(LANES // CHUNK, dtype=jnp.int32)[:, None, None]
    row = jnp.arange(LANES, dtype=jnp.int32)[None, :, None]
    return (row - CHUNK * half == degree[None, None, :]).astype(jnp.bfloat16)


def order_mask(kappa_row):
    shape = (2 * ORD, CHUNK * ORD)
    row_order = lax.broadcasted_iota(jnp.int32, shape, 0) // 2
    lane_order = lax.broadcasted_iota(jnp.int32, shape, 1) % ORD
    return jnp.where(row_order == lane_order, kappa_row, 0.0)


def synth_kernel(
    comps,
    groups,
    chunks,
    group_ref,
    chunk_ref,
    start_ref,
    count_ref,
    spec_ref,
    place_ref,
    coef_ref,
    kappa_ref,
    spread_ref,
    geometry_ref,
    out_ref,
    table_ref,
    sorted_ref,
    even_ref,
    odd_ref,
    prev_ref,
    last_ref,
    log_ref,
    buffer_ref,
    sems,
):
    rows = 2 * ORD
    half = CHUNK * ORD // 2
    lane_blocks = geometry_ref.shape[1] // LANES
    for c in range(comps):
        moved = jnp.dot(place_ref[...], spec_ref[c], preferred_element_type=jnp.float32)
        sorted_ref[c] = moved.astype(jnp.bfloat16)
    count = count_ref[0]

    def table_copy(item, slot):
        return pltpu.make_async_copy(buffer_ref.at[slot], table_ref.at[item], sems.at[slot])

    def body(item, carry):
        group = group_ref[item]
        chunk = chunk_ref[item]
        slot = lax.rem(item, 2)
        place = group * chunks + chunk

        @pl.when(start_ref[item] == 1)
        def _():
            even_ref[...] = jnp.zeros_like(even_ref)
            odd_ref[...] = jnp.zeros_like(odd_ref)
            prev_ref[...] = jnp.zeros_like(prev_ref)
            last_ref[...] = jnp.zeros_like(last_ref)
            head = coef_ref[place]
            order = head[:, CHUNK + CHUNK // BLOCK : CHUNK + CHUNK // BLOCK + 1]
            start = head[:, CHUNK + CHUNK // BLOCK + 1 : CHUNK + CHUNK // BLOCK + 2]
            log_ref[...] = start + order * geometry_ref[1:2, :]

        @pl.when(item >= 2)
        def _():
            table_copy(item - 2, slot).wait()

        coefs = coef_ref[place]
        order_at = CHUNK + CHUNK // BLOCK
        order = coefs[:, order_at : order_at + 1]
        seed_at = order - (chunk * CHUNK).astype(jnp.float32)
        twice = geometry_ref[0:1, :]
        prev = prev_ref[...]
        last = last_ref[...]
        logs = log_ref[...]
        for b in range(CHUNK // BLOCK):
            scale = jnp.exp(logs)
            held = []
            for i in range(BLOCK):
                step = b * BLOCK + i
                now = twice * last - coefs[:, step : step + 1] * prev
                now = jnp.where(seed_at == float(step), 1.0, now)
                held.append(now * scale)
                prev, last = last, now
            for p in range(2):
                for i in range(p, BLOCK, 4):
                    pair = jnp.concatenate([held[i], held[i + 2]], axis=0).astype(jnp.bfloat16)
                    at = (b * BLOCK + i - p) // 2 * ORD
                    buffer_ref[slot, p, at : at + 2 * ORD, :] = pair
            end = coefs[:, CHUNK + b : CHUNK + b + 1]
            last = last * end
            prev = prev * end
            large = jnp.abs(last) > two_power
            factor = jnp.where(large, inverse_power, 1.0)
            last = last * factor
            prev = prev * factor
            logs = logs + jnp.where(large, log_jump, 0.0)
        prev_ref[...] = prev
        last_ref[...] = last
        log_ref[...] = logs
        table_copy(item, slot).start()

        at = pl.multiple_of(group * rows, rows)
        lane = pl.multiple_of(chunk // (LANES // CHUNK) * LANES, LANES)
        piece = jnp.concatenate(
            [sorted_ref[c, pl.ds(at, rows), pl.ds(lane, LANES)] for c in range(comps)], axis=0
        )
        spread = spread_ref[lax.rem(chunk, LANES // CHUNK)]
        wide = jnp.dot(piece, spread, preferred_element_type=jnp.float32)
        mask = order_mask(kappa_ref[pl.ds(place, 1), :])
        wide = jnp.concatenate(
            [wide[c * rows : (c + 1) * rows] * mask for c in range(comps)], axis=0
        ).astype(jnp.bfloat16)
        even_ref[...] += jnp.dot(
            wide[:, :half], buffer_ref[slot, 0], preferred_element_type=jnp.float32
        )
        odd_ref[...] += jnp.dot(
            wide[:, half:], buffer_ref[slot, 1], preferred_element_type=jnp.float32
        )

        @pl.when(chunk == chunks - 1)
        def _():
            sign = jnp.where(group < groups // 2, 1.0, -1.0)
            for c in range(comps):
                even = even_ref[c * rows : (c + 1) * rows, :]
                odd = odd_ref[c * rows : (c + 1) * rows, :]
                north = (even + odd).astype(jnp.bfloat16)
                south = (sign * (even - odd)).astype(jnp.bfloat16)
                for b in range(lane_blocks):
                    lanes = slice(b * LANES, (b + 1) * LANES)
                    out_ref[b, c, group] = north[:, lanes]
                    out_ref[2 * lane_blocks - 1 - b, c, group] = south[:, lanes]

        return carry

    lax.fori_loop(0, count, body, 0)
    for back in (2, 1):
        item = count - back
        table_copy(item, lax.rem(item, 2)).wait()


def analysis_kernel(
    comps,
    groups,
    chunks,
    group_ref,
    chunk_ref,
    start_ref,
    count_ref,
    grid_ref,
    table_ref,
    place_ref,
    kappa_ref,
    spread_ref,
    weight_ref,
    out_ref,
    sorted_ref,
    even_ref,
    odd_ref,
    buffer_ref,
    sems,
):
    rows = 2 * ORD
    half = CHUNK * ORD // 2
    lane_blocks = weight_ref.shape[1] // LANES
    count = count_ref[0]
    sorted_ref[...] = jnp.zeros_like(sorted_ref)

    def table_copy(item, slot):
        return pltpu.make_async_copy(table_ref.at[item], buffer_ref.at[slot], sems.at[slot])

    table_copy(0, 0).start()

    def body(item, carry):
        group = group_ref[item]
        chunk = chunk_ref[item]
        slot = lax.rem(item, 2)
        place = group * chunks + chunk

        @pl.when(item + 1 < count)
        def _():
            table_copy(item + 1, 1 - slot).start()

        @pl.when(start_ref[item] == 1)
        def _():
            sign = jnp.where(group < groups // 2, 1.0, -1.0)
            for b in range(lane_blocks):
                lanes = slice(b * LANES, (b + 1) * LANES)
                weight = weight_ref[:, lanes]
                for c in range(comps):
                    north = grid_ref[b, c, group].astype(jnp.float32)
                    south = sign * grid_ref[2 * lane_blocks - 1 - b, c, group].astype(jnp.float32)
                    at = slice(c * rows, (c + 1) * rows)
                    even_ref[at, lanes] = (weight * (north + south)).astype(jnp.bfloat16)
                    odd_ref[at, lanes] = (weight * (north - south)).astype(jnp.bfloat16)

        table_copy(item, slot).wait()
        contract = (((1,), (1,)), ((), ()))
        wide_even = lax.dot_general(
            even_ref[...], buffer_ref[slot, 0], contract, preferred_element_type=jnp.float32
        )
        wide_odd = lax.dot_general(
            odd_ref[...], buffer_ref[slot, 1], contract, preferred_element_type=jnp.float32
        )
        mask = order_mask(kappa_ref[pl.ds(place, 1), :])
        wide = jnp.concatenate(
            [
                jnp.concatenate(
                    [
                        wide_even[c * rows : (c + 1) * rows] * mask[:, :half],
                        wide_odd[c * rows : (c + 1) * rows] * mask[:, half:],
                    ],
                    axis=1,
                )
                for c in range(comps)
            ],
            axis=0,
        ).astype(jnp.bfloat16)
        spread = spread_ref[lax.rem(chunk, LANES // CHUNK)]
        narrow = lax.dot_general(wide, spread, contract, preferred_element_type=jnp.float32)
        narrow = narrow.astype(jnp.bfloat16)
        at = pl.multiple_of(group * rows, rows)
        lane = pl.multiple_of(chunk // (LANES // CHUNK) * LANES, LANES)
        for c in range(comps):
            where = (c, pl.ds(at, rows), pl.ds(lane, LANES))
            sorted_ref[where] = sorted_ref[where] + narrow[c * rows : (c + 1) * rows]
        return carry

    lax.fori_loop(0, count, body, 0)
    for c in range(comps):
        moved = jnp.dot(place_ref[...], sorted_ref[c], preferred_element_type=jnp.float32)
        out_ref[c] = moved.astype(jnp.bfloat16)


def grid_kernel(
    norm, packs, grid_ref, forward_ref, backward_ref, viscosity_ref, out_ref, field_ref, stress_ref
):
    blocks, _, groups, rows, lanes = grid_ref.shape
    half_groups = groups // 2
    depth = blocks * half_groups * rows
    points = forward_ref.shape[1]
    tile = 256
    width = packs * lanes
    for w in range(packs):
        for p in range(2):
            for d in range(blocks):
                piece = grid_ref[d, w, p * half_groups : (p + 1) * half_groups]
                field_ref[
                    p,
                    d * half_groups * rows : (d + 1) * half_groups * rows,
                    w * lanes : (w + 1) * lanes,
                ] = piece.reshape(half_groups * rows, lanes)

    def points_step(i, carry):
        at = pl.multiple_of(i * tile, tile)
        even = jnp.dot(
            forward_ref[0, pl.ds(at, tile), :], field_ref[0], preferred_element_type=jnp.float32
        )
        odd = jnp.dot(
            forward_ref[1, pl.ds(at, tile), :], field_ref[1], preferred_element_type=jnp.float32
        )
        near = viscosity_ref[pl.ds(at, tile), :]
        far = viscosity_ref[pl.ds(points + at, tile), :]
        if packs > 1:
            near = jnp.concatenate([near] * packs, axis=1)
            far = jnp.concatenate([far] * packs, axis=1)
        near = (near * (even + odd)).astype(jnp.bfloat16).astype(jnp.float32)
        far = (far * (even - odd)).astype(jnp.bfloat16).astype(jnp.float32)
        stress_ref[0, pl.ds(at, tile), :] = (near + far).astype(jnp.bfloat16)
        stress_ref[1, pl.ds(at, tile), :] = (near - far).astype(jnp.bfloat16)
        return carry

    lax.fori_loop(0, points // tile, points_step, 0)
    step_rows = half_groups * rows

    def orders_step(d, carry):
        at = pl.multiple_of(d * step_rows, step_rows)
        for p in range(2):
            found = jnp.dot(
                backward_ref[p, pl.ds(at, step_rows), :],
                stress_ref[p],
                preferred_element_type=jnp.float32,
            )
            found = (found * norm).astype(jnp.bfloat16)
            for w in range(packs):
                out_ref[d, w, p * half_groups : (p + 1) * half_groups] = found[
                    :, w * lanes : (w + 1) * lanes
                ].reshape(half_groups, rows, lanes)
        return carry

    lax.fori_loop(0, blocks, orders_step, 0)


def whole(shape):
    return pl.BlockSpec(shape, lambda *_: (0,) * len(shape))


def run_synth(items, spectra, place, coefs, kappa, spread, geometry, groups, chunks):
    comps, slots, degrees = spectra.shape
    half_cycles = geometry.shape[1]
    blocks = 2 * half_cycles // LANES
    rows = 2 * ORD
    half = CHUNK * ORD // 2
    smem = pl.BlockSpec(memory_space=pltpu.SMEM)
    vmem = pl.BlockSpec(memory_space=pltpu.VMEM)
    return pl.pallas_call(
        functools.partial(synth_kernel, comps, groups, chunks),
        out_shape=(
            jax.ShapeDtypeStruct((blocks, comps, groups, rows, LANES), jnp.bfloat16),
            jax.ShapeDtypeStruct((groups * chunks, 2, half, half_cycles), jnp.bfloat16),
        ),
        in_specs=[smem] * 4 + [vmem] * 6,
        out_specs=(vmem, pl.BlockSpec(memory_space=pl.ANY)),
        scratch_shapes=[
            pltpu.VMEM((comps, slots, degrees), jnp.bfloat16),
            pltpu.VMEM((comps * rows, half_cycles), jnp.float32),
            pltpu.VMEM((comps * rows, half_cycles), jnp.float32),
            pltpu.VMEM((ORD, half_cycles), jnp.float32),
            pltpu.VMEM((ORD, half_cycles), jnp.float32),
            pltpu.VMEM((ORD, half_cycles), jnp.float32),
            pltpu.VMEM((2, 2, half, half_cycles), jnp.bfloat16),
            pltpu.SemaphoreType.DMA((2,)),
        ],
        compiler_params=pltpu.CompilerParams(vmem_limit_bytes=VMEM_LIMIT),
        name="synthesis",
    )(*items, spectra, place, coefs, kappa, spread, geometry)


def run_analysis(items, gridded, table, place, kappa, spread, weights, degrees, groups, chunks):
    blocks, comps, _, rows, _ = gridded.shape
    half_cycles = weights.shape[1]
    half = CHUNK * ORD // 2
    slots = place.shape[0]
    smem = pl.BlockSpec(memory_space=pltpu.SMEM)
    vmem = pl.BlockSpec(memory_space=pltpu.VMEM)
    return pl.pallas_call(
        functools.partial(analysis_kernel, comps, groups, chunks),
        out_shape=jax.ShapeDtypeStruct((comps, slots, degrees), jnp.bfloat16),
        in_specs=[smem] * 4 + [vmem, pl.BlockSpec(memory_space=pl.ANY)] + [vmem] * 4,
        out_specs=vmem,
        scratch_shapes=[
            pltpu.VMEM((comps, slots, degrees), jnp.bfloat16),
            pltpu.VMEM((comps * rows, half_cycles), jnp.bfloat16),
            pltpu.VMEM((comps * rows, half_cycles), jnp.bfloat16),
            pltpu.VMEM((2, 2, half, half_cycles), jnp.bfloat16),
            pltpu.SemaphoreType.DMA((2,)),
        ],
        compiler_params=pltpu.CompilerParams(vmem_limit_bytes=VMEM_LIMIT),
        name="analysis",
    )(*items, gridded, table, place, kappa, spread, weights)


def run_grid(received, forward, backward, viscosity, norm):
    blocks, comps, groups, rows, lanes = received.shape
    packs = 2 if comps % 2 == 0 else 1
    depth = blocks * groups // 2 * rows
    half_points = forward.shape[1]
    part = pl.BlockSpec((blocks, packs, groups, rows, lanes), lambda i: (0, i, 0, 0, 0))
    return pl.pallas_call(
        functools.partial(grid_kernel, norm, packs),
        out_shape=jax.ShapeDtypeStruct(received.shape, jnp.bfloat16),
        grid=(comps // packs,),
        in_specs=[part, whole(forward.shape), whole(backward.shape), whole(viscosity.shape)],
        out_specs=part,
        scratch_shapes=[
            pltpu.VMEM((2, depth, packs * lanes), jnp.bfloat16),
            pltpu.VMEM((2, half_points, packs * lanes), jnp.bfloat16),
        ],
        compiler_params=pltpu.CompilerParams(vmem_limit_bytes=VMEM_LIMIT),
        name="grid_transforms",
    )(received, forward, backward, viscosity)


def wave_tables(sorted_all, point_count, groups):
    blocks = sorted_all.shape[0]
    orders = sorted_all.reshape(blocks, 2, groups // 2, ORD).transpose(1, 0, 2, 3).reshape(2, -1)
    shift = jnp.arange(2, dtype=jnp.int32) * (point_count // 4)
    longitudes = jnp.arange(point_count // 2, dtype=jnp.int32)

    def values(phase):
        angles = (phase % point_count).astype(jnp.float32) * (2.0 * math.pi / point_count)
        return jnp.cos(angles).astype(jnp.bfloat16)

    rows = (2, orders.shape[1] * 2)
    order_rows = jnp.broadcast_to(orders[:, :, None], orders.shape + (2,)).reshape(rows)
    shift_rows = jnp.broadcast_to(shift, orders.shape + (2,)).reshape(rows)
    backward = values(order_rows[:, :, None] * longitudes + shift_rows[:, :, None])
    forward = values(order_rows[:, None, :] * longitudes[:, None] + shift_rows[:, None, :])
    return forward, backward


def to_blocks(gridded, cycle_local):
    blocks, comps, groups, rows, _ = gridded.shape
    share = LANES // cycle_local
    if share == 1:
        return gridded
    cut = gridded.reshape(2, blocks // 2, comps, groups, rows, share, cycle_local)
    cut = cut.transpose(0, 1, 5, 2, 3, 4, 6)
    cut = jnp.stack([cut[0], jnp.flip(cut[1], axis=1)])
    return cut.reshape(blocks * share, comps, groups, rows, cycle_local)


def from_blocks(gridded, cycle_local):
    blocks, comps, groups, rows, _ = gridded.shape
    share = LANES // cycle_local
    if share == 1:
        return gridded
    cut = gridded.reshape(2, blocks // share // 2, share, comps, groups, rows, cycle_local)
    cut = jnp.stack([cut[0], jnp.flip(cut[1], axis=1)])
    cut = cut.transpose(0, 1, 3, 4, 5, 2, 6)
    return cut.reshape(blocks // share, comps, groups, rows, LANES)


def pack_comps(gridded):
    blocks, comps, groups, rows, cycle_local = gridded.shape
    if cycle_local == LANES:
        return gridded
    side = gridded.transpose(0, 2, 3, 1, 4).reshape(blocks, 1, groups, rows, comps * cycle_local)
    extra = -(comps * cycle_local) % LANES
    return jnp.pad(side, ((0, 0),) * 4 + ((0, extra),))


def unpack_comps(gridded, comps, cycle_local):
    if cycle_local == LANES:
        return gridded
    blocks, _, groups, rows, _ = gridded.shape
    side = gridded[..., : comps * cycle_local]
    side = side.reshape(blocks, groups, rows, comps, cycle_local)
    return side.transpose(0, 3, 1, 2, 4)


def shards(strain_spec, order_map, viscosity, radial_weight):
    comps, shells, slots, parts, degrees = strain_spec.shape
    block_count = lax.axis_size("blk")
    block = lax.axis_index("blk")
    cycle_local = viscosity.shape[1]
    cycle_count = cycle_local * block_count
    half_cycles = cycle_count // 2
    points = viscosity.shape[2]
    groups = slots // ORD
    chunks = degrees // CHUNK

    rank_all = rank_orders(order_map.reshape(block_count, slots))
    sorted_all = apply_rank(order_map.reshape(block_count, slots), rank_all)
    rank = lax.dynamic_index_in_dim(rank_all, block, 0, keepdims=False)
    sorted_orders = lax.dynamic_index_in_dim(sorted_all, block, 0, keepdims=False)
    items = work_items(sorted_orders, degrees)
    coefs, kappa = recursion_coefficients(sorted_orders, degrees)
    spread = spread_matrix()

    cycle_index = jnp.arange(half_cycles, dtype=jnp.float32)
    colatitude = math.pi * (2.0 * cycle_index + 1.0) / (2.0 * cycle_count)
    geometry = jnp.stack([2.0 * jnp.cos(colatitude), jnp.log(jnp.sin(colatitude))])

    row_rank = (rank[:, None] * 2 + jnp.arange(2, dtype=jnp.int32)).reshape(-1)
    place = jnp.arange(slots * 2, dtype=jnp.int32)
    hit = row_rank[None, :] == place[:, None]
    my_orders = lax.dynamic_index_in_dim(
        order_map.reshape(block_count, slots), block, 0, keepdims=False
    )
    doubling = jnp.repeat(jnp.where(my_orders == 0, 1.0, 2.0), 2)
    place_in = jnp.where(hit, doubling[None, :], 0.0).astype(jnp.bfloat16)
    place_out = hit.T.astype(jnp.bfloat16)

    spectra = strain_spec.reshape(comps, slots * parts, degrees)
    gridded, table = run_synth(
        items, spectra, place_in, coefs, kappa, spread, geometry, groups, chunks
    )
    received = lax.all_to_all(to_blocks(gridded, cycle_local), "blk", 0, 0, tiled=True)

    forward, backward = wave_tables(sorted_all, points, groups)
    weights = fejer_weights(cycle_count)[None, :]
    mirror = jnp.arange(cycle_local, dtype=jnp.int32)
    mirror = jnp.where(block * 2 < block_count, mirror, cycle_local - 1 - mirror)
    turn = (mirror[None, :] == jnp.arange(cycle_local, dtype=jnp.int32)[:, None]).astype(jnp.float32)
    local = jnp.einsum("jk,ji->ki", viscosity[0], turn, precision=lax.Precision.HIGHEST)
    if cycle_local < LANES:
        local = jnp.concatenate([local] * comps, axis=1)
        local = jnp.pad(local, ((0, 0), (0, -local.shape[1] % LANES)))
    spectrum = run_grid(pack_comps(received), forward, backward, local, 2.0 * math.pi / points)
    spectrum = unpack_comps(spectrum, comps, cycle_local)
    returned = lax.all_to_all(spectrum, "blk", 0, 0, tiled=True)

    stress = run_analysis(
        items,
        from_blocks(returned, cycle_local),
        table,
        place_out,
        kappa,
        spread,
        weights,
        degrees,
        groups,
        chunks,
    )
    shell_count = lax.axis_size("shell")
    all_weights = lax.all_gather(radial_weight, "shell").reshape(shell_count)
    cut = stress.reshape(comps, slots * parts, shell_count, degrees // shell_count)
    shared = lax.all_to_all(cut.transpose(2, 0, 1, 3), "shell", 0, 0, tiled=True)
    integrated = jnp.sum(shared.astype(jnp.float32) * all_weights[:, None, None, None], axis=0)
    stress_spec = stress.reshape(strain_spec.shape)
    return (stress_spec, integrated.reshape(comps, slots, parts, degrees // shell_count))


def solution(mesh):
    return jax.shard_map(
        shards,
        mesh=mesh,
        in_specs=(P(None, "shell", "blk", None, None), P(), P("shell", "blk", None), P("shell")),
        out_specs=(P(None, "shell", "blk", None, None), P(None, "blk", None, "shell")),
        check_vma=False,
    )
```

time: 1850 us -> 485 us (0.26); the launches traced: 1830 us -> 482 us
  other arithmetic: 721 us -> 93.5 us
  loops' own time: 327 us -> 0 us
  matrix products: 265 us -> 1.97 us
  local copies, waits for them, and re-layouts: 298 us -> 37.1 us
  Pallas kernels: 0 us -> 227 us
  waiting for transfers between devices: 188 us -> 67.9 us
  blocking collectives: 0 us -> 36.4 us
    while x496 -> x0, other arithmetic: 597 us -> none
    another operation x1 -> x0, loops' own time: 327 us -> none  [legendre_tables(): lax.scan(pair_step, initial, jnp.arange(degree_count // 2, dtype=jnp.int3...]
    dot_general x6 -> x1, matrix products: 265 us -> 1.97 us  [shards(): jnp.einsum('jk,ji->ki', viscosity[0], turn, precision=lax.Precision.HIGHEST)]
    pallas_call x0 -> x3, Pallas kernels: none -> 227 us  [the longest x1 118 us: run_analysis(): pl.pallas_call(functools.partial(analysis_kernel, comps, groups, chunks),...]
    dynamic_update_slice x16 -> x0, local copies, waits for them, and re-layouts: 124 us -> none  [legendre_tables(): lax.scan(pair_step, initial, jnp.arange(degree_count // 2, dtype=jnp.int3...]
    all_to_all x2 -> x3, waiting for transfers between devices: 137 us -> 67.9 us  [the longest x1 64.4 us: shards(): returned = lax.all_to_all(spectrum, 'blk', 0, 0, tiled=True)]
    convert_element_type x3 -> x7, other arithmetic: 7.81 us -> 67.3 us  [the longest x1 64.4 us: values(): return jnp.cos(angles).astype(jnp.bfloat16)]
    psum x1 -> x0, waiting for transfers between devices: 51 us -> none  [shards(): lax.psum(weighted.astype(jnp.bfloat16), 'shell').astype(jnp.float32)]
  transfers between devices with their start and end apart: 3 -> 3, of which waited for: 3 -> 2; matrix products, arithmetic and copies ran while one was open for 3% -> 17% of each run, Pallas kernels for 0% -> 0%
where the time goes in v1:
time: 485 us; the launch traced here: 482 us
  Pallas kernels  227 us (47%)
  other arithmetic  93.5 us (19%)
  waiting for transfers between devices  67.9 us (14%)
  local copies, waits for them, and re-layouts  37.1 us (8%)
  blocking collectives  36.4 us (8%)
  starting transfers between devices  16.4 us (3%)
    pallas_call x1, Pallas kernels, run_analysis(): pl.pallas_call(functools.partial(analysis_kernel, comps, groups, chunks),...  118 us
    pallas_call x1, Pallas kernels, run_synth(): pl.pallas_call(functools.partial(synth_kernel, comps, groups, chunks), ou...  90.7 us
    all_to_all x1, waiting for transfers between devices, shards(): returned = lax.all_to_all(spectrum, 'blk', 0, 0, tiled=True)  64.4 us
    convert_element_type x1, other arithmetic, values(): return jnp.cos(angles).astype(jnp.bfloat16)  64.4 us
    unnamed x1, blocking collectives  36.4 us
    pallas_call x1, Pallas kernels, run_grid(): pl.pallas_call(functools.partial(grid_kernel, norm, packs), out_shape=jax...  18.6 us
  transfers between devices with their start and end apart: 3, of which 2 were waited for; matrix products, arithmetic and copies ran while one was open for 17% of the time, Pallas kernels for 0%

profile of v1, /device:TPU:0, one launch (start us, length us, event | category | flops | bytes accessed | tf_op | source)
XLA Modules:
  0.0 481.8 jit_solution(5251526747572490182)
XLA Ops:
  3.2 3.4 sqrt_select_fusion
  6.9 3.6 pad_multiply_fusion.3
  10.8 3.9 pad_multiply_fusion.2
  16.0 2.9 copy.52
  22.3 5.8 %copy.53 = f32[16,16,2,32,8]{1,0,4,3,2:T(8,128)} copy(f32[16,16,2,32,8]{0,4,2,3,1:T(8,128)} %bitcast.41) | data formatting | bytes 1048576 | tf_op jit(solution)/shard_map/transpose | solution.py:64
  28.1 3.5 reshape.413
  34.8 5.7 %reshape.410.spec_ref = bf16[6,256,1024]{2,1,0:T(8,128)(2,1)} reshape(bf16[6,1,128,2,1024]{4,3,2,1,0:T(2,128)(2,1)} %param.4) | data formatting | bytes 6291456 | tf_op jit(solution)/shard_map/reshape | solution.py:567
  42.9 1.6 maximum_maximum_fusion
  44.5 90.7 %synthesis.1 = (bf16[8,6,16,16,128]{4,3,2,1,0:T(8,128)(2,1)}, bf16[256,2,256,512]{3,2,1,0:T(8,128)(2,1)}) custom-call(s32[256]{0:T(256)} %copy-done.3, s32[256]{0:T(256)} %fusion.39.chunk_ref, s32[256]{0:T(256)} %compare_convert_fusion.1.start_ref, s32[1]{0:T(128)} %slice.22.count_ref, bf16[6,256,1024]{2,1,0:T(8,128)(2,1)} %reshape.410.spec_ref, ...), custom_call_target="tpu_custom_call" | custom-call | tf_op jit(solution)/shard_map/synthesis/pallas_call | solution.py:408
  135.2 7.2 %all-to-all-start = ((bf16[8,6,16,16,128]{4,3,2,1,0:T(8,128)(2,1)}), bf16[8,6,16,16,128]{4,3,2,1,0:T(8,128)(2,1)}, u32[]{:S(2)}, u32[]{:S(2)}) async-start(bf16[8,6,16,16,128]{4,3,2,1,0:T(8,128)(2,1)} %get-tuple-element.4), calls=%async_computation | async-start | bytes 6291456 | tf_op jit(solution)/shard_map/all_to_all | solution.py:571
  143.3 2.0 convolution_bitcast_fusion.viscosity_ref
  145.3 64.4 %fusion.9 = (bf16[2,1024,1024]{2,1,0:T(8,128)(2,1)}, bf16[2,1024,1024]{2,1,0:T(8,128)(2,1)}) fusion(s32[1024]{0:T(1024)S(1)} %broadcast_in_dim.151, s32[2,1024]{1,0:T(2,128)S(1)} %mul.315), kind=kLoop, calls=%fused_computation.15 | loop fusion | flops 67108864 | bytes 8400896 | tf_op jit(solution)/shard_map/convert_element_type | solution.py:484
  209.7 3.5 all-to-all-done.grid_ref
  213.2 18.6 %grid_transforms.1 = bf16[8,6,16,16,128]{4,3,2,1,0:T(8,128)(2,1)} custom-call(bf16[8,6,16,16,128]{4,3,2,1,0:T(8,128)(2,1)} %all-to-all-done.grid_ref, bf16[2,1024,1024]{2,1,0:T(8,128)(2,1)} %get-tuple-element.21.forward_ref, bf16[2,1024,1024]{2,1,0:T(8,128)(2,1)} %get-tuple-element.20.backward_ref, f32[2048,128]{1,0:T(8,128)} %convolution_bitcast_fusion.viscosity_ref), custom_call_target="tpu_custom_call" | custom-call | tf_op jit(solution)/shard_map/grid_transforms/pallas_call | solution.py:461
  231.8 4.4 all-to-all-start.1
  236.3 4.4 fusion.16
  242.0 64.4 %all-to-all-done.1.grid_ref = bf16[8,6,16,16,128]{4,3,2,1,0:T(8,128)(2,1)} async-done(((bf16[8,6,16,16,128]{4,3,2,1,0:T(8,128)(2,1)}), bf16[8,6,16,16,128]{4,3,2,1,0:T(8,128)(2,1)}, u32[]{:S(2)}, u32[]{:S(2)}) %all-to-all-start.1) | async-done | bytes 3145760 | tf_op jit(solution)/shard_map/all_to_all | solution.py:584
  306.4 117.6 %analysis.1 = bf16[6,256,1024]{2,1,0:T(8,128)(2,1)} custom-call(s32[256]{0:T(256)} %copy-done.3, s32[256]{0:T(256)} %fusion.39.chunk_ref, s32[256]{0:T(256)} %compare_convert_fusion.1.start_ref, s32[1]{0:T(128)} %slice.22.count_ref, bf16[8,6,16,16,128]{4,3,2,1,0:T(8,128)(2,1)} %all-to-all-done.1.grid_ref, ...), custom_call_target="tpu_custom_call" | custom-call | tf_op jit(solution)/shard_map/analysis/pallas_call | solution.py:438
  424.0 4.0 copy.64
  428.0 4.8 all-to-all-start.2
  434.7 36.4 %all-reduce.4 = f32[4]{0:T(128)S(1)} all-reduce(f32[4]{0:T(128)S(1)} %dynamic-update-slice), channel_id=2, replica_groups=mesh['shell'=4,'blk'=8] {'shell'}, use_global_device_ids=true, to_apply=%add.4 | all-reduce | flops 4 | bytes 32
  471.2 5.8 %reshape.415 = bf16[6,1,128,2,1024]{4,3,2,0,1:T(2,128)(2,1)} reshape(bf16[6,256,1024]{2,1,0:T(8,128)(2,1)} %analysis.1) | data formatting | bytes 6291456 | tf_op jit(solution)/shard_map/reshape | solution.py:603
  477.0 2.8 multiply_reduce_fusion
  479.7 2.1 reshape.417
  (83 shorter events, 16.8 us)
Async XLA Ops:
  0.6 142.7 %copy-start = (f32[1,128,2048]{2,1,0:T(8,128)S(1)}, f32[1,128,2048]{2,1,0:T(8,128)}, u32[]{:S(2)}) copy-start(f32[1,128,2048]{2,1,0:T(8,128)} %param.6) | copy-start | bytes 3145732
  16.0 3.2 copy-start.2
  19.6 8.5 %copy-start.3 = (s32[256]{0:T(256)}, s32[256]{0:T(256)S(1)}, u32[]{:S(2)}) copy-start(s32[256]{0:T(256)S(1)} %broadcast_minimum_fusion.group_ref) | copy-start | bytes 3076
  28.1 4.6 slice-start
  135.2 78.0 %all-to-all-start = ((bf16[8,6,16,16,128]{4,3,2,1,0:T(8,128)(2,1)}), bf16[8,6,16,16,128]{4,3,2,1,0:T(8,128)(2,1)}, u32[]{:S(2)}, u32[]{:S(2)}) async-start(bf16[8,6,16,16,128]{4,3,2,1,0:T(8,128)(2,1)} %get-tuple-element.4), calls=%async_computation | async-start | bytes 6291456 | tf_op jit(solution)/shard_map/all_to_all | solution.py:571
  231.8 74.7 %all-to-all-start.1 = ((bf16[8,6,16,16,128]{4,3,2,1,0:T(8,128)(2,1)}), bf16[8,6,16,16,128]{4,3,2,1,0:T(8,128)(2,1)}, u32[]{:S(2)}, u32[]{:S(2)}) async-start(bf16[8,6,16,16,128]{4,3,2,1,0:T(8,128)(2,1)} %grid_transforms.1), calls=%async_computation.1 | async-start | bytes 6291456 | tf_op jit(solution)/shard_map/all_to_all | solution.py:584
  428.0 5.4 %copy-start.4 = (u32[32]{0:T(128)S(1)}, u32[32]{0:T(128)}, u32[]{:S(2)}) copy-start(u32[32]{0:T(128)} %constant.191) | copy-start | bytes 388
  428.0 49.0 %all-to-all-start.2 = ((bf16[4,6,256,256]{3,2,1,0:T(8,128)(2,1)}), bf16[4,6,256,256]{3,2,1,0:T(8,128)(2,1)}, u32[]{:S(2)}, u32[]{:S(2)}) async-start(bf16[4,6,256,256]{3,2,1,0:T(8,128)(2,1)} %bitcast.42), calls=%async_computation.2 | async-start | bytes 6291456 | tf_op jit(solution)/shard_map/all_to_all | solution.py:601
  471.2 10.6 %copy-start.1 = (f32[1,128,2048]{2,1,0:T(8,128)S(1)}, f32[1,128,2048]{2,1,0:T(8,128)}, u32[]{:S(2)}) copy-start(f32[1,128,2048]{2,1,0:T(8,128)} %param.6) | copy-start | bytes 3145732

commit v2 on v1

v2 whole, which is shorter than its diff:
```python
import functools
import math

import jax
import jax.numpy as jnp
from jax import lax
from jax.experimental import pallas as pl
from jax.experimental.pallas import tpu as pltpu
from jax.sharding import PartitionSpec as P

two_power = 1099511627776.0
inverse_power = 1.0 / 1099511627776.0
log_jump = 40.0 * math.log(2.0)

ORD = 8
CHUNK = 64
BLOCK = 16
LANES = 128
SLOTS = 4
PARTS = 2
VMEM_LIMIT = 56 * 1024 * 1024


def fejer_weights(cycle_count):
    half_count = cycle_count // 2
    cycle_index = jnp.arange(half_count, dtype=jnp.int32)
    wave_number = jnp.arange(1, half_count + 1, dtype=jnp.int32)
    phase_index = wave_number[:, None] * (2 * cycle_index[None, :] + 1) % (2 * cycle_count)
    angles = phase_index.astype(jnp.float32) * (math.pi / cycle_count)
    wave_float = wave_number.astype(jnp.float32)
    divisor = 4.0 * wave_float * wave_float - 1.0
    series = jnp.sum(jnp.cos(angles) / divisor[:, None], axis=0)
    return 2.0 / cycle_count * (1.0 - 2.0 * series)


def rank_orders(orders):
    top = orders.shape[-1]
    key = orders + (orders % 2) * (1 << 20)
    return jnp.sum((key[..., None, :] < key[..., :, None]).astype(jnp.int32), axis=-1)


def apply_rank(values, rank):
    count = rank.shape[-1]
    place = jnp.arange(count, dtype=jnp.int32)
    hit = rank[..., :, None] == place
    return jnp.sum(jnp.where(hit, values[..., :, None], 0), axis=-2)


def lane_fill(values):
    return jnp.broadcast_to(values.reshape(-1, ORD, 1), (values.shape[0] // ORD, ORD, LANES))


def spread_matrix():
    place = jnp.arange(CHUNK * ORD, dtype=jnp.int32)
    parity = place // (CHUNK * ORD // 2)
    degree = 2 * (place % (CHUNK * ORD // 2) // ORD) + parity
    half = jnp.arange(LANES // CHUNK, dtype=jnp.int32)[:, None, None]
    row = jnp.arange(LANES, dtype=jnp.int32)[None, :, None]
    return (row - CHUNK * half == degree[None, None, :]).astype(jnp.bfloat16)


def gather_matrix():
    return spread_matrix()[0, :CHUNK, :]


def degree_rows(degree_count):
    below = jnp.arange(degree_count, dtype=jnp.float32) - 1.0
    bottom = 4.0 * below * below - 1.0
    rows = jnp.stack([4.0 * below * below / bottom, 4.0 / bottom])
    return jnp.broadcast_to(rows[:, :, None], (2, degree_count, LANES))


def kappa_lanes(order):
    lane = lax.broadcasted_iota(jnp.int32, order.shape, 1)
    degree = lane.astype(jnp.float32)
    square = degree * degree
    gap = jnp.maximum(square - order * order, 1.0)
    kappa = jnp.where(degree > order, jnp.sqrt((square - 0.25) / gap), 1.0)
    step = 1
    while step < BLOCK:
        moved = pltpu.roll(kappa, step, 1)
        kappa = kappa * jnp.where(lane % BLOCK >= step, moved, 1.0)
        step *= 2
    return kappa


def synth_kernel(
    comps,
    groups,
    chunks,
    sign,
    first_ref,
    last_ref,
    spec_ref,
    place_ref,
    order_ref,
    start_ref,
    degree_ref,
    spread_ref,
    geometry_ref,
    out_ref,
    table_ref,
    kappa_ref,
    sorted_ref,
    even_ref,
    odd_ref,
    prev_ref,
    last_row_ref,
    log_ref,
    end_ref,
    wide_ref,
    buffer_ref,
    sems,
):
    rows = 2 * ORD
    half = CHUNK * ORD // 2
    lane_blocks = geometry_ref.shape[1] // LANES
    for c in range(comps):
        moved = jnp.dot(place_ref[...], spec_ref[c], preferred_element_type=jnp.float32)
        sorted_ref[c] = moved.astype(jnp.bfloat16)
    degrees = chunks * CHUNK
    batch = math.gcd(groups, 4)

    def fill_kappa(i, carry):
        order = order_ref[pl.ds(i * batch, batch)].reshape(batch * ORD, LANES)
        kappa = kappa_lanes(jnp.concatenate([order] * (degrees // LANES), axis=1))
        kappa = kappa.reshape(batch, ORD, degrees)
        kappa_ref[pl.ds(i * batch, batch)] = kappa
        for b in range(degrees // BLOCK):
            end = kappa[:, :, (b + 1) * BLOCK - 1 : (b + 1) * BLOCK]
            end_ref[pl.ds(i * batch, batch), b] = jnp.broadcast_to(end, (batch, ORD, LANES))
        return carry

    lax.fori_loop(0, groups // batch, fill_kappa, 0)
    shape = (rows, CHUNK * ORD)
    row_order = lax.broadcasted_iota(jnp.int32, shape, 0) % ORD
    lane_order = lax.broadcasted_iota(jnp.int32, shape, 1) % ORD
    mask = jnp.where(row_order == lane_order, 1.0, 0.0)
    count = lax.fori_loop(0, groups, lambda g, n: n + chunks - first_ref[g], jnp.int32(0))
    even_ref[...] = jnp.zeros_like(even_ref)
    odd_ref[...] = jnp.zeros_like(odd_ref)
    wide_ref[...] = jnp.zeros_like(wide_ref)
    buffer_ref[SLOTS - 1] = jnp.zeros_like(buffer_ref[SLOTS - 1])

    def table_copies(item, slot):
        return [
            pltpu.make_async_copy(
                buffer_ref.at[slot, p], table_ref.at[item, p], sems.at[slot, p]
            )
            for p in range(2)
        ]

    def products(slot):
        even_ref[...] += jnp.dot(
            wide_ref[:, :half], buffer_ref[slot, 0], preferred_element_type=jnp.float32
        )
        odd_ref[...] += jnp.dot(
            wide_ref[:, half:], buffer_ref[slot, 1], preferred_element_type=jnp.float32
        )

    def recursion(seeded, group, chunk, slot):
        order = order_ref[group]
        begin = chunk * CHUNK
        odd_chunk = lax.rem(chunk, LANES // CHUNK)
        lane = pl.multiple_of((chunk - odd_chunk) * CHUNK, LANES)
        kappa = kappa_ref[group, :, pl.ds(lane, LANES)]
        square = order * order
        seed_at = jnp.concatenate([order - begin.astype(jnp.float32)] * lane_blocks, axis=1)
        twice = geometry_ref[0:1, :]
        prev = prev_ref[...]
        last = last_row_ref[...]
        logs = log_ref[...]
        for b in range(CHUNK // BLOCK):
            scale = jnp.exp(logs)
            held = []
            for i in range(BLOCK):
                step = b * BLOCK + i
                one = degree_ref[0, pl.ds(begin + step, 1), :]
                two = degree_ref[1, pl.ds(begin + step, 1), :]
                coef = jnp.concatenate([one - two * square] * lane_blocks, axis=1)
                now = twice * last - coef * prev
                if seeded:
                    now = jnp.where(seed_at == float(step), 1.0, now)
                held.append(now * scale)
                prev, last = last, now
            for p in range(2):
                for i in range(p, BLOCK, 4):
                    pair = jnp.concatenate([held[i], held[i + 2]], axis=0).astype(jnp.bfloat16)
                    at = (b * BLOCK + i - p) // 2 * ORD
                    buffer_ref[slot, p, at : at + 2 * ORD, :] = pair
            end = end_ref[group, chunk * (CHUNK // BLOCK) + b]
            end = jnp.concatenate([end] * lane_blocks, axis=1)
            last = last * end
            prev = prev * end
            large = jnp.abs(last) > two_power
            factor = jnp.where(large, inverse_power, 1.0)
            last = last * factor
            prev = prev * factor
            logs = logs + jnp.where(large, log_jump, 0.0)
        prev_ref[...] = prev
        last_row_ref[...] = last
        log_ref[...] = logs
        at = pl.multiple_of(group * rows, rows)
        factors = jnp.concatenate([kappa, kappa], axis=0)
        piece = jnp.concatenate(
            [
                (sorted_ref[c, pl.ds(at, rows), pl.ds(lane, LANES)] * factors).astype(jnp.bfloat16)
                for c in range(comps)
            ],
            axis=0,
        )
        wide = jnp.dot(piece, spread_ref[odd_chunk], preferred_element_type=jnp.float32)
        for c in range(comps):
            at = slice(c * rows, (c + 1) * rows)
            wide_ref[at, :] = (wide[at] * mask).astype(jnp.bfloat16)

    def finish(group):
        for c in range(comps):
            even = even_ref[c * rows : (c + 1) * rows, :]
            odd = odd_ref[c * rows : (c + 1) * rows, :]
            north = (even + odd).astype(jnp.bfloat16)
            south = (sign * (even - odd)).astype(jnp.bfloat16)
            for b in range(lane_blocks):
                lanes = slice(b * LANES, (b + 1) * LANES)
                out_ref[b, c, group] = north[:, lanes]
                out_ref[2 * lane_blocks - 1 - b, c, group] = south[:, lanes]
        even_ref[...] = jnp.zeros_like(even_ref)
        odd_ref[...] = jnp.zeros_like(odd_ref)

    def body(item, carry):
        before_group, before_chunk, group, chunk = carry
        slot = lax.rem(item, SLOTS)
        before = lax.rem(item + SLOTS - 1, SLOTS)

        @pl.when(item >= SLOTS)
        def _():
            for copy in table_copies(item - SLOTS, slot):
                copy.wait()

        @pl.when(chunk == first_ref[group])
        def _():
            prev_ref[...] = jnp.zeros_like(prev_ref)
            last_row_ref[...] = jnp.zeros_like(last_row_ref)
            wide_order = jnp.concatenate([order_ref[group]] * lane_blocks, axis=1)
            wide_start = jnp.concatenate([start_ref[group]] * lane_blocks, axis=1)
            log_ref[...] = wide_start + wide_order * geometry_ref[1:2, :]

        @pl.when(chunk <= last_ref[group])
        def _():
            products(before)
            recursion(True, group, chunk, slot)

        @pl.when(chunk > last_ref[group])
        def _():
            products(before)
            recursion(False, group, chunk, slot)

        for copy in table_copies(item, slot):
            copy.start()

        @pl.when(jnp.logical_and(before_chunk == chunks - 1, item > 0))
        def _():
            finish(before_group)

        done = chunk == chunks - 1
        next_group = jnp.minimum(group + done.astype(jnp.int32), groups - 1)
        next_chunk = jnp.where(done, first_ref[next_group], chunk + 1)
        return group, chunk, next_group, next_chunk

    zero = jnp.int32(0)
    lax.fori_loop(0, count, body, (zero, zero, zero, first_ref[0]))
    products(lax.rem(count - 1, SLOTS))
    finish(jnp.int32(groups - 1))
    for back in range(SLOTS, 0, -1):

        @pl.when(count >= back)
        def _():
            for copy in table_copies(count - back, lax.rem(count - back, SLOTS)):
                copy.wait()


def analysis_kernel(
    comps,
    groups,
    chunks,
    sign,
    first_ref,
    radial_ref,
    grid_ref,
    table_ref,
    kappa_ref,
    gather_ref,
    weight_ref,
    sorted_ref,
    shared_ref,
    side_ref,
    wide_ref,
    found_ref,
    buffer_ref,
    sems,
):
    rows = 2 * ORD
    half = CHUNK * ORD // 2
    half_cycles = weight_ref.shape[1]
    degrees = chunks * CHUNK
    lane_blocks = half_cycles // LANES
    width = found_ref.shape[1]
    count = lax.fori_loop(0, groups, lambda g, n: n + chunks - first_ref[g], jnp.int32(0))
    shape = (ORD, width)
    lane = lax.broadcasted_iota(jnp.int32, shape, 1)
    own = lax.broadcasted_iota(jnp.int32, shape, 0) == lane % ORD
    mask = jnp.where(own, 1.0, 0.0)
    mask = jnp.concatenate([mask] * (half // ORD), axis=0)
    unit = (
        lax.broadcasted_iota(jnp.int32, (width, width), 0)
        == lax.broadcasted_iota(jnp.int32, (width, width), 1)
    ).astype(jnp.bfloat16)
    contract = (((1,), (1,)), ((), ()))
    wide_ref[...] = jnp.zeros_like(wide_ref)
    radial = radial_ref[0]
    shells, share = shared_ref.shape[0], shared_ref.shape[3]

    def table_copies(item, slot):
        return [
            pltpu.make_async_copy(
                table_ref.at[item, p], buffer_ref.at[slot, p], sems.at[slot, p]
            )
            for p in range(2)
        ]

    for ahead in range(SLOTS - 1):

        @pl.when(ahead < count)
        def _():
            for copy in table_copies(ahead, ahead):
                copy.start()

    def narrow(chunk):
        found = jnp.dot(gather_ref[...], wide_ref[...], preferred_element_type=jnp.float32)
        found_ref[pl.ds(pl.multiple_of(chunk * CHUNK, CHUNK), CHUNK), :] = found.astype(
            jnp.bfloat16
        )

    def advance(group, chunk, carry):
        item, before = carry
        slot = lax.rem(item, SLOTS)
        ahead = item + SLOTS - 1

        @pl.when(ahead < count)
        def _():
            for copy in table_copies(ahead, lax.rem(ahead, SLOTS)):
                copy.start()

        for copy in table_copies(item, slot):
            copy.wait()
        narrow(before)
        for p in range(2):
            wide = jnp.dot(buffer_ref[slot, p], side_ref[p], preferred_element_type=jnp.float32)
            wide_ref[p * half : (p + 1) * half, :] = (wide * mask).astype(jnp.bfloat16)
        return item + 1, chunk

    def group_body(group, item):
        for b in range(lane_blocks):
            lanes = slice(b * LANES, (b + 1) * LANES)
            weight = weight_ref[:, lanes]
            norths, souths = [], []
            for c in range(comps):
                norths.append(grid_ref[b, c, group].astype(jnp.float32))
                souths.append(sign * grid_ref[2 * lane_blocks - 1 - b, c, group].astype(jnp.float32))
            fill = jnp.zeros((width - comps * rows, LANES), jnp.float32)
            north = jnp.concatenate(norths + [fill], axis=0)
            south = jnp.concatenate(souths + [fill], axis=0)
            side_ref[0, lanes, :] = (weight * (north + south)).T.astype(jnp.bfloat16)
            side_ref[1, lanes, :] = (weight * (north - south)).T.astype(jnp.bfloat16)
        found_ref[...] = jnp.zeros_like(found_ref)
        item, before = lax.fori_loop(
            first_ref[group], chunks, functools.partial(advance, group), (item, jnp.int32(chunks))
        )
        narrow(before)
        turned = lax.dot_general(
            unit, found_ref[:degrees], contract, preferred_element_type=jnp.float32
        )
        kappa = kappa_ref[group]
        at = pl.multiple_of(group * rows, rows)
        factors = jnp.concatenate([kappa, kappa], axis=0)
        for c in range(comps):
            piece = turned[c * rows : (c + 1) * rows] * factors
            sorted_ref[c, pl.ds(at, rows), :] = piece.astype(jnp.bfloat16)
            piece = (piece * radial).astype(jnp.bfloat16)
            for n in range(shells):
                shared_ref[n, c, pl.ds(at, rows), :] = piece[:, n * share : (n + 1) * share]
        return item

    lax.fori_loop(0, groups, group_body, jnp.int32(0))


def unsort_kernel(counts, place_ref, *refs):
    out_ref = refs[-1]
    for c in range(out_ref.shape[0]):
        found = 0.0
        for part, ref in enumerate(refs[:-1]):
            lanes = slice(part * counts, (part + 1) * counts)
            found += jnp.dot(place_ref[:, lanes], ref[c], preferred_element_type=jnp.float32)
        out_ref[c] = found.astype(jnp.bfloat16)


def shell_sum_kernel(counts, place_ref, *refs):
    out_ref = refs[-1]
    for c in range(out_ref.shape[0]):
        found = 0.0
        for part, ref in enumerate(refs[:-1]):
            lanes = slice(part * counts, (part + 1) * counts)
            for n in range(ref.shape[0]):
                found += jnp.dot(place_ref[:, lanes], ref[n, c], preferred_element_type=jnp.float32)
        out_ref[c] = found


def wave_kernel(forward_base, forward_turn, backward_base, backward_turn, forward_ref, backward_ref):
    points = forward_ref.shape[1]
    step = 512
    per = forward_ref.shape[2] // step

    def forward_lanes(i, carry):
        p, block = i // per, i % per
        at = pl.multiple_of(block * step, step)
        turn_cos = forward_turn[0, p, :, pl.ds(at, step)]
        turn_sin = forward_turn[1, p, :, pl.ds(at, step)]

        def turn(n, state):
            cos, sin = state
            later_cos = cos * turn_cos - sin * turn_sin
            later_sin = sin * turn_cos + cos * turn_sin
            rows = pl.ds(pl.multiple_of(n * 2 * ORD, 2 * ORD), 2 * ORD)
            forward_ref[p, rows, pl.ds(at, step)] = jnp.concatenate(
                [cos, later_cos], axis=0
            ).astype(jnp.bfloat16)
            cos = later_cos * turn_cos - later_sin * turn_sin
            sin = later_sin * turn_cos + later_cos * turn_sin
            return cos, sin

        state = (forward_base[0, p, :, pl.ds(at, step)], forward_base[1, p, :, pl.ds(at, step)])
        lax.fori_loop(0, points // (2 * ORD), turn, state)
        return carry

    lax.fori_loop(0, 2 * per, forward_lanes, 0)
    count = backward_base.shape[2]

    def backward_rows(i, carry):
        p, q = i // count, i % count
        real, imaginary = backward_base[0, p, q], backward_base[1, p, q]
        turn_cos, turn_sin = backward_turn[0, p, q], backward_turn[1, p, q]
        rows = pl.ds(pl.multiple_of(q * 2 * ORD, 2 * ORD), 2 * ORD)
        for a in range(points // LANES):
            backward_ref[p, rows, a * LANES : (a + 1) * LANES] = jnp.concatenate(
                [real, imaginary], axis=0
            ).astype(jnp.bfloat16)
            real, imaginary = (
                real * turn_cos + imaginary * turn_sin,
                imaginary * turn_cos - real * turn_sin,
            )
        return carry

    lax.fori_loop(0, 2 * count, backward_rows, 0)


def grid_kernel(norm, packs, parts, *refs):
    grid_refs, out_refs = refs[:parts], refs[parts + 3 : 2 * parts + 3]
    forward_ref, backward_ref, viscosity_ref = refs[parts : parts + 3]
    field_ref, stress_ref = refs[2 * parts + 3 :]
    blocks, _, groups, rows, lanes = grid_refs[0].shape
    halves = parts // 2
    step_rows = halves * groups * rows
    points = forward_ref.shape[1]
    tile = 256
    for part, grid_ref in enumerate(grid_refs):
        p, offset = part // halves, part % halves * groups * rows
        for w in range(packs):
            for d in range(blocks):
                at = d * step_rows + offset
                field_ref[p, at : at + groups * rows, w * lanes : (w + 1) * lanes] = grid_ref[
                    d, w
                ].reshape(groups * rows, lanes)

    def points_step(i, carry):
        at = pl.multiple_of(i * tile, tile)
        even = jnp.dot(
            forward_ref[0, pl.ds(at, tile), :], field_ref[0], preferred_element_type=jnp.float32
        )
        odd = jnp.dot(
            forward_ref[1, pl.ds(at, tile), :], field_ref[1], preferred_element_type=jnp.float32
        )
        near = viscosity_ref[pl.ds(at, tile), :]
        far = viscosity_ref[pl.ds(points + at, tile), :]
        if packs > 1:
            near = jnp.concatenate([near] * packs, axis=1)
            far = jnp.concatenate([far] * packs, axis=1)
        near = (near * (even + odd)).astype(jnp.bfloat16).astype(jnp.float32)
        far = (far * (even - odd)).astype(jnp.bfloat16).astype(jnp.float32)
        stress_ref[0, pl.ds(at, tile), :] = (near + far).astype(jnp.bfloat16)
        stress_ref[1, pl.ds(at, tile), :] = (near - far).astype(jnp.bfloat16)
        return carry

    lax.fori_loop(0, points // tile, points_step, 0)
    def orders_step(d, carry):
        for p in range(2):
            at = pl.multiple_of(d * step_rows, step_rows)
            found = jnp.dot(
                backward_ref[p, pl.ds(at, step_rows), :],
                stress_ref[p],
                preferred_element_type=jnp.float32,
            )
            found = (found * norm).astype(jnp.bfloat16)
            for h in range(halves):
                piece = found[h * groups * rows : (h + 1) * groups * rows]
                for w in range(packs):
                    out_refs[p * halves + h][d, w] = piece[:, w * lanes : (w + 1) * lanes].reshape(
                        groups, rows, lanes
                    )
        return carry

    lax.fori_loop(0, blocks, orders_step, 0)


def whole(shape):
    return pl.BlockSpec(shape, lambda *_: (0,) * len(shape))


def params(flops, nbytes):
    return dict(
        compiler_params=pltpu.CompilerParams(vmem_limit_bytes=VMEM_LIMIT),
        cost_estimate=pl.CostEstimate(flops=flops, bytes_accessed=nbytes, transcendentals=0),
    )


def run_synth(bounds, spectra, place, orders, starts, degree_table, spread, geometry, chunks, sign):
    comps, slots, degrees = spectra.shape
    groups = orders.shape[0]
    half_cycles = geometry.shape[1]
    blocks = 2 * half_cycles // LANES
    rows = 2 * ORD
    half = CHUNK * ORD // 2
    smem = pl.BlockSpec(memory_space=pltpu.SMEM)
    vmem = pl.BlockSpec(memory_space=pltpu.VMEM)
    return pl.pallas_call(
        functools.partial(synth_kernel, comps, groups, chunks, sign),
        out_shape=(
            jax.ShapeDtypeStruct((blocks, comps, groups, rows, LANES), jnp.bfloat16),
            jax.ShapeDtypeStruct((groups * chunks, 2, half, half_cycles), jnp.bfloat16),
            jax.ShapeDtypeStruct((groups, ORD, degrees), jnp.float32),
        ),
        in_specs=[smem] * 2 + [vmem] * 7,
        out_specs=(vmem, pl.BlockSpec(memory_space=pl.ANY), vmem),
        scratch_shapes=[
            pltpu.VMEM((comps, groups * rows, degrees), jnp.bfloat16),
            pltpu.VMEM((comps * rows, half_cycles), jnp.float32),
            pltpu.VMEM((comps * rows, half_cycles), jnp.float32),
            pltpu.VMEM((ORD, half_cycles), jnp.float32),
            pltpu.VMEM((ORD, half_cycles), jnp.float32),
            pltpu.VMEM((ORD, half_cycles), jnp.float32),
            pltpu.VMEM((groups, degrees // BLOCK, ORD, LANES), jnp.float32),
            pltpu.VMEM((comps * rows, CHUNK * ORD), jnp.bfloat16),
            pltpu.VMEM((SLOTS, 2, half, half_cycles), jnp.bfloat16),
            pltpu.SemaphoreType.DMA((SLOTS, 2)),
        ],
        name="synthesis",
        **params(groups * chunks * 2 * comps * rows * 2 * half * half_cycles, 40 << 20),
    )(*bounds, spectra, place, orders, starts, degree_table, spread, geometry)


def run_analysis(first, radial_weight, gridded, table, kappa, gather, weights, shells, sign):
    blocks, comps, groups, rows, _ = gridded.shape
    half_cycles = weights.shape[1]
    half = CHUNK * ORD // 2
    degrees = kappa.shape[2]
    chunks = degrees // CHUNK
    width = -(-comps * rows // LANES) * LANES
    smem = pl.BlockSpec(memory_space=pltpu.SMEM)
    vmem = pl.BlockSpec(memory_space=pltpu.VMEM)
    return pl.pallas_call(
        functools.partial(analysis_kernel, comps, groups, chunks, sign),
        out_shape=(
            jax.ShapeDtypeStruct((comps, groups * rows, degrees), jnp.bfloat16),
            jax.ShapeDtypeStruct((shells, comps, groups * rows, degrees // shells), jnp.bfloat16),
        ),
        in_specs=[smem, smem, vmem, pl.BlockSpec(memory_space=pl.ANY)] + [vmem] * 3,
        out_specs=(vmem, vmem),
        scratch_shapes=[
            pltpu.VMEM((2, half_cycles, width), jnp.bfloat16),
            pltpu.VMEM((2 * half, width), jnp.bfloat16),
            pltpu.VMEM((degrees + CHUNK, width), jnp.bfloat16),
            pltpu.VMEM((SLOTS, 2, half, half_cycles), jnp.bfloat16),
            pltpu.SemaphoreType.DMA((SLOTS, 2)),
        ],
        name="analysis",
        **params(groups * chunks * 2 * comps * rows * 2 * half * half_cycles, 40 << 20),
    )(first, radial_weight, gridded, table, kappa, gather, weights)


def run_grid(received, forward, backward, viscosity, norm):
    blocks, comps, groups, rows, lanes = received[0].shape
    parts = len(received)
    packs = 2 if comps % 2 == 0 else 1
    depth = forward.shape[2]
    half_points = forward.shape[1]
    part = pl.BlockSpec((blocks, packs, groups, rows, lanes), lambda i: (0, i, 0, 0, 0))
    return pl.pallas_call(
        functools.partial(grid_kernel, norm, packs, parts),
        out_shape=[jax.ShapeDtypeStruct(received[0].shape, jnp.bfloat16)] * parts,
        grid=(comps // packs,),
        in_specs=[part] * parts
        + [whole(forward.shape), whole(backward.shape), whole(viscosity.shape)],
        out_specs=[part] * parts,
        scratch_shapes=[
            pltpu.VMEM((2, depth, packs * lanes), jnp.bfloat16),
            pltpu.VMEM((2, half_points, packs * lanes), jnp.bfloat16),
        ],
        name="grid_transforms",
        **params(8 * comps * lanes * depth * half_points, 16 << 20),
    )(*received, forward, backward, viscosity)


def run_place(kernel, place, pieces, out_shape, counts):
    vmem = pl.BlockSpec(memory_space=pltpu.VMEM)
    return pl.pallas_call(
        functools.partial(kernel, counts),
        out_shape=out_shape,
        in_specs=[vmem] * (1 + len(pieces)),
        out_specs=vmem,
        name="natural_order",
        **params(2 * place.shape[1] * math.prod(out_shape.shape), 8 << 20),
    )(place, *pieces)


def wave_tables(sorted_all, point_count, groups):
    blocks = sorted_all.shape[0]
    half_points = point_count // 2
    orders = sorted_all.reshape(blocks, 2, groups // 2, 1, ORD).transpose(1, 0, 2, 3, 4)
    shape = (2, blocks, groups // 2, 2, ORD)
    depth = math.prod(shape[1:])
    shift = jnp.arange(2, dtype=jnp.int32)[:, None] * (point_count // 4)
    lane_orders = jnp.broadcast_to(orders, shape).reshape(2, 1, depth)
    lane_shift = jnp.broadcast_to(shift, shape).reshape(2, 1, depth)

    def angle(phase):
        return (phase % point_count).astype(jnp.float32) * (2.0 * math.pi / point_count)

    def both(phase):
        return jnp.stack([jnp.cos(angle(phase)), jnp.sin(angle(phase))])

    rows = jnp.arange(ORD, dtype=jnp.int32)[None, :, None]
    forward_base = both(lane_orders * rows + lane_shift)
    forward_turn = both(lane_orders * ORD)
    row_orders = orders.reshape(2, depth // (2 * ORD), ORD, 1)
    longitudes = jnp.arange(LANES, dtype=jnp.int32)
    angles = angle(row_orders * longitudes)
    backward_base = jnp.stack([jnp.cos(angles), -jnp.sin(angles)])
    turn_shape = (2, 2, depth // (2 * ORD), ORD, LANES)
    backward_turn = jnp.broadcast_to(both(row_orders * LANES), turn_shape)
    vmem = pl.BlockSpec(memory_space=pltpu.VMEM)
    return pl.pallas_call(
        wave_kernel,
        out_shape=(
            jax.ShapeDtypeStruct((2, half_points, depth), jnp.bfloat16),
            jax.ShapeDtypeStruct((2, depth, half_points), jnp.bfloat16),
        ),
        in_specs=[vmem] * 4,
        out_specs=(vmem, vmem),
        name="waves",
        **params(8 * depth * half_points, 12 << 20),
    )(forward_base, forward_turn, backward_base, backward_turn)


def to_blocks(gridded, cycle_local):
    blocks, comps, groups, rows, _ = gridded.shape
    share = LANES // cycle_local
    if share == 1:
        return gridded
    cut = gridded.reshape(2, blocks // 2, comps, groups, rows, share, cycle_local)
    cut = cut.transpose(0, 1, 5, 2, 3, 4, 6)
    cut = jnp.stack([cut[0], jnp.flip(cut[1], axis=1)])
    return cut.reshape(blocks * share, comps, groups, rows, cycle_local)


def from_blocks(gridded, cycle_local):
    blocks, comps, groups, rows, _ = gridded.shape
    share = LANES // cycle_local
    if share == 1:
        return gridded
    cut = gridded.reshape(2, blocks // share // 2, share, comps, groups, rows, cycle_local)
    cut = jnp.stack([cut[0], jnp.flip(cut[1], axis=1)])
    cut = cut.transpose(0, 1, 3, 4, 5, 2, 6)
    return cut.reshape(blocks // share, comps, groups, rows, LANES)


def pack_comps(gridded):
    blocks, comps, groups, rows, cycle_local = gridded.shape
    if cycle_local == LANES:
        return gridded
    side = gridded.transpose(0, 2, 3, 1, 4).reshape(blocks, 1, groups, rows, comps * cycle_local)
    extra = -(comps * cycle_local) % LANES
    return jnp.pad(side, ((0, 0),) * 4 + ((0, extra),))


def unpack_comps(gridded, comps, cycle_local):
    if cycle_local == LANES:
        return gridded
    blocks, _, groups, rows, _ = gridded.shape
    side = gridded[..., : comps * cycle_local]
    side = side.reshape(blocks, groups, rows, comps, cycle_local)
    return side.transpose(0, 3, 1, 2, 4)


def shards(strain_spec, order_map, viscosity, radial_weight):
    comps, shells, slots, parts, degrees = strain_spec.shape
    block_count = lax.axis_size("blk")
    block = lax.axis_index("blk")
    cycle_local = viscosity.shape[1]
    cycle_count = cycle_local * block_count
    half_cycles = cycle_count // 2
    points = viscosity.shape[2]
    groups = slots // ORD
    chunks = degrees // CHUNK

    rank_all = rank_orders(order_map.reshape(block_count, slots))
    sorted_all = apply_rank(order_map.reshape(block_count, slots), rank_all)
    rank = lax.dynamic_index_in_dim(rank_all, block, 0, keepdims=False)
    sorted_orders = lax.dynamic_index_in_dim(sorted_all, block, 0, keepdims=False)
    by_group = sorted_orders.reshape(groups, ORD)
    first, last = by_group[:, 0] // CHUNK, by_group[:, -1] // CHUNK
    order = sorted_orders.astype(jnp.float32)
    counter = jnp.arange(1, degrees, dtype=jnp.float32)
    logs = jnp.where(counter <= order[:, None], jnp.log(1.0 - 0.5 / counter), 0.0)
    starts = 0.5 * jnp.log((2.0 * order + 1.0) / (4.0 * math.pi)) + 0.5 * jnp.sum(logs, axis=1)
    order_lanes = lane_fill(order)

    cycle_index = jnp.arange(half_cycles, dtype=jnp.float32)
    colatitude = math.pi * (2.0 * cycle_index + 1.0) / (2.0 * cycle_count)
    geometry = jnp.stack([2.0 * jnp.cos(colatitude), jnp.log(jnp.sin(colatitude))])

    row_rank = rank // ORD * (2 * ORD) + rank % ORD
    row_rank = (row_rank[:, None] + ORD * jnp.arange(2, dtype=jnp.int32)).reshape(-1)
    place = jnp.arange(slots * 2, dtype=jnp.int32)
    hit = row_rank[None, :] == place[:, None]
    my_orders = lax.dynamic_index_in_dim(
        order_map.reshape(block_count, slots), block, 0, keepdims=False
    )
    doubling = jnp.repeat(jnp.where(my_orders == 0, 1.0, 2.0), 2)
    place_in = jnp.where(hit, doubling[None, :], 0.0).astype(jnp.bfloat16)
    place_out = hit.T.astype(jnp.bfloat16)

    spectra = strain_spec.reshape(comps, slots * parts, degrees)
    part_count = min(PARTS, groups)
    part_groups = groups // part_count
    part_rows = part_groups * 2 * ORD
    sections = [slice(i * part_groups, (i + 1) * part_groups) for i in range(part_count)]
    signs = [1.0 if i < part_count // 2 else -1.0 for i in range(part_count)]
    start_lanes, degree_table, spread = lane_fill(starts), degree_rows(degrees), spread_matrix()
    received, tables = [], []
    for i, part in enumerate(sections):
        gridded, table, kappa = run_synth(
            (first[part], last[part]),
            spectra,
            place_in[i * part_rows : (i + 1) * part_rows],
            order_lanes[part],
            start_lanes[part],
            degree_table,
            spread,
            geometry,
            chunks,
            signs[i],
        )
        tables.append((table, kappa))
        arrived = lax.all_to_all(to_blocks(gridded, cycle_local), "blk", 0, 0, tiled=True)
        received.append(pack_comps(arrived))

    forward, backward = wave_tables(sorted_all, points, groups)
    weights = fejer_weights(cycle_count)[None, :]
    mirror = jnp.arange(cycle_local, dtype=jnp.int32)
    mirror = jnp.where(block * 2 < block_count, mirror, cycle_local - 1 - mirror)
    turn = (mirror[None, :] == jnp.arange(cycle_local, dtype=jnp.int32)[:, None]).astype(jnp.float32)
    local = jnp.einsum("jk,ji->ki", viscosity[0], turn, precision=lax.Precision.HIGHEST)
    if cycle_local < LANES:
        local = jnp.concatenate([local] * comps, axis=1)
        local = jnp.pad(local, ((0, 0), (0, -local.shape[1] % LANES)))
    spectrum = run_grid(received, forward, backward, local, 2.0 * math.pi / points)
    returned = [
        lax.all_to_all(unpack_comps(piece, comps, cycle_local), "blk", 0, 0, tiled=True)
        for piece in spectrum
    ]

    shell_count = lax.axis_size("shell")
    gather = gather_matrix()
    ordered, shared = [], []
    for i, part in enumerate(sections):
        table, kappa = tables[i]
        coefs, weighted = run_analysis(
            first[part],
            radial_weight,
            from_blocks(returned[i], cycle_local),
            table,
            kappa,
            gather,
            weights,
            shell_count,
            signs[i],
        )
        ordered.append(coefs)
        shared.append(lax.all_to_all(weighted, "shell", 0, 0, tiled=True))
    stress = run_place(
        unsort_kernel,
        place_out,
        ordered,
        jax.ShapeDtypeStruct((comps, slots * parts, degrees), jnp.bfloat16),
        part_rows,
    )
    integrated = run_place(
        shell_sum_kernel,
        place_out,
        shared,
        jax.ShapeDtypeStruct((comps, slots * parts, degrees // shell_count), jnp.float32),
        part_rows,
    )
    stress_spec = stress.reshape(strain_spec.shape)
    return (stress_spec, integrated.reshape(comps, slots, parts, degrees // shell_count))


def solution(mesh):
    return jax.shard_map(
        shards,
        mesh=mesh,
        in_specs=(P(None, "shell", "blk", None, None), P(), P("shell", "blk", None), P("shell")),
        out_specs=(P(None, "shell", "blk", None, None), P(None, "blk", None, "shell")),
        check_vma=False,
    )
```

time: 485 us -> 333 us (0.69)
  other arithmetic: 93.5 us -> 15.8 us
  waiting for transfers between devices: 67.9 us -> 24.3 us
  Pallas kernels: 227 us -> 190 us
  starting transfers between devices: 16.4 us -> 27.7 us
  local copies, waits for them, and re-layouts: 37.1 us -> 28.8 us
    convert_element_type x4 -> x0, other arithmetic: 65 us -> none  [the longest x1 64.4 us: values(): return jnp.cos(angles).astype(jnp.bfloat16)]
    all_to_all x2 -> x3, waiting for transfers between devices: 64.4 us -> 8.25 us  [the longest x2 8.25 us: shards(): shared.append(lax.all_to_all(weighted, 'shell', 0, 0, tiled=True))]
    all_to_all x0 -> x1, blocking collectives: none -> 41 us  [shards(): lax.all_to_all(unpack_comps(piece, comps, cycle_local), 'blk', 0, 0, tile...]
    pallas_call x3 -> x8, Pallas kernels: 227 us -> 190 us  [the longest x2 82.4 us: run_synth(): pl.pallas_call(functools.partial(synth_kernel, comps, groups, chunks, sig...]
    unnamed x1 -> x0, blocking collectives: 36.4 us -> none
    all_to_all x1 -> x2, waiting for transfers between devices: 3.5 us -> 16.1 us  [shards(): lax.all_to_all(to_blocks(gridded, cycle_local), 'blk', 0, 0, tiled=True)]
    all_to_all x1 -> x2, starting transfers between devices: 7.15 us -> 16 us  [shards(): lax.all_to_all(to_blocks(gridded, cycle_local), 'blk', 0, 0, tiled=True)]
    reshape x5 -> x2, local copies, waits for them, and re-layouts: 8.67 us -> 0.16 us  [the longest x1 0.08 us: wave_tables(): sorted_all.reshape(blocks, 2, groups // 2, 1, ORD).transpose(1, 0, 2, 3, 4)]
  transfers between devices with their start and end apart: 3 -> 5, of which waited for: 2 -> 2; matrix products, arithmetic and copies ran while one was open for 17% -> 7% of each run, Pallas kernels for 0% -> 37%
where the time goes in v2:
time: 333 us; the launch traced here: 332 us
  Pallas kernels  190 us (57%)
  blocking collectives  41 us (12%)
  local copies, waits for them, and re-layouts  28.8 us (9%)
  starting transfers between devices  27.7 us (8%)
  waiting for transfers between devices  24.3 us (7%)
  other arithmetic  15.8 us (5%)
    pallas_call x2, Pallas kernels, run_synth(): pl.pallas_call(functools.partial(synth_kernel, comps, groups, chunks, sig...  82.4 us
    pallas_call x2, Pallas kernels, run_analysis(): pl.pallas_call(functools.partial(analysis_kernel, comps, groups, chunks,...  68.5 us
    all_to_all x1, blocking collectives, shards(): lax.all_to_all(unpack_comps(piece, comps, cycle_local), 'blk', 0, 0, tile...  41 us
    pallas_call x1, Pallas kernels, run_grid(): pl.pallas_call(functools.partial(grid_kernel, norm, packs, parts), out_sh...  18.7 us
    all_to_all x2, waiting for transfers between devices, shards(): lax.all_to_all(to_blocks(gridded, cycle_local), 'blk', 0, 0, tiled=True)  16.1 us
    all_to_all x2, starting transfers between devices, shards(): lax.all_to_all(to_blocks(gridded, cycle_local), 'blk', 0, 0, tiled=True)  16 us
    pallas_call x1, Pallas kernels, wave_tables(): pl.pallas_call(wave_kernel, out_shape=(jax.ShapeDtypeStruct((2, half_poin...  10.6 us
    pallas_call x2, Pallas kernels, run_place(): pl.pallas_call(functools.partial(kernel, counts), out_shape=out_shape, in...  10.2 us
  transfers between devices with their start and end apart: 5, of which 2 were waited for; matrix products, arithmetic and copies ran while one was open for 7% of the time, Pallas kernels for 37%

profile of v2, /device:TPU:0, one launch (start us, length us, event | category | flops | bytes accessed | tf_op | source)
XLA Modules:
  0.0 331.7 jit_solution(986239753212641258)
XLA Ops:
  7.1 5.7 %reshape.646.spec_ref = bf16[6,256,1024]{2,1,0:T(8,128)(2,1)} reshape(bf16[6,1,128,2,1024]{4,3,2,1,0:T(2,128)(2,1)} %param.4) | data formatting | bytes 6291456 | tf_op jit(solution)/shard_map/reshape | solution.py:751
  15.6 1.3 broadcast_in_dim.124.degree_ref
  16.9 42.7 %synthesis.3 = (bf16[8,6,8,16,128]{4,3,2,1,0:T(8,128)(2,1)}, bf16[128,2,256,512]{3,2,1,0:T(8,128)(2,1)}, f32[8,8,1024]{2,1,0:T(8,128)}) custom-call(s32[8]{0:T(128)} %get-tuple-element.58.first_ref, s32[8]{0:T(128)} %get-tuple-element.56.last_ref, bf16[6,256,1024]{2,1,0:T(8,128)(2,1)} %reshape.646.spec_ref, bf16[128,256]{1,0:T(8,128)(2,1)} %get-tuple-element.46.place_ref, ...), custom_call_target="tpu_custom_call" | custom-call | flops 6442450944 | bytes 41943040 | tf_op jit(solution)/shard_map/synthesis/pallas_call | solution.py:544
  59.6 5.9 %all-to-all-start.1 = ((bf16[8,6,8,16,128]{4,3,2,1,0:T(8,128)(2,1)}), bf16[8,6,8,16,128]{4,3,2,1,0:T(8,128)(2,1)S(1)}, u32[]{:S(2)}, u32[]{:S(2)}) async-start(bf16[8,6,8,16,128]{4,3,2,1,0:T(8,128)(2,1)} %get-tuple-element.17), calls=%async_computation.1 | async-start | bytes 3145728 | tf_op jit(solution)/shard_map/all_to_all | solution.py:773
  67.0 39.7 %synthesis.2 = (bf16[8,6,8,16,128]{4,3,2,1,0:T(8,128)(2,1)}, bf16[128,2,256,512]{3,2,1,0:T(8,128)(2,1)}, f32[8,8,1024]{2,1,0:T(8,128)}) custom-call(s32[8]{0:T(128)} %get-tuple-element.59.first_ref, s32[8]{0:T(128)} %get-tuple-element.57.last_ref, bf16[6,256,1024]{2,1,0:T(8,128)(2,1)} %reshape.646.spec_ref, bf16[128,256]{1,0:T(8,128)(2,1)} %get-tuple-element.47.place_ref, ...), custom_call_target="tpu_custom_call" | custom-call | flops 6442450944 | bytes 41943040 | tf_op jit(solution)/shard_map/synthesis/pallas_call | solution.py:544
  107.8 10.1 %all-to-all-start = ((bf16[8,6,8,16,128]{4,3,2,1,0:T(8,128)(2,1)}), bf16[8,6,8,16,128]{4,3,2,1,0:T(8,128)(2,1)}, u32[]{:S(2)}, u32[]{:S(2)}) async-start(bf16[8,6,8,16,128]{4,3,2,1,0:T(8,128)(2,1)} %get-tuple-element.16), calls=%async_computation | async-start | bytes 3145728 | tf_op jit(solution)/shard_map/all_to_all | solution.py:773
  121.2 2.1 fusion.13
  125.7 10.6 %waves.1 = (bf16[2,1024,1024]{2,1,0:T(8,128)(2,1)}, bf16[2,1024,1024]{2,1,0:T(8,128)(2,1)}) custom-call(f32[2,2,8,1024]{3,2,1,0:T(8,128)} %pad_maximum_fusion.1.forward_base, f32[2,2,1,1024]{3,2,1,0:T(1,128)} %pad_maximum_fusion.2.forward_turn, f32[2,2,64,8,128]{4,3,2,1,0:T(8,128)} %pad_maximum_fusion.backward_base, ...), custom_call_target="tpu_custom_call" | custom-call | flops 8388608 | bytes 12582912 | tf_op jit(solution)/shard_map/waves/pallas_call | solution.py:660
  136.3 2.0 convolution_bitcast_fusion.refs_4_
  138.3 16.1 %all-to-all-done.refs_0_ = bf16[8,6,8,16,128]{4,3,2,1,0:T(8,128)(2,1)} async-done(((bf16[8,6,8,16,128]{4,3,2,1,0:T(8,128)(2,1)}), bf16[8,6,8,16,128]{4,3,2,1,0:T(8,128)(2,1)}, u32[]{:S(2)}, u32[]{:S(2)}) %all-to-all-start) | async-done | bytes 1572896 | tf_op jit(solution)/shard_map/all_to_all | solution.py:773
  154.4 18.7 %grid_transforms.1 = (bf16[8,6,8,16,128]{4,3,2,1,0:T(8,128)(2,1)}, bf16[8,6,8,16,128]{4,3,2,1,0:T(8,128)(2,1)}) custom-call(bf16[8,6,8,16,128]{4,3,2,1,0:T(8,128)(2,1)} %all-to-all-done.refs_0_, bf16[8,6,8,16,128]{4,3,2,1,0:T(8,128)(2,1)} %copy-done.3, bf16[2,1024,1024]{2,1,0:T(8,128)(2,1)} %get-tuple-element.18.refs_2_, ...), custom_call_target="tpu_custom_call" | custom-call | flops 6442450944 | bytes 16777216 | tf_op jit(solution)/shard_map/grid_transforms/pallas_call | solution.py:606
  173.1 41.0 %all_to_all.30.grid_ref = bf16[8,6,8,16,128]{4,3,2,1,0:T(8,128)(2,1)} all-to-all(bf16[8,6,8,16,128]{4,3,2,1,0:T(8,128)(2,1)} %get-tuple-element.24), channel_id=1, replica_groups=mesh['shell'=4,'blk'=8] {'blk'}, dimensions={0} | all-to-all | bytes 3145728 | tf_op jit(solution)/shard_map/all_to_all | solution.py:787
  214.0 3.6 %all-to-all-start.2 = ((bf16[8,6,8,16,128]{4,3,2,1,0:T(8,128)(2,1)}), bf16[8,6,8,16,128]{4,3,2,1,0:T(8,128)(2,1)S(1)}, u32[]{:S(2)}, u32[]{:S(2)}) async-start(bf16[8,6,8,16,128]{4,3,2,1,0:T(8,128)(2,1)} %get-tuple-element.20), calls=%async_computation.2 | async-start | bytes 3145728 | tf_op jit(solution)/shard_map/all_to_all | solution.py:787
  218.3 4.4 %fusion.6 = f32[512]{0:T(512)S(1)} fusion(f32[512]{0:T(512)S(1)} %fusion.38, s32[512]{0:T(512)S(1)} %get-tuple-element.68, s32[512]{0:T(512)S(1)} %get-tuple-element.69), kind=kLoop, calls=%fused_computation.13 | loop fusion | flops 4193792 | bytes 8192 | tf_op jit(solution)/shard_map/reduce_sum | solution.py:32
  223.3 1.5 slice_bitcast_fusion.gather_ref
  224.8 35.4 %analysis.3 = (bf16[6,128,1024]{2,1,0:T(8,128)(2,1)}, bf16[4,6,128,256]{3,2,1,0:T(8,128)(2,1)}) custom-call(s32[8]{0:T(128)} %get-tuple-element.58.first_ref, f32[1]{0:T(128)S(6)} %copy.34.radial_ref, bf16[8,6,8,16,128]{4,3,2,1,0:T(8,128)(2,1)} %all_to_all.30.grid_ref, bf16[128,2,256,512]{3,2,1,0:T(8,128)(2,1)} %get-tuple-element.25.table_ref, ...), custom_call_target="tpu_custom_call" | custom-call | flops 6442450944 | bytes 41943040 | tf_op jit(solution)/shard_map/analysis/pallas_call | solution.py:579
  261.3 3.6 %all-to-all-start.5 = ((bf16[4,6,128,256]{3,2,1,0:T(8,128)(2,1)}), bf16[4,6,128,256]{3,2,1,0:T(8,128)(2,1)S(1)}, u32[]{:S(2)}, u32[]{:S(2)}) async-start(bf16[4,6,128,256]{3,2,1,0:T(8,128)(2,1)} %get-tuple-element.29), calls=%async_computation.5 | async-start | bytes 3145728 | tf_op jit(solution)/shard_map/all_to_all | solution.py:808
  264.9 33.1 %analysis.2 = (bf16[6,128,1024]{2,1,0:T(8,128)(2,1)}, bf16[4,6,128,256]{3,2,1,0:T(8,128)(2,1)}) custom-call(s32[8]{0:T(128)} %get-tuple-element.59.first_ref, f32[1]{0:T(128)S(6)} %copy.34.radial_ref, bf16[8,6,8,16,128]{4,3,2,1,0:T(8,128)(2,1)} %copy-done.2, bf16[128,2,256,512]{3,2,1,0:T(8,128)(2,1)} %get-tuple-element.21.table_ref, ...), custom_call_target="tpu_custom_call" | custom-call | flops 6442450944 | bytes 41943040 | tf_op jit(solution)/shard_map/analysis/pallas_call | solution.py:579
  299.1 4.6 %all-to-all-start.4 = ((bf16[4,6,128,256]{3,2,1,0:T(8,128)(2,1)}), bf16[4,6,128,256]{3,2,1,0:T(8,128)(2,1)}, u32[]{:S(2)}, u32[]{:S(2)}) async-start(bf16[4,6,128,256]{3,2,1,0:T(8,128)(2,1)} %get-tuple-element.28), calls=%async_computation.4 | async-start | bytes 3145728 | tf_op jit(solution)/shard_map/all_to_all | solution.py:808
  304.5 5.4 %natural_order.2 = bf16[6,256,1024]{2,1,0:T(8,128)(2,1)} custom-call(bf16[256,256]{1,0:T(8,128)(2,1)} %fusion.14.place_ref, bf16[6,128,1024]{2,1,0:T(8,128)(2,1)} %get-tuple-element.23.refs_0_, bf16[6,128,1024]{2,1,0:T(8,128)(2,1)} %get-tuple-element.27.refs_1_), custom_call_target="tpu_custom_call" | custom-call | flops 805306368 | bytes 8388608 | tf_op jit(solution)/shard_map/natural_order/pallas_call | solution.py:624
  309.9 5.7 %reshape.648 = bf16[6,1,128,2,1024]{4,3,2,0,1:T(2,128)(2,1)} reshape(bf16[6,256,1024]{2,1,0:T(8,128)(2,1)} %natural_order.2) | data formatting | bytes 6291456 | tf_op jit(solution)/shard_map/reshape | solution.py:823
  315.6 8.2 %all-to-all-done.4.refs_0_ = bf16[4,6,128,256]{3,2,1,0:T(8,128)(2,1)} async-done(((bf16[4,6,128,256]{3,2,1,0:T(8,128)(2,1)}), bf16[4,6,128,256]{3,2,1,0:T(8,128)(2,1)}, u32[]{:S(2)}, u32[]{:S(2)}) %all-to-all-start.4) | async-done | bytes 1572896 | tf_op jit(solution)/shard_map/all_to_all | solution.py:808
  323.8 4.8 %natural_order.3 = f32[6,256,256]{2,1,0:T(8,128)} custom-call(bf16[256,256]{1,0:T(8,128)(2,1)} %fusion.14.place_ref, bf16[4,6,128,256]{3,2,1,0:T(8,128)(2,1)} %all-to-all-done.4.refs_0_, bf16[4,6,128,256]{3,2,1,0:T(8,128)(2,1)} %copy-done.1), custom_call_target="tpu_custom_call" | custom-call | flops 201326592 | bytes 8388608 | tf_op jit(solution)/shard_map/natural_order/pallas_call | solution.py:624
  328.7 3.0 reshape.649
  (81 shorter events, 20.9 us)
Async XLA Ops:
  0.6 135.7 %copy-start = (f32[1,128,2048]{2,1,0:T(8,128)S(1)}, f32[1,128,2048]{2,1,0:T(8,128)}, u32[]{:S(2)}) copy-start(f32[1,128,2048]{2,1,0:T(8,128)} %param.6) | copy-start | bytes 3145732
  59.6 47.0 %all-to-all-start.1 = ((bf16[8,6,8,16,128]{4,3,2,1,0:T(8,128)(2,1)}), bf16[8,6,8,16,128]{4,3,2,1,0:T(8,128)(2,1)S(1)}, u32[]{:S(2)}, u32[]{:S(2)}) async-start(bf16[8,6,8,16,128]{4,3,2,1,0:T(8,128)(2,1)} %get-tuple-element.17), calls=%async_computation.1 | async-start | bytes 3145728 | tf_op jit(solution)/shard_map/all_to_all | solution.py:773
  106.7 1.1 copy-start.3
  107.8 46.6 %all-to-all-start = ((bf16[8,6,8,16,128]{4,3,2,1,0:T(8,128)(2,1)}), bf16[8,6,8,16,128]{4,3,2,1,0:T(8,128)(2,1)}, u32[]{:S(2)}, u32[]{:S(2)}) async-start(bf16[8,6,8,16,128]{4,3,2,1,0:T(8,128)(2,1)} %get-tuple-element.16), calls=%async_computation | async-start | bytes 3145728 | tf_op jit(solution)/shard_map/all_to_all | solution.py:773
  214.0 46.2 %all-to-all-start.2 = ((bf16[8,6,8,16,128]{4,3,2,1,0:T(8,128)(2,1)}), bf16[8,6,8,16,128]{4,3,2,1,0:T(8,128)(2,1)S(1)}, u32[]{:S(2)}, u32[]{:S(2)}) async-start(bf16[8,6,8,16,128]{4,3,2,1,0:T(8,128)(2,1)} %get-tuple-element.20), calls=%async_computation.2 | async-start | bytes 3145728 | tf_op jit(solution)/shard_map/all_to_all | solution.py:787
  260.2 1.1 copy-start.2
  261.3 36.7 %all-to-all-start.5 = ((bf16[4,6,128,256]{3,2,1,0:T(8,128)(2,1)}), bf16[4,6,128,256]{3,2,1,0:T(8,128)(2,1)S(1)}, u32[]{:S(2)}, u32[]{:S(2)}) async-start(bf16[4,6,128,256]{3,2,1,0:T(8,128)(2,1)} %get-tuple-element.29), calls=%async_computation.5 | async-start | bytes 3145728 | tf_op jit(solution)/shard_map/all_to_all | solution.py:808
  298.0 1.1 copy-start.1
  299.1 24.7 %all-to-all-start.4 = ((bf16[4,6,128,256]{3,2,1,0:T(8,128)(2,1)}), bf16[4,6,128,256]{3,2,1,0:T(8,128)(2,1)}, u32[]{:S(2)}, u32[]{:S(2)}) async-start(bf16[4,6,128,256]{3,2,1,0:T(8,128)(2,1)} %get-tuple-element.28), calls=%async_computation.4 | async-start | bytes 3145728 | tf_op jit(solution)/shard_map/all_to_all | solution.py:808

commit v3 on v2

--- a/solution.py
+++ b/solution.py
@@ -13,11 +13,11 @@
 log_jump = 40.0 * math.log(2.0)
 
 ORD = 8
-CHUNK = 64
+CHUNK = 128
 BLOCK = 16
 LANES = 128
+TILE = 256
 SLOTS = 4
-PARTS = 2
 VMEM_LIMIT = 56 * 1024 * 1024
 
 
@@ -50,17 +50,12 @@
     return jnp.broadcast_to(values.reshape(-1, ORD, 1), (values.shape[0] // ORD, ORD, LANES))
 
 
-def spread_matrix():
+def gather_matrix():
     place = jnp.arange(CHUNK * ORD, dtype=jnp.int32)
     parity = place // (CHUNK * ORD // 2)
     degree = 2 * (place % (CHUNK * ORD // 2) // ORD) + parity
-    half = jnp.arange(LANES // CHUNK, dtype=jnp.int32)[:, None, None]
-    row = jnp.arange(LANES, dtype=jnp.int32)[None, :, None]
-    return (row - CHUNK * half == degree[None, None, :]).astype(jnp.bfloat16)
-
-
-def gather_matrix():
-    return spread_matrix()[0, :CHUNK, :]
+    row = jnp.arange(CHUNK, dtype=jnp.int32)
+    return (row[:, None] == degree[None, :]).astype(jnp.bfloat16)
 
 
 def degree_rows(degree_count):
@@ -90,13 +85,11 @@
     chunks,
     sign,
     first_ref,
-    last_ref,
     spec_ref,
     place_ref,
     order_ref,
     start_ref,
     degree_ref,
-    spread_ref,
     geometry_ref,
     out_ref,
     table_ref,
@@ -110,6 +103,7 @@
     end_ref,
     wide_ref,
     buffer_ref,
+    second_ref,
     sems,
 ):
     rows = 2 * ORD
@@ -140,25 +134,26 @@
     even_ref[...] = jnp.zeros_like(even_ref)
     odd_ref[...] = jnp.zeros_like(odd_ref)
     wide_ref[...] = jnp.zeros_like(wide_ref)
-    buffer_ref[SLOTS - 1] = jnp.zeros_like(buffer_ref[SLOTS - 1])
-
-    def table_copies(item, slot):
+    second_ref[SLOTS // 2 - 1] = jnp.zeros_like(second_ref[SLOTS // 2 - 1])
+
+    def table_copies(item, slot, which):
+        offset = 0 if which is buffer_ref else SLOTS // 2
         return [
             pltpu.make_async_copy(
-                buffer_ref.at[slot, p], table_ref.at[item, p], sems.at[slot, p]
+                which.at[slot, p], table_ref.at[item, p], sems.at[slot + offset, p]
             )
             for p in range(2)
         ]
 
-    def products(slot):
+    def products(other, before):
         even_ref[...] += jnp.dot(
-            wide_ref[:, :half], buffer_ref[slot, 0], preferred_element_type=jnp.float32
+            wide_ref[:, :half], other[before, 0], preferred_element_type=jnp.float32
         )
         odd_ref[...] += jnp.dot(
-            wide_ref[:, half:], buffer_ref[slot, 1], preferred_element_type=jnp.float32
+            wide_ref[:, half:], other[before, 1], preferred_element_type=jnp.float32
         )
 
-    def recursion(seeded, group, chunk, slot):
+    def recursion(group, chunk, slot, mine):
         order = order_ref[group]
         begin = chunk * CHUNK
         odd_chunk = lax.rem(chunk, LANES // CHUNK)
@@ -179,15 +174,14 @@
                 two = degree_ref[1, pl.ds(begin + step, 1), :]
                 coef = jnp.concatenate([one - two * square] * lane_blocks, axis=1)
                 now = twice * last - coef * prev
-                if seeded:
-                    now = jnp.where(seed_at == float(step), 1.0, now)
+                now = jnp.where(seed_at == float(step), 1.0, now)
                 held.append(now * scale)
                 prev, last = last, now
             for p in range(2):
                 for i in range(p, BLOCK, 4):
                     pair = jnp.concatenate([held[i], held[i + 2]], axis=0).astype(jnp.bfloat16)
                     at = (b * BLOCK + i - p) // 2 * ORD
-                    buffer_ref[slot, p, at : at + 2 * ORD, :] = pair
+                    mine[slot, p, at : at + 2 * ORD, :] = pair
             end = end_ref[group, chunk * (CHUNK // BLOCK) + b]
             end = jnp.concatenate([end] * lane_blocks, axis=1)
             last = last * end
@@ -209,10 +203,15 @@
             ],
             axis=0,
         )
-        wide = jnp.dot(piece, spread_ref[odd_chunk], preferred_element_type=jnp.float32)
+        lane_at = lax.broadcasted_iota(jnp.int32, (rows, LANES), 1)
         for c in range(comps):
-            at = slice(c * rows, (c + 1) * rows)
-            wide_ref[at, :] = (wide[at] * mask).astype(jnp.bfloat16)
+            source = piece[c * rows : (c + 1) * rows].astype(jnp.float32)
+            for q in range(CHUNK * ORD // LANES):
+                p, t = q // (CHUNK * ORD // LANES // 2), q % (CHUNK * ORD // LANES // 2)
+                index = 2 * (lane_at // ORD + t * (LANES // ORD)) + p + odd_chunk * CHUNK
+                moved = jnp.take_along_axis(source, index, axis=1)
+                lanes = slice(q * LANES, (q + 1) * LANES)
+                wide_ref[c * rows : (c + 1) * rows, lanes] = (moved * mask[:, lanes]).astype(jnp.bfloat16)
 
     def finish(group):
         for c in range(comps):
@@ -229,13 +228,13 @@
 
     def body(item, carry):
         before_group, before_chunk, group, chunk = carry
-        slot = lax.rem(item, SLOTS)
-        before = lax.rem(item + SLOTS - 1, SLOTS)
-
-        @pl.when(item >= SLOTS)
-        def _():
-            for copy in table_copies(item - SLOTS, slot):
-                copy.wait()
+        for parity in range(2):
+
+            @pl.when(jnp.logical_and(item >= SLOTS, lax.rem(item, 2) == parity))
+            def _(parity=parity):
+                which = second_ref if parity else buffer_ref
+                for copy in table_copies(item - SLOTS, lax.rem(item // 2, SLOTS // 2), which):
+                    copy.wait()
 
         @pl.when(chunk == first_ref[group])
         def _():
@@ -245,18 +244,17 @@
             wide_start = jnp.concatenate([start_ref[group]] * lane_blocks, axis=1)
             log_ref[...] = wide_start + wide_order * geometry_ref[1:2, :]
 
-        @pl.when(chunk <= last_ref[group])
-        def _():
-            products(before)
-            recursion(True, group, chunk, slot)
-
-        @pl.when(chunk > last_ref[group])
-        def _():
-            products(before)
-            recursion(False, group, chunk, slot)
-
-        for copy in table_copies(item, slot):
-            copy.start()
+        for parity in range(2):
+
+            @pl.when(lax.rem(item, 2) == parity)
+            def _(parity=parity):
+                mine, other = (buffer_ref, second_ref) if parity == 0 else (second_ref, buffer_ref)
+                place = lax.rem(item // 2, SLOTS // 2)
+                before = lax.rem((item + SLOTS - 1) // 2, SLOTS // 2)
+                products(other, before)
+                recursion(group, chunk, place, mine)
+                for copy in table_copies(item, place, mine):
+                    copy.start()
 
         @pl.when(jnp.logical_and(before_chunk == chunks - 1, item > 0))
         def _():
@@ -269,14 +267,22 @@
 
     zero = jnp.int32(0)
     lax.fori_loop(0, count, body, (zero, zero, zero, first_ref[0]))
-    products(lax.rem(count - 1, SLOTS))
+    for parity in range(2):
+        which = second_ref if parity else buffer_ref
+
+        @pl.when(lax.rem(count - 1, 2) == parity)
+        def _(which=which):
+            products(which, lax.rem((count - 1) // 2, SLOTS // 2))
+
+        for back in range(SLOTS, 0, -1):
+            item = count - back
+
+            @pl.when(jnp.logical_and(item >= 0, lax.rem(item + SLOTS, 2) == parity))
+            def _(item=item, which=which):
+                for copy in table_copies(item, lax.rem(item // 2, SLOTS // 2), which):
+                    copy.wait()
+
     finish(jnp.int32(groups - 1))
-    for back in range(SLOTS, 0, -1):
-
-        @pl.when(count >= back)
-        def _():
-            for copy in table_copies(count - back, lax.rem(count - back, SLOTS)):
-                copy.wait()
 
 
 def analysis_kernel(
@@ -311,11 +317,6 @@
     own = lax.broadcasted_iota(jnp.int32, shape, 0) == lane % ORD
     mask = jnp.where(own, 1.0, 0.0)
     mask = jnp.concatenate([mask] * (half // ORD), axis=0)
-    unit = (
-        lax.broadcasted_iota(jnp.int32, (width, width), 0)
-        == lax.broadcasted_iota(jnp.int32, (width, width), 1)
-    ).astype(jnp.bfloat16)
-    contract = (((1,), (1,)), ((), ()))
     wide_ref[...] = jnp.zeros_like(wide_ref)
     radial = radial_ref[0]
     shells, share = shared_ref.shape[0], shared_ref.shape[3]
@@ -370,16 +371,14 @@
             fill = jnp.zeros((width - comps * rows, LANES), jnp.float32)
             north = jnp.concatenate(norths + [fill], axis=0)
             south = jnp.concatenate(souths + [fill], axis=0)
-            side_ref[0, lanes, :] = (weight * (north + south)).T.astype(jnp.bfloat16)
-            side_ref[1, lanes, :] = (weight * (north - south)).T.astype(jnp.bfloat16)
+            side_ref[0, lanes, :] = (weight * (north + south)).astype(jnp.bfloat16).T
+            side_ref[1, lanes, :] = (weight * (north - south)).astype(jnp.bfloat16).T
         found_ref[...] = jnp.zeros_like(found_ref)
         item, before = lax.fori_loop(
             first_ref[group], chunks, functools.partial(advance, group), (item, jnp.int32(chunks))
         )
         narrow(before)
-        turned = lax.dot_general(
-            unit, found_ref[:degrees], contract, preferred_element_type=jnp.float32
-        )
+        turned = found_ref[:degrees].T.astype(jnp.float32)
         kappa = kappa_ref[group]
         at = pl.multiple_of(group * rows, rows)
         factors = jnp.concatenate([kappa, kappa], axis=0)
@@ -463,62 +462,81 @@
     lax.fori_loop(0, 2 * count, backward_rows, 0)
 
 
-def grid_kernel(norm, packs, parts, *refs):
-    grid_refs, out_refs = refs[:parts], refs[parts + 3 : 2 * parts + 3]
-    forward_ref, backward_ref, viscosity_ref = refs[parts : parts + 3]
-    field_ref, stress_ref = refs[2 * parts + 3 :]
-    blocks, _, groups, rows, lanes = grid_refs[0].shape
-    halves = parts // 2
-    step_rows = halves * groups * rows
-    points = forward_ref.shape[1]
-    tile = 256
-    for part, grid_ref in enumerate(grid_refs):
-        p, offset = part // halves, part % halves * groups * rows
+def lay_field(grid_ref, field_ref):
+    blocks, packs, groups, rows, lanes = grid_ref.shape
+    for w in range(packs):
+        for d in range(blocks):
+            at = d * groups * rows
+            field_ref[at : at + groups * rows, w * lanes : (w + 1) * lanes] = grid_ref[
+                d, w
+            ].reshape(groups * rows, lanes)
+
+
+def even_field_kernel(grid_ref, forward_ref, even_ref, field_ref):
+    lay_field(grid_ref, field_ref)
+
+    def step(i, carry):
+        at = pl.multiple_of(i * TILE, TILE)
+        even_ref[0, pl.ds(at, TILE), :] = jnp.dot(
+            forward_ref[pl.ds(at, TILE), :], field_ref[...], preferred_element_type=jnp.float32
+        )
+        return carry
+
+    lax.fori_loop(0, forward_ref.shape[0] // TILE, step, 0)
+
+
+def lay_spectrum(norm, wave_ref, stress, out_ref):
+    blocks, packs, groups, rows, lanes = out_ref.shape
+    count = groups * rows
+
+    def step(d, carry):
+        at = pl.multiple_of(d * count, count)
+        found = jnp.dot(
+            wave_ref[pl.ds(at, count), :], stress[...], preferred_element_type=jnp.float32
+        )
+        found = (found * norm).astype(jnp.bfloat16)
         for w in range(packs):
-            for d in range(blocks):
-                at = d * step_rows + offset
-                field_ref[p, at : at + groups * rows, w * lanes : (w + 1) * lanes] = grid_ref[
-                    d, w
-                ].reshape(groups * rows, lanes)
-
-    def points_step(i, carry):
-        at = pl.multiple_of(i * tile, tile)
-        even = jnp.dot(
-            forward_ref[0, pl.ds(at, tile), :], field_ref[0], preferred_element_type=jnp.float32
-        )
-        odd = jnp.dot(
-            forward_ref[1, pl.ds(at, tile), :], field_ref[1], preferred_element_type=jnp.float32
-        )
-        near = viscosity_ref[pl.ds(at, tile), :]
-        far = viscosity_ref[pl.ds(points + at, tile), :]
-        if packs > 1:
-            near = jnp.concatenate([near] * packs, axis=1)
-            far = jnp.concatenate([far] * packs, axis=1)
+            out_ref[d, w] = found[:, w * lanes : (w + 1) * lanes].reshape(groups, rows, lanes)
+        return carry
+
+    lax.fori_loop(0, blocks, step, 0)
+
+
+def stress_kernel(
+    norm,
+    grid_ref,
+    even_ref,
+    forward_ref,
+    backward_ref,
+    viscosity_ref,
+    out_ref,
+    difference_ref,
+    field_ref,
+    sum_ref,
+):
+    packs = grid_ref.shape[1]
+    points = forward_ref.shape[0]
+    lay_field(grid_ref, field_ref)
+
+    def step(i, carry):
+        at = pl.multiple_of(i * TILE, TILE)
+        rows = pl.ds(at, TILE)
+        even = even_ref[0, rows, :]
+        odd = jnp.dot(forward_ref[rows, :], field_ref[...], preferred_element_type=jnp.float32)
+        near = jnp.concatenate([viscosity_ref[rows, :]] * packs, axis=1)
+        far = jnp.concatenate([viscosity_ref[pl.ds(points + at, TILE), :]] * packs, axis=1)
         near = (near * (even + odd)).astype(jnp.bfloat16).astype(jnp.float32)
         far = (far * (even - odd)).astype(jnp.bfloat16).astype(jnp.float32)
-        stress_ref[0, pl.ds(at, tile), :] = (near + far).astype(jnp.bfloat16)
-        stress_ref[1, pl.ds(at, tile), :] = (near - far).astype(jnp.bfloat16)
+        sum_ref[rows, :] = (near + far).astype(jnp.bfloat16)
+        difference_ref[0, rows, :] = (near - far).astype(jnp.bfloat16)
         return carry
 
-    lax.fori_loop(0, points // tile, points_step, 0)
-    def orders_step(d, carry):
-        for p in range(2):
-            at = pl.multiple_of(d * step_rows, step_rows)
-            found = jnp.dot(
-                backward_ref[p, pl.ds(at, step_rows), :],
-                stress_ref[p],
-                preferred_element_type=jnp.float32,
-            )
-            found = (found * norm).astype(jnp.bfloat16)
-            for h in range(halves):
-                piece = found[h * groups * rows : (h + 1) * groups * rows]
-                for w in range(packs):
-                    out_refs[p * halves + h][d, w] = piece[:, w * lanes : (w + 1) * lanes].reshape(
-                        groups, rows, lanes
-                    )
-        return carry
-
-    lax.fori_loop(0, blocks, orders_step, 0)
+    lax.fori_loop(0, points // TILE, step, 0)
+    lay_spectrum(norm, backward_ref, sum_ref, out_ref)
+
+
+def odd_spectrum_kernel(norm, difference_ref, backward_ref, out_ref):
+    lay_spectrum(norm, backward_ref, difference_ref.at[0], out_ref)
 
 
 def whole(shape):
@@ -532,7 +550,7 @@
     )
 
 
-def run_synth(bounds, spectra, place, orders, starts, degree_table, spread, geometry, chunks, sign):
+def run_synth(first, spectra, place, orders, starts, degree_table, geometry, chunks, sign):
     comps, slots, degrees = spectra.shape
     groups = orders.shape[0]
     half_cycles = geometry.shape[1]
@@ -548,7 +566,7 @@
             jax.ShapeDtypeStruct((groups * chunks, 2, half, half_cycles), jnp.bfloat16),
             jax.ShapeDtypeStruct((groups, ORD, degrees), jnp.float32),
         ),
-        in_specs=[smem] * 2 + [vmem] * 7,
+        in_specs=[smem] + [vmem] * 6,
         out_specs=(vmem, pl.BlockSpec(memory_space=pl.ANY), vmem),
         scratch_shapes=[
             pltpu.VMEM((comps, groups * rows, degrees), jnp.bfloat16),
@@ -559,12 +577,13 @@
             pltpu.VMEM((ORD, half_cycles), jnp.float32),
             pltpu.VMEM((groups, degrees // BLOCK, ORD, LANES), jnp.float32),
             pltpu.VMEM((comps * rows, CHUNK * ORD), jnp.bfloat16),
-            pltpu.VMEM((SLOTS, 2, half, half_cycles), jnp.bfloat16),
+            pltpu.VMEM((SLOTS // 2, 2, half, half_cycles), jnp.bfloat16),
+            pltpu.VMEM((SLOTS // 2, 2, half, half_cycles), jnp.bfloat16),
             pltpu.SemaphoreType.DMA((SLOTS, 2)),
         ],
         name="synthesis",
         **params(groups * chunks * 2 * comps * rows * 2 * half * half_cycles, 40 << 20),
-    )(*bounds, spectra, place, orders, starts, degree_table, spread, geometry)
+    )(first, spectra, place, orders, starts, degree_table, geometry)
 
 
 def run_analysis(first, radial_weight, gridded, table, kappa, gather, weights, shells, sign):
@@ -598,25 +617,61 @@
 
 def run_grid(received, forward, backward, viscosity, norm):
     blocks, comps, groups, rows, lanes = received[0].shape
-    parts = len(received)
     packs = 2 if comps % 2 == 0 else 1
-    depth = forward.shape[2]
-    half_points = forward.shape[1]
+    steps = comps // packs
+    _, half_points, depth = forward.shape
+    width = packs * lanes
     part = pl.BlockSpec((blocks, packs, groups, rows, lanes), lambda i: (0, i, 0, 0, 0))
-    return pl.pallas_call(
-        functools.partial(grid_kernel, norm, packs, parts),
-        out_shape=[jax.ShapeDtypeStruct(received[0].shape, jnp.bfloat16)] * parts,
-        grid=(comps // packs,),
-        in_specs=[part] * parts
-        + [whole(forward.shape), whole(backward.shape), whole(viscosity.shape)],
-        out_specs=[part] * parts,
+    field = pl.BlockSpec((1, half_points, width), lambda i: (i, 0, 0))
+
+    def wave(p, shape):
+        return pl.BlockSpec((None,) + shape, lambda i: (p, 0, 0))
+
+    forward_shape, backward_shape = (half_points, depth), (depth, half_points)
+    spectrum_type = jax.ShapeDtypeStruct(received[0].shape, jnp.bfloat16)
+    one_product = 2 * steps * width * depth * half_points
+    even = pl.pallas_call(
+        even_field_kernel,
+        out_shape=jax.ShapeDtypeStruct((steps, half_points, width), jnp.float32),
+        grid=(steps,),
+        in_specs=[part, wave(0, forward_shape)],
+        out_specs=field,
+        scratch_shapes=[pltpu.VMEM((depth, width), jnp.bfloat16)],
+        name="even_field",
+        **params(one_product, 8 << 20),
+    )(received[0], forward)
+    first, difference = pl.pallas_call(
+        functools.partial(stress_kernel, norm),
+        out_shape=(
+            spectrum_type,
+            jax.ShapeDtypeStruct((steps, half_points, width), jnp.bfloat16),
+        ),
+        grid=(steps,),
+        in_specs=[
+            part,
+            field,
+            wave(1, forward_shape),
+            wave(0, backward_shape),
+            whole(viscosity.shape),
+        ],
+        out_specs=(part, field),
         scratch_shapes=[
-            pltpu.VMEM((2, depth, packs * lanes), jnp.bfloat16),
-            pltpu.VMEM((2, half_points, packs * lanes), jnp.bfloat16),
+            pltpu.VMEM((depth, width), jnp.bfloat16),
+            pltpu.VMEM((half_points, width), jnp.bfloat16),
         ],
-        name="grid_transforms",
-        **params(8 * comps * lanes * depth * half_points, 16 << 20),
-    )(*received, forward, backward, viscosity)
+        name="stress",
+        **params(2 * one_product, 16 << 20),
+    )(received[1], even, forward, backward, viscosity)
+    second = pl.pallas_call(
+        functools.partial(odd_spectrum_kernel, norm),
+        out_shape=spectrum_type,
+        grid=(steps,),
+        in_specs=[field, wave(1, backward_shape)],
+        out_specs=part,
+        name="odd_spectrum",
+        **params(one_product, 6 << 20),
+    )(difference, backward)
+    return [first, second]
 
 
 def run_place(kernel, place, pieces, out_shape, counts):
@@ -726,7 +781,7 @@
     rank = lax.dynamic_index_in_dim(rank_all, block, 0, keepdims=False)
     sorted_orders = lax.dynamic_index_in_dim(sorted_all, block, 0, keepdims=False)
     by_group = sorted_orders.reshape(groups, ORD)
-    first, last = by_group[:, 0] // CHUNK, by_group[:, -1] // CHUNK
+    first = by_group[:, 0] // CHUNK
     order = sorted_orders.astype(jnp.float32)
     counter = jnp.arange(1, degrees, dtype=jnp.float32)
     logs = jnp.where(counter <= order[:, None], jnp.log(1.0 - 0.5 / counter), 0.0)
@@ -749,22 +804,21 @@
     place_out = hit.T.astype(jnp.bfloat16)
 
     spectra = strain_spec.reshape(comps, slots * parts, degrees)
-    part_count = min(PARTS, groups)
+    part_count = 2
     part_groups = groups // part_count
     part_rows = part_groups * 2 * ORD
     sections = [slice(i * part_groups, (i + 1) * part_groups) for i in range(part_count)]
     signs = [1.0 if i < part_count // 2 else -1.0 for i in range(part_count)]
-    start_lanes, degree_table, spread = lane_fill(starts), degree_rows(degrees), spread_matrix()
+    start_lanes, degree_table = lane_fill(starts), degree_rows(degrees)
     received, tables = [], []
     for i, part in enumerate(sections):
         gridded, table, kappa = run_synth(
-            (first[part], last[part]),
+            first[part],
             spectra,
             place_in[i * part_rows : (i + 1) * part_rows],
             order_lanes[part],
             start_lanes[part],
             degree_table,
-            spread,
             geometry,
             chunks,
             signs[i],
@@ -775,6 +829,8 @@
 
     forward, backward = wave_tables(sorted_all, points, groups)
     weights = fejer_weights(cycle_count)[None, :]
+    gather = gather_matrix()
+    forward, weights, gather = lax.optimization_barrier((forward, weights, gather))
     mirror = jnp.arange(cycle_local, dtype=jnp.int32)
     mirror = jnp.where(block * 2 < block_count, mirror, cycle_local - 1 - mirror)
     turn = (mirror[None, :] == jnp.arange(cycle_local, dtype=jnp.int32)[:, None]).astype(jnp.float32)
@@ -789,7 +845,6 @@
     ]
 
     shell_count = lax.axis_size("shell")
-    gather = gather_matrix()
     ordered, shared = [], []
     for i, part in enumerate(sections):
         table, kappa = tables[i]

time: 333 us -> 307 us (0.922)
  blocking collectives: 41 us -> 0 us
  waiting for transfers between devices: 24.3 us -> 49.7 us
  Pallas kernels: 190 us -> 178 us
    all_to_all x1 -> x0, blocking collectives: 41 us -> none  [shards(): lax.all_to_all(unpack_comps(piece, comps, cycle_local), 'blk', 0, 0, tile...]
    all_to_all x1 -> x2, waiting for transfers between devices: 0.01 us -> 35.7 us  [shards(): lax.all_to_all(unpack_comps(piece, comps, cycle_local), 'blk', 0, 0, tile...]
    pallas_call x2, Pallas kernels: 68.5 us -> 55.9 us  [run_analysis(): pl.pallas_call(functools.partial(analysis_kernel, comps, groups, chunks,...]
    pallas_call x2, Pallas kernels: 82.4 us -> 71.8 us  [run_synth(): pl.pallas_call(functools.partial(synth_kernel, comps, groups, chunks, sig...]
    pallas_call x1 -> x3, Pallas kernels: 18.7 us -> 29.2 us  [the longest x1 14.1 us: run_grid(): pl.pallas_call(functools.partial(stress_kernel, norm), out_shape=(spectru...]
    all_to_all x2, waiting for transfers between devices: 16.1 us -> 5.71 us  [shards(): lax.all_to_all(to_blocks(gridded, cycle_local), 'blk', 0, 0, tiled=True)]
    all_to_all x1 -> x2, starting transfers between devices: 3.58 us -> 7.27 us  [shards(): lax.all_to_all(unpack_comps(piece, comps, cycle_local), 'blk', 0, 0, tile...]
  transfers between devices with their start and end apart: 5 -> 6, of which waited for: 2 -> 5; matrix products, arithmetic and copies ran while one was open for 7% -> 8% of each run, Pallas kernels for 37% -> 40%
where the time goes in v3:
time: 307 us; the launch traced here: 304 us
  Pallas kernels  178 us (58%)
  waiting for transfers between devices  49.7 us (16%)
  local copies, waits for them, and re-layouts  29.2 us (10%)
  starting transfers between devices  28.1 us (9%)
  other arithmetic  15.6 us (5%)
    pallas_call x2, Pallas kernels, run_synth(): pl.pallas_call(functools.partial(synth_kernel, comps, groups, chunks, sig...  71.8 us
    pallas_call x2, Pallas kernels, run_analysis(): pl.pallas_call(functools.partial(analysis_kernel, comps, groups, chunks,...  55.9 us
    all_to_all x2, waiting for transfers between devices, shards(): lax.all_to_all(unpack_comps(piece, comps, cycle_local), 'blk', 0, 0, tile...  35.7 us
    pallas_call x1, Pallas kernels, run_grid(): pl.pallas_call(functools.partial(stress_kernel, norm), out_shape=(spectru...  14.1 us
    all_to_all x2, starting transfers between devices, shards(): lax.all_to_all(to_blocks(gridded, cycle_local), 'blk', 0, 0, tiled=True)  12.7 us
    pallas_call x1, Pallas kernels, wave_tables(): pl.pallas_call(wave_kernel, out_shape=(jax.ShapeDtypeStruct((2, half_poin...  10.6 us
    pallas_call x2, Pallas kernels, run_place(): pl.pallas_call(functools.partial(kernel, counts), out_shape=out_shape, in...  10.2 us
    pallas_call x1, Pallas kernels, run_grid(): pl.pallas_call(functools.partial(odd_spectrum_kernel, norm), out_shape=sp...  8.35 us
  transfers between devices with their start and end apart: 6, of which 5 were waited for; matrix products, arithmetic and copies ran while one was open for 8% of the time, Pallas kernels for 40%

profile of v3, /device:TPU:0, one launch (start us, length us, event | category | flops | bytes accessed | tf_op | source)
XLA Modules:
  0.0 303.9 jit_solution(14473931727415015180)
XLA Ops:
  4.9 5.7 %reshape.617.spec_ref = bf16[6,256,1024]{2,1,0:T(8,128)(2,1)} reshape(bf16[6,1,128,2,1024]{4,3,2,1,0:T(2,128)(2,1)} %param.4) | data formatting | bytes 6291456 | tf_op jit(solution)/shard_map/reshape | solution.py:806
  15.4 38.4 %synthesis.3 = (bf16[8,6,8,16,128]{4,3,2,1,0:T(8,128)(2,1)}, bf16[64,2,512,512]{3,2,1,0:T(8,128)(2,1)}, f32[8,8,1024]{2,1,0:T(8,128)}) custom-call(s32[8]{0:T(128)} %get-tuple-element.61.first_ref, bf16[6,256,1024]{2,1,0:T(8,128)(2,1)} %reshape.617.spec_ref, bf16[128,256]{1,0:T(8,128)(2,1)} %get-tuple-element.50.place_ref, ...), custom_call_target="tpu_custom_call" | custom-call | flops 6442450944 | bytes 41943040 | tf_op jit(solution)/shard_map/synthesis/pallas_call | solution.py:562
  53.9 4.6 %all-to-all-start.1 = ((bf16[8,6,8,16,128]{4,3,2,1,0:T(8,128)(2,1)}), bf16[8,6,8,16,128]{4,3,2,1,0:T(8,128)(2,1)S(1)}, u32[]{:S(2)}, u32[]{:S(2)}) async-start(bf16[8,6,8,16,128]{4,3,2,1,0:T(8,128)(2,1)} %get-tuple-element.20), calls=%async_computation.1 | async-start | bytes 3145728 | tf_op jit(solution)/shard_map/all_to_all | solution.py:827
  60.8 33.3 %synthesis.2 = (bf16[8,6,8,16,128]{4,3,2,1,0:T(8,128)(2,1)}, bf16[64,2,512,512]{3,2,1,0:T(8,128)(2,1)}, f32[8,8,1024]{2,1,0:T(8,128)}) custom-call(s32[8]{0:T(128)} %get-tuple-element.60.first_ref, bf16[6,256,1024]{2,1,0:T(8,128)(2,1)} %reshape.617.spec_ref, bf16[128,256]{1,0:T(8,128)(2,1)} %get-tuple-element.51.place_ref, ...), custom_call_target="tpu_custom_call" | custom-call | flops 6442450944 | bytes 41943040 | tf_op jit(solution)/shard_map/synthesis/pallas_call | solution.py:562
  96.6 8.2 %all-to-all-start = ((bf16[8,6,8,16,128]{4,3,2,1,0:T(8,128)(2,1)}), bf16[8,6,8,16,128]{4,3,2,1,0:T(8,128)(2,1)S(1)}, u32[]{:S(2)}, u32[]{:S(2)}) async-start(bf16[8,6,8,16,128]{4,3,2,1,0:T(8,128)(2,1)} %get-tuple-element.19), calls=%async_computation | async-start | bytes 3145728 | tf_op jit(solution)/shard_map/all_to_all | solution.py:827
  111.6 10.6 %waves.1 = (bf16[2,1024,1024]{2,1,0:T(8,128)(2,1)}, bf16[2,1024,1024]{2,1,0:T(8,128)(2,1)}) custom-call(f32[2,2,8,1024]{3,2,1,0:T(8,128)} %pad_maximum_fusion.1.forward_base, f32[2,2,1,1024]{3,2,1,0:T(1,128)} %pad_maximum_fusion.2.forward_turn, f32[2,2,64,8,128]{4,3,2,1,0:T(8,128)} %pad_maximum_fusion.backward_base, ...), custom_call_target="tpu_custom_call" | custom-call | flops 8388608 | bytes 12582912 | tf_op jit(solution)/shard_map/waves/pallas_call | solution.py:715
  122.3 4.4 %fusion.6 = f32[512]{0:T(512)S(1)} fusion(f32[512]{0:T(512)S(1)} %fusion.46, s32[512]{0:T(512)S(1)} %get-tuple-element.68, s32[512]{0:T(512)S(1)} %get-tuple-element.69), kind=kLoop, calls=%fused_computation.13 | loop fusion | flops 4193792 | bytes 8192 | tf_op jit(solution)/shard_map/reduce_sum | solution.py:32
  130.0 6.8 %even_field.1.even_ref = f32[3,1024,256]{2,1,0:T(8,128)} custom-call(bf16[8,6,8,16,128]{4,3,2,1,0:T(8,128)(2,1)} %copy-done.3, bf16[2,1024,1024]{2,1,0:T(8,128)(2,1)} %get-tuple-element.22.forward_ref), custom_call_target="tpu_custom_call" | custom-call | flops 1610612736 | bytes 8388608 | tf_op jit(solution)/shard_map/even_field/pallas_call | solution.py:633
  136.8 4.4 %all-to-all-done.grid_ref = bf16[8,6,8,16,128]{4,3,2,1,0:T(8,128)(2,1)S(1)} async-done(((bf16[8,6,8,16,128]{4,3,2,1,0:T(8,128)(2,1)}), bf16[8,6,8,16,128]{4,3,2,1,0:T(8,128)(2,1)S(1)}, u32[]{:S(2)}, u32[]{:S(2)}) %all-to-all-start) | async-done | bytes 1572896 | tf_op jit(solution)/shard_map/all_to_all | solution.py:827
  142.4 14.1 %stress.1 = (bf16[8,6,8,16,128]{4,3,2,1,0:T(8,128)(2,1)}, bf16[3,1024,256]{2,1,0:T(8,128)(2,1)}) custom-call(bf16[8,6,8,16,128]{4,3,2,1,0:T(8,128)(2,1)} %copy-done.1, f32[3,1024,256]{2,1,0:T(8,128)} %even_field.1.even_ref, bf16[2,1024,1024]{2,1,0:T(8,128)(2,1)} %get-tuple-element.22.forward_ref, bf16[2,1024,1024]{2,1,0:T(8,128)(2,1)} %get-tuple-element.23.backward_ref, ...), custom_call_target="tpu_custom_call" | custom-call | flops 3221225472 | bytes 16777216 | tf_op jit(solution)/shard_map/stress/pallas_call | solution.py:643
  156.5 3.6 %all-to-all-start.2 = ((bf16[8,6,8,16,128]{4,3,2,1,0:T(8,128)(2,1)}), bf16[8,6,8,16,128]{4,3,2,1,0:T(8,128)(2,1)S(1)}, u32[]{:S(2)}, u32[]{:S(2)}) async-start(bf16[8,6,8,16,128]{4,3,2,1,0:T(8,128)(2,1)} %get-tuple-element.24), calls=%async_computation.2 | async-start | bytes 3145728 | tf_op jit(solution)/shard_map/all_to_all | solution.py:843
  160.1 8.3 %odd_spectrum.1 = bf16[8,6,8,16,128]{4,3,2,1,0:T(8,128)(2,1)} custom-call(bf16[3,1024,256]{2,1,0:T(8,128)(2,1)} %get-tuple-element.30.difference_ref, bf16[2,1024,1024]{2,1,0:T(8,128)(2,1)} %get-tuple-element.23.backward_ref), custom_call_target="tpu_custom_call" | custom-call | flops 1610612736 | bytes 6291456 | tf_op jit(solution)/shard_map/odd_spectrum/pallas_call | solution.py:665
  168.5 28.8 %all-to-all-done.2.grid_ref = bf16[8,6,8,16,128]{4,3,2,1,0:T(8,128)(2,1)S(1)} async-done(((bf16[8,6,8,16,128]{4,3,2,1,0:T(8,128)(2,1)}), bf16[8,6,8,16,128]{4,3,2,1,0:T(8,128)(2,1)S(1)}, u32[]{:S(2)}, u32[]{:S(2)}) %all-to-all-start.2) | async-done | bytes 1572896 | tf_op jit(solution)/shard_map/all_to_all | solution.py:843
  198.5 3.6 %all-to-all-start.3 = ((bf16[8,6,8,16,128]{4,3,2,1,0:T(8,128)(2,1)}), bf16[8,6,8,16,128]{4,3,2,1,0:T(8,128)(2,1)S(1)}, u32[]{:S(2)}, u32[]{:S(2)}) async-start(bf16[8,6,8,16,128]{4,3,2,1,0:T(8,128)(2,1)} %odd_spectrum.1), calls=%async_computation.3 | async-start | bytes 3145728 | tf_op jit(solution)/shard_map/all_to_all | solution.py:843
  202.7 29.7 %analysis.2 = (bf16[6,128,1024]{2,1,0:T(8,128)(2,1)}, bf16[4,6,128,256]{3,2,1,0:T(8,128)(2,1)}) custom-call(s32[8]{0:T(128)} %get-tuple-element.61.first_ref, f32[1]{0:T(128)S(6)} %copy.34.radial_ref, bf16[8,6,8,16,128]{4,3,2,1,0:T(8,128)(2,1)} %copy-done.5, bf16[64,2,512,512]{3,2,1,0:T(8,128)(2,1)} %get-tuple-element.25.table_ref, ...), custom_call_target="tpu_custom_call" | custom-call | flops 6442450944 | bytes 41943040 | tf_op jit(solution)/shard_map/analysis/pallas_call | solution.py:598
  232.5 6.8 %all-to-all-done.3.grid_ref = bf16[8,6,8,16,128]{4,3,2,1,0:T(8,128)(2,1)S(1)} async-done(((bf16[8,6,8,16,128]{4,3,2,1,0:T(8,128)(2,1)}), bf16[8,6,8,16,128]{4,3,2,1,0:T(8,128)(2,1)S(1)}, u32[]{:S(2)}, u32[]{:S(2)}) %all-to-all-start.3) | async-done | bytes 1572896 | tf_op jit(solution)/shard_map/all_to_all | solution.py:843
  240.4 3.6 %all-to-all-start.4 = ((bf16[4,6,128,256]{3,2,1,0:T(8,128)(2,1)}), bf16[4,6,128,256]{3,2,1,0:T(8,128)(2,1)S(1)}, u32[]{:S(2)}, u32[]{:S(2)}) async-start(bf16[4,6,128,256]{3,2,1,0:T(8,128)(2,1)} %get-tuple-element.34), calls=%async_computation.4 | async-start | bytes 3145728 | tf_op jit(solution)/shard_map/all_to_all | solution.py:863
  244.0 26.2 %analysis.3 = (bf16[6,128,1024]{2,1,0:T(8,128)(2,1)}, bf16[4,6,128,256]{3,2,1,0:T(8,128)(2,1)}) custom-call(s32[8]{0:T(128)} %get-tuple-element.60.first_ref, f32[1]{0:T(128)S(6)} %copy.34.radial_ref, bf16[8,6,8,16,128]{4,3,2,1,0:T(8,128)(2,1)} %copy-done.4, bf16[64,2,512,512]{3,2,1,0:T(8,128)(2,1)} %get-tuple-element.31.table_ref, ...), custom_call_target="tpu_custom_call" | custom-call | flops 6442450944 | bytes 41943040 | tf_op jit(solution)/shard_map/analysis/pallas_call | solution.py:598
  271.4 4.6 %all-to-all-start.5 = ((bf16[4,6,128,256]{3,2,1,0:T(8,128)(2,1)}), bf16[4,6,128,256]{3,2,1,0:T(8,128)(2,1)}, u32[]{:S(2)}, u32[]{:S(2)}) async-start(bf16[4,6,128,256]{3,2,1,0:T(8,128)(2,1)} %get-tuple-element.35), calls=%async_computation.5 | async-start | bytes 3145728 | tf_op jit(solution)/shard_map/all_to_all | solution.py:863
  276.7 5.3 %natural_order.2 = bf16[6,256,1024]{2,1,0:T(8,128)(2,1)} custom-call(bf16[256,256]{1,0:T(8,128)(2,1)} %fusion.15.place_ref, bf16[6,128,1024]{2,1,0:T(8,128)(2,1)} %get-tuple-element.29.refs_0_, bf16[6,128,1024]{2,1,0:T(8,128)(2,1)} %get-tuple-element.33.refs_1_), custom_call_target="tpu_custom_call" | custom-call | flops 805306368 | bytes 8388608 | tf_op jit(solution)/shard_map/natural_order/pallas_call | solution.py:679
  282.0 5.7 %reshape.619 = bf16[6,1,128,2,1024]{4,3,2,0,1:T(2,128)(2,1)} reshape(bf16[6,256,1024]{2,1,0:T(8,128)(2,1)} %natural_order.2) | data formatting | bytes 6291456 | tf_op jit(solution)/shard_map/reshape | solution.py:878
  287.7 8.3 %all-to-all-done.5.refs_1_ = bf16[4,6,128,256]{3,2,1,0:T(8,128)(2,1)} async-done(((bf16[4,6,128,256]{3,2,1,0:T(8,128)(2,1)}), bf16[4,6,128,256]{3,2,1,0:T(8,128)(2,1)}, u32[]{:S(2)}, u32[]{:S(2)}) %all-to-all-start.5) | async-done | bytes 1572896 | tf_op jit(solution)/shard_map/all_to_all | solution.py:863
  296.0 4.8 %natural_order.3 = f32[6,256,256]{2,1,0:T(8,128)} custom-call(bf16[256,256]{1,0:T(8,128)(2,1)} %fusion.15.place_ref, bf16[4,6,128,256]{3,2,1,0:T(8,128)(2,1)} %copy-done.2, bf16[4,6,128,256]{3,2,1,0:T(8,128)(2,1)} %all-to-all-done.5.refs_1_), custom_call_target="tpu_custom_call" | custom-call | flops 201326592 | bytes 8388608 | tf_op jit(solution)/shard_map/natural_order/pallas_call | solution.py:679
  300.9 3.0 reshape.620
  (84 shorter events, 29.3 us)
Async XLA Ops:
  0.6 127.4 %copy-start = (f32[1,128,2048]{2,1,0:T(8,128)S(1)}, f32[1,128,2048]{2,1,0:T(8,128)}, u32[]{:S(2)}) copy-start(f32[1,128,2048]{2,1,0:T(8,128)} %param.6) | copy-start | bytes 3145732
  53.9 41.6 %all-to-all-start.1 = ((bf16[8,6,8,16,128]{4,3,2,1,0:T(8,128)(2,1)}), bf16[8,6,8,16,128]{4,3,2,1,0:T(8,128)(2,1)S(1)}, u32[]{:S(2)}, u32[]{:S(2)}) async-start(bf16[8,6,8,16,128]{4,3,2,1,0:T(8,128)(2,1)} %get-tuple-element.20), calls=%async_computation.1 | async-start | bytes 3145728 | tf_op jit(solution)/shard_map/all_to_all | solution.py:827
  95.4 1.2 copy-start.3
  96.6 44.6 %all-to-all-start = ((bf16[8,6,8,16,128]{4,3,2,1,0:T(8,128)(2,1)}), bf16[8,6,8,16,128]{4,3,2,1,0:T(8,128)(2,1)S(1)}, u32[]{:S(2)}, u32[]{:S(2)}) async-start(bf16[8,6,8,16,128]{4,3,2,1,0:T(8,128)(2,1)} %get-tuple-element.19), calls=%async_computation | async-start | bytes 3145728 | tf_op jit(solution)/shard_map/all_to_all | solution.py:827
  141.2 1.1 copy-start.1
  156.5 40.8 %all-to-all-start.2 = ((bf16[8,6,8,16,128]{4,3,2,1,0:T(8,128)(2,1)}), bf16[8,6,8,16,128]{4,3,2,1,0:T(8,128)(2,1)S(1)}, u32[]{:S(2)}, u32[]{:S(2)}) async-start(bf16[8,6,8,16,128]{4,3,2,1,0:T(8,128)(2,1)} %get-tuple-element.24), calls=%async_computation.2 | async-start | bytes 3145728 | tf_op jit(solution)/shard_map/all_to_all | solution.py:843
  197.3 1.1 copy-start.5
  198.5 40.8 %all-to-all-start.3 = ((bf16[8,6,8,16,128]{4,3,2,1,0:T(8,128)(2,1)}), bf16[8,6,8,16,128]{4,3,2,1,0:T(8,128)(2,1)S(1)}, u32[]{:S(2)}, u32[]{:S(2)}) async-start(bf16[8,6,8,16,128]{4,3,2,1,0:T(8,128)(2,1)} %odd_spectrum.1), calls=%async_computation.3 | async-start | bytes 3145728 | tf_op jit(solution)/shard_map/all_to_all | solution.py:843
  239.3 1.1 copy-start.4
  240.4 29.8 %all-to-all-start.4 = ((bf16[4,6,128,256]{3,2,1,0:T(8,128)(2,1)}), bf16[4,6,128,256]{3,2,1,0:T(8,128)(2,1)S(1)}, u32[]{:S(2)}, u32[]{:S(2)}) async-start(bf16[4,6,128,256]{3,2,1,0:T(8,128)(2,1)} %get-tuple-element.34), calls=%async_computation.4 | async-start | bytes 3145728 | tf_op jit(solution)/shard_map/all_to_all | solution.py:863
  270.2 1.1 copy-start.2
  271.4 24.7 %all-to-all-start.5 = ((bf16[4,6,128,256]{3,2,1,0:T(8,128)(2,1)}), bf16[4,6,128,256]{3,2,1,0:T(8,128)(2,1)}, u32[]{:S(2)}, u32[]{:S(2)}) async-start(bf16[4,6,128,256]{3,2,1,0:T(8,128)(2,1)} %get-tuple-element.35), calls=%async_computation.5 | async-start | bytes 3145728 | tf_op jit(solution)/shard_map/all_to_all | solution.py:863

commit v4 on v3

--- a/solution.py
+++ b/solution.py
@@ -33,10 +33,19 @@
     return 2.0 / cycle_count * (1.0 - 2.0 * series)
 
 
+def late_share(groups):
+    return groups // 4
+
+
 def rank_orders(orders):
-    top = orders.shape[-1]
+    groups = orders.shape[-1] // ORD
+    half, late = groups // 2, late_share(groups)
     key = orders + (orders % 2) * (1 << 20)
-    return jnp.sum((key[..., None, :] < key[..., :, None]).astype(jnp.int32), axis=-1)
+    rank = jnp.sum((key[..., None, :] < key[..., :, None]).astype(jnp.int32), axis=-1)
+    parity = (rank >= half * ORD).astype(jnp.int32)
+    group = rank // ORD - parity * half
+    early = 2 * late + parity * (half - late) + group - late
+    return jnp.where(group < late, parity * late + group, early) * ORD + rank % ORD
 
 
 def apply_rank(values, rank):
@@ -44,10 +53,6 @@
     place = jnp.arange(count, dtype=jnp.int32)
     hit = rank[..., :, None] == place
     return jnp.sum(jnp.where(hit, values[..., :, None], 0), axis=-2)
-
-
-def lane_fill(values):
-    return jnp.broadcast_to(values.reshape(-1, ORD, 1), (values.shape[0] // ORD, ORD, LANES))
 
 
 def gather_matrix():
@@ -58,11 +63,12 @@
     return (row[:, None] == degree[None, :]).astype(jnp.bfloat16)
 
 
-def degree_rows(degree_count):
-    below = jnp.arange(degree_count, dtype=jnp.float32) - 1.0
-    bottom = 4.0 * below * below - 1.0
-    rows = jnp.stack([4.0 * below * below / bottom, 4.0 / bottom])
-    return jnp.broadcast_to(rows[:, :, None], (2, degree_count, LANES))
+def fill_degrees(degree_ref):
+    row = lax.broadcasted_iota(jnp.int32, degree_ref.shape[1:], 0)
+    below = row.astype(jnp.float32) - 1.0
+    square = 4.0 * below * below
+    degree_ref[0] = square / (square - 1.0)
+    degree_ref[1] = 4.0 / (square - 1.0)
 
 
 def kappa_lanes(order):
@@ -83,17 +89,16 @@
     comps,
     groups,
     chunks,
-    sign,
+    base,
     first_ref,
     spec_ref,
     place_ref,
-    order_ref,
-    start_ref,
-    degree_ref,
+    lanes_ref,
     geometry_ref,
     out_ref,
     table_ref,
     kappa_ref,
+    degree_ref,
     sorted_ref,
     even_ref,
     odd_ref,
@@ -109,14 +114,16 @@
     rows = 2 * ORD
     half = CHUNK * ORD // 2
     lane_blocks = geometry_ref.shape[1] // LANES
+    own = place_ref[base * rows : (base + groups) * rows, :]
+    fill_degrees(degree_ref)
     for c in range(comps):
-        moved = jnp.dot(place_ref[...], spec_ref[c], preferred_element_type=jnp.float32)
+        moved = jnp.dot(own, spec_ref[c], preferred_element_type=jnp.float32)
         sorted_ref[c] = moved.astype(jnp.bfloat16)
     degrees = chunks * CHUNK
-    batch = math.gcd(groups, 4)
+    batch = next(n for n in (4, 3, 2, 1) if groups % n == 0)
 
     def fill_kappa(i, carry):
-        order = order_ref[pl.ds(i * batch, batch)].reshape(batch * ORD, LANES)
+        order = lanes_ref[0, pl.ds(base + i * batch, batch)].reshape(batch * ORD, LANES)
         kappa = kappa_lanes(jnp.concatenate([order] * (degrees // LANES), axis=1))
         kappa = kappa.reshape(batch, ORD, degrees)
         kappa_ref[pl.ds(i * batch, batch)] = kappa
@@ -130,7 +137,7 @@
     row_order = lax.broadcasted_iota(jnp.int32, shape, 0) % ORD
     lane_order = lax.broadcasted_iota(jnp.int32, shape, 1) % ORD
     mask = jnp.where(row_order == lane_order, 1.0, 0.0)
-    count = lax.fori_loop(0, groups, lambda g, n: n + chunks - first_ref[g], jnp.int32(0))
+    count = lax.fori_loop(0, groups, lambda g, n: n + chunks - first_ref[base + g], jnp.int32(0))
     even_ref[...] = jnp.zeros_like(even_ref)
     odd_ref[...] = jnp.zeros_like(odd_ref)
     wide_ref[...] = jnp.zeros_like(wide_ref)
@@ -154,7 +161,7 @@
         )
 
     def recursion(group, chunk, slot, mine):
-        order = order_ref[group]
+        order = lanes_ref[0, base + group]
         begin = chunk * CHUNK
         odd_chunk = lax.rem(chunk, LANES // CHUNK)
         lane = pl.multiple_of((chunk - odd_chunk) * CHUNK, LANES)
@@ -214,6 +221,7 @@
                 wide_ref[c * rows : (c + 1) * rows, lanes] = (moved * mask[:, lanes]).astype(jnp.bfloat16)
 
     def finish(group):
+        sign = jnp.where(group < groups // 2, 1.0, -1.0)
         for c in range(comps):
             even = even_ref[c * rows : (c + 1) * rows, :]
             odd = odd_ref[c * rows : (c + 1) * rows, :]
@@ -236,12 +244,12 @@
                 for copy in table_copies(item - SLOTS, lax.rem(item // 2, SLOTS // 2), which):
                     copy.wait()
 
-        @pl.when(chunk == first_ref[group])
+        @pl.when(chunk == first_ref[base + group])
         def _():
             prev_ref[...] = jnp.zeros_like(prev_ref)
             last_row_ref[...] = jnp.zeros_like(last_row_ref)
-            wide_order = jnp.concatenate([order_ref[group]] * lane_blocks, axis=1)
-            wide_start = jnp.concatenate([start_ref[group]] * lane_blocks, axis=1)
+            wide_order = jnp.concatenate([lanes_ref[0, base + group]] * lane_blocks, axis=1)
+            wide_start = jnp.concatenate([lanes_ref[1, base + group]] * lane_blocks, axis=1)
             log_ref[...] = wide_start + wide_order * geometry_ref[1:2, :]
 
         for parity in range(2):
@@ -262,11 +270,11 @@
 
         done = chunk == chunks - 1
         next_group = jnp.minimum(group + done.astype(jnp.int32), groups - 1)
-        next_chunk = jnp.where(done, first_ref[next_group], chunk + 1)
+        next_chunk = jnp.where(done, first_ref[base + next_group], chunk + 1)
         return group, chunk, next_group, next_chunk
 
     zero = jnp.int32(0)
-    lax.fori_loop(0, count, body, (zero, zero, zero, first_ref[0]))
+    lax.fori_loop(0, count, body, (zero, zero, zero, first_ref[base]))
     for parity in range(2):
         which = second_ref if parity else buffer_ref
 
@@ -289,7 +297,7 @@
     comps,
     groups,
     chunks,
-    sign,
+    base,
     first_ref,
     radial_ref,
     grid_ref,
@@ -311,7 +319,7 @@
     degrees = chunks * CHUNK
     lane_blocks = half_cycles // LANES
     width = found_ref.shape[1]
-    count = lax.fori_loop(0, groups, lambda g, n: n + chunks - first_ref[g], jnp.int32(0))
+    count = lax.fori_loop(0, groups, lambda g, n: n + chunks - first_ref[base + g], jnp.int32(0))
     shape = (ORD, width)
     lane = lax.broadcasted_iota(jnp.int32, shape, 1)
     own = lax.broadcasted_iota(jnp.int32, shape, 0) == lane % ORD
@@ -361,6 +369,7 @@
         return item + 1, chunk
 
     def group_body(group, item):
+        sign = jnp.where(group < groups // 2, 1.0, -1.0)
         for b in range(lane_blocks):
             lanes = slice(b * LANES, (b + 1) * LANES)
             weight = weight_ref[:, lanes]
@@ -375,7 +384,7 @@
             side_ref[1, lanes, :] = (weight * (north - south)).astype(jnp.bfloat16).T
         found_ref[...] = jnp.zeros_like(found_ref)
         item, before = lax.fori_loop(
-            first_ref[group], chunks, functools.partial(advance, group), (item, jnp.int32(chunks))
+            first_ref[base + group], chunks, functools.partial(advance, group), (item, jnp.int32(chunks))
         )
         narrow(before)
         turned = found_ref[:degrees].T.astype(jnp.float32)
@@ -393,24 +402,23 @@
     lax.fori_loop(0, groups, group_body, jnp.int32(0))
 
 
-def unsort_kernel(counts, place_ref, *refs):
+def unsort_kernel(offsets, place_ref, *refs):
     out_ref = refs[-1]
     for c in range(out_ref.shape[0]):
         found = 0.0
-        for part, ref in enumerate(refs[:-1]):
-            lanes = slice(part * counts, (part + 1) * counts)
-            found += jnp.dot(place_ref[:, lanes], ref[c], preferred_element_type=jnp.float32)
+        for offset, ref in zip(offsets, refs[:-1]):
+            place = place_ref[:, offset : offset + ref.shape[1]]
+            found += jnp.dot(place, ref[c], preferred_element_type=jnp.float32)
         out_ref[c] = found.astype(jnp.bfloat16)
 
 
-def shell_sum_kernel(counts, place_ref, *refs):
+def shell_sum_kernel(offset, place_ref, shared_ref, *refs):
     out_ref = refs[-1]
+    place = place_ref[:, offset : offset + shared_ref.shape[2]]
     for c in range(out_ref.shape[0]):
-        found = 0.0
-        for part, ref in enumerate(refs[:-1]):
-            lanes = slice(part * counts, (part + 1) * counts)
-            for n in range(ref.shape[0]):
-                found += jnp.dot(place_ref[:, lanes], ref[n, c], preferred_element_type=jnp.float32)
+        found = refs[0][c] if len(refs) > 1 else 0.0
+        for n in range(shared_ref.shape[0]):
+            found += jnp.dot(place, shared_ref[n, c], preferred_element_type=jnp.float32)
         out_ref[c] = found
 
 
@@ -462,81 +470,100 @@
     lax.fori_loop(0, 2 * count, backward_rows, 0)
 
 
-def lay_field(grid_ref, field_ref):
-    blocks, packs, groups, rows, lanes = grid_ref.shape
+def lay_field(grid_ref, field_ref, begin, end):
+    blocks, packs, _, rows, lanes = grid_ref.shape
+    count = (end - begin) * rows
     for w in range(packs):
         for d in range(blocks):
-            at = d * groups * rows
-            field_ref[at : at + groups * rows, w * lanes : (w + 1) * lanes] = grid_ref[
-                d, w
-            ].reshape(groups * rows, lanes)
-
-
-def even_field_kernel(grid_ref, forward_ref, even_ref, field_ref):
-    lay_field(grid_ref, field_ref)
+            field_ref[d * count : (d + 1) * count, w * lanes : (w + 1) * lanes] = grid_ref[
+                d, w, begin:end
+            ].reshape(count, lanes)
+
+
+def early_field_kernel(grid_ref, even_wave_ref, odd_wave_ref, out_ref, field_ref):
+    groups = grid_ref.shape[2] // 2
+    depth = field_ref.shape[1]
+    for p in range(2):
+        lay_field(grid_ref, field_ref.at[p], p * groups, (p + 1) * groups)
+
+    def step(i, carry):
+        tile = pl.ds(pl.multiple_of(i * TILE, TILE), TILE)
+        for p, wave_ref in enumerate((even_wave_ref, odd_wave_ref)):
+            out_ref[0, p, tile, :] = jnp.dot(
+                wave_ref[tile, :depth], field_ref[p], preferred_element_type=jnp.float32
+            )
+        return carry
+
+    lax.fori_loop(0, out_ref.shape[2] // TILE, step, 0)
+
+
+def lay_spectrum(norm, wave_ref, offset, stress, out_ref, begin, end):
+    blocks, packs, _, rows, lanes = out_ref.shape
+    count = (end - begin) * rows
+    batch = math.gcd(blocks, max(1, TILE // count))
+
+    def step(i, carry):
+        at = pl.multiple_of(offset + i * (batch * count), 2 * ORD)
+        found = jnp.dot(
+            wave_ref[pl.ds(at, batch * count), :], stress[...], preferred_element_type=jnp.float32
+        )
+        found = (found * norm).astype(jnp.bfloat16)
+        for n in range(batch):
+            piece = found[n * count : (n + 1) * count]
+            for w in range(packs):
+                out_ref[i * batch + n, w, begin:end] = piece[
+                    :, w * lanes : (w + 1) * lanes
+                ].reshape(end - begin, rows, lanes)
+        return carry
+
+    lax.fori_loop(0, blocks // batch, step, 0)
+
+
+def stress_kernel(norm, packs, late, early_depth, *refs):
+    refs = list(refs)
+    grid_ref = refs.pop(0) if late else None
+    early_ref, even_wave_ref, odd_wave_ref, even_back_ref, odd_back_ref, viscosity_ref = refs[:6]
+    total_ref = refs[6]
+    out_ref, field_ref = refs[7:] if late else (None, None)
+    points = even_wave_ref.shape[0]
+    for p in range(2):
+        if late:
+            lay_field(grid_ref, field_ref.at[p], p * late, (p + 1) * late)
 
     def step(i, carry):
         at = pl.multiple_of(i * TILE, TILE)
-        even_ref[0, pl.ds(at, TILE), :] = jnp.dot(
-            forward_ref[pl.ds(at, TILE), :], field_ref[...], preferred_element_type=jnp.float32
-        )
-        return carry
-
-    lax.fori_loop(0, forward_ref.shape[0] // TILE, step, 0)
-
-
-def lay_spectrum(norm, wave_ref, stress, out_ref):
-    blocks, packs, groups, rows, lanes = out_ref.shape
-    count = groups * rows
-
-    def step(d, carry):
-        at = pl.multiple_of(d * count, count)
-        found = jnp.dot(
-            wave_ref[pl.ds(at, count), :], stress[...], preferred_element_type=jnp.float32
-        )
-        found = (found * norm).astype(jnp.bfloat16)
-        for w in range(packs):
-            out_ref[d, w] = found[:, w * lanes : (w + 1) * lanes].reshape(groups, rows, lanes)
-        return carry
-
-    lax.fori_loop(0, blocks, step, 0)
-
-
-def stress_kernel(
-    norm,
-    grid_ref,
-    even_ref,
-    forward_ref,
-    backward_ref,
-    viscosity_ref,
-    out_ref,
-    difference_ref,
-    field_ref,
-    sum_ref,
-):
-    packs = grid_ref.shape[1]
-    points = forward_ref.shape[0]
-    lay_field(grid_ref, field_ref)
-
-    def step(i, carry):
-        at = pl.multiple_of(i * TILE, TILE)
-        rows = pl.ds(at, TILE)
-        even = even_ref[0, rows, :]
-        odd = jnp.dot(forward_ref[rows, :], field_ref[...], preferred_element_type=jnp.float32)
-        near = jnp.concatenate([viscosity_ref[rows, :]] * packs, axis=1)
+        tile = pl.ds(at, TILE)
+        fields = []
+        for p, wave_ref in enumerate((even_wave_ref, odd_wave_ref)):
+            field = early_ref[0, p, tile, :]
+            if late:
+                field += jnp.dot(
+                    wave_ref[tile, early_depth:], field_ref[p], preferred_element_type=jnp.float32
+                )
+            fields.append(field)
+        even, odd = fields
+        near = jnp.concatenate([viscosity_ref[tile, :]] * packs, axis=1)
         far = jnp.concatenate([viscosity_ref[pl.ds(points + at, TILE), :]] * packs, axis=1)
         near = (near * (even + odd)).astype(jnp.bfloat16).astype(jnp.float32)
         far = (far * (even - odd)).astype(jnp.bfloat16).astype(jnp.float32)
-        sum_ref[rows, :] = (near + far).astype(jnp.bfloat16)
-        difference_ref[0, rows, :] = (near - far).astype(jnp.bfloat16)
+        total_ref[0, 0, tile, :] = (near + far).astype(jnp.bfloat16)
+        total_ref[0, 1, tile, :] = (near - far).astype(jnp.bfloat16)
         return carry
 
     lax.fori_loop(0, points // TILE, step, 0)
-    lay_spectrum(norm, backward_ref, sum_ref, out_ref)
-
-
-def odd_spectrum_kernel(norm, difference_ref, backward_ref, out_ref):
-    lay_spectrum(norm, backward_ref, difference_ref.at[0], out_ref)
+    for p, back_ref in enumerate((even_back_ref, odd_back_ref)):
+        if late:
+            lay_spectrum(
+                norm, back_ref, early_depth, total_ref.at[0, p], out_ref, p * late, (p + 1) * late
+            )
+
+
+def early_spectrum_kernel(norm, total_ref, even_back_ref, odd_back_ref, out_ref):
+    groups = out_ref.shape[2] // 2
+    for p, back_ref in enumerate((even_back_ref, odd_back_ref)):
+        lay_spectrum(
+            norm, back_ref, 0, total_ref.at[0, p], out_ref, p * groups, (p + 1) * groups
+        )
 
 
 def whole(shape):
@@ -550,9 +577,8 @@
     )
 
 
-def run_synth(first, spectra, place, orders, starts, degree_table, geometry, chunks, sign):
+def run_synth(first, spectra, place, order_lanes, geometry, chunks, base, groups):
     comps, slots, degrees = spectra.shape
-    groups = orders.shape[0]
     half_cycles = geometry.shape[1]
     blocks = 2 * half_cycles // LANES
     rows = 2 * ORD
@@ -560,15 +586,16 @@
     smem = pl.BlockSpec(memory_space=pltpu.SMEM)
     vmem = pl.BlockSpec(memory_space=pltpu.VMEM)
     return pl.pallas_call(
-        functools.partial(synth_kernel, comps, groups, chunks, sign),
+        functools.partial(synth_kernel, comps, groups, chunks, base),
         out_shape=(
             jax.ShapeDtypeStruct((blocks, comps, groups, rows, LANES), jnp.bfloat16),
             jax.ShapeDtypeStruct((groups * chunks, 2, half, half_cycles), jnp.bfloat16),
             jax.ShapeDtypeStruct((groups, ORD, degrees), jnp.float32),
         ),
-        in_specs=[smem] + [vmem] * 6,
+        in_specs=[smem] + [vmem] * 4,
         out_specs=(vmem, pl.BlockSpec(memory_space=pl.ANY), vmem),
         scratch_shapes=[
+            pltpu.VMEM((2, degrees, LANES), jnp.float32),
             pltpu.VMEM((comps, groups * rows, degrees), jnp.bfloat16),
             pltpu.VMEM((comps * rows, half_cycles), jnp.float32),
             pltpu.VMEM((comps * rows, half_cycles), jnp.float32),
@@ -583,10 +610,10 @@
         ],
         name="synthesis",
         **params(groups * chunks * 2 * comps * rows * 2 * half * half_cycles, 40 << 20),
-    )(first, spectra, place, orders, starts, degree_table, geometry)
-
-
-def run_analysis(first, radial_weight, gridded, table, kappa, gather, weights, shells, sign):
+    )(first, spectra, place, order_lanes, geometry)
+
+
+def run_analysis(first, radial_weight, gridded, table, kappa, gather, weights, shells, base):
     blocks, comps, groups, rows, _ = gridded.shape
     half_cycles = weights.shape[1]
     half = CHUNK * ORD // 2
@@ -596,7 +623,7 @@
     smem = pl.BlockSpec(memory_space=pltpu.SMEM)
     vmem = pl.BlockSpec(memory_space=pltpu.VMEM)
     return pl.pallas_call(
-        functools.partial(analysis_kernel, comps, groups, chunks, sign),
+        functools.partial(analysis_kernel, comps, groups, chunks, base),
         out_shape=(
             jax.ShapeDtypeStruct((comps, groups * rows, degrees), jnp.bfloat16),
             jax.ShapeDtypeStruct((shells, comps, groups * rows, degrees // shells), jnp.bfloat16),
@@ -616,68 +643,68 @@
 
 
 def run_grid(received, forward, backward, viscosity, norm):
-    blocks, comps, groups, rows, lanes = received[0].shape
+    blocks, comps, early_groups, rows, lanes = received[0].shape
+    late_groups = received[1].shape[2] if len(received) > 1 else 0
     packs = 2 if comps % 2 == 0 else 1
     steps = comps // packs
     _, half_points, depth = forward.shape
     width = packs * lanes
-    part = pl.BlockSpec((blocks, packs, groups, rows, lanes), lambda i: (0, i, 0, 0, 0))
-    field = pl.BlockSpec((1, half_points, width), lambda i: (i, 0, 0))
+    early_depth = blocks * early_groups // 2 * rows
+
+    def part(groups):
+        return pl.BlockSpec((blocks, packs, groups, rows, lanes), lambda i: (0, i, 0, 0, 0))
 
     def wave(p, shape):
         return pl.BlockSpec((None,) + shape, lambda i: (p, 0, 0))
 
-    forward_shape, backward_shape = (half_points, depth), (depth, half_points)
-    spectrum_type = jax.ShapeDtypeStruct(received[0].shape, jnp.bfloat16)
+    fields = pl.BlockSpec((1, 2, half_points, width), lambda i: (i, 0, 0, 0))
+    fields_shape = (steps, 2, half_points, width)
+    forward_specs = [wave(p, (half_points, depth)) for p in range(2)]
+    backward_specs = [wave(p, (depth, half_points)) for p in range(2)]
     one_product = 2 * steps * width * depth * half_points
-    even = pl.pallas_call(
-        even_field_kernel,
-        out_shape=jax.ShapeDtypeStruct((steps, half_points, width), jnp.float32),
+    early_field = pl.pallas_call(
+        early_field_kernel,
+        out_shape=jax.ShapeDtypeStruct(fields_shape, jnp.float32),
         grid=(steps,),
-        in_specs=[part, wave(0, forward_shape)],
-        out_specs=field,
-        scratch_shapes=[pltpu.VMEM((depth, width), jnp.bfloat16)],
-        name="even_field",
+        in_specs=[part(early_groups)] + forward_specs,
+        out_specs=fields,
+        scratch_shapes=[pltpu.VMEM((2, early_depth, width), jnp.bfloat16)],
+        name="early_field",
         **params(one_product, 8 << 20),
-    )(received[0], forward)
-    first, difference = pl.pallas_call(
-        functools.partial(stress_kernel, norm),
-        out_shape=(
-            spectrum_type,
-            jax.ShapeDtypeStruct((steps, half_points, width), jnp.bfloat16),
-        ),
+    )(received[0], forward, forward)
+    total_type = jax.ShapeDtypeStruct(fields_shape, jnp.bfloat16)
+    late_type = [jax.ShapeDtypeStruct(piece.shape, jnp.bfloat16) for piece in received[1:]]
+    late_scratch = pltpu.VMEM((2, depth - early_depth, width), jnp.bfloat16)
+    total, *late = pl.pallas_call(
+        functools.partial(stress_kernel, norm, packs, late_groups // 2, early_depth),
+        out_shape=[total_type] + late_type,
         grid=(steps,),
-        in_specs=[
-            part,
-            field,
-            wave(1, forward_shape),
-            wave(0, backward_shape),
-            whole(viscosity.shape),
-        ],
-        out_specs=(part, field),
-        scratch_shapes=[
-            pltpu.VMEM((depth, width), jnp.bfloat16),
-            pltpu.VMEM((half_points, width), jnp.bfloat16),
-        ],
+        in_specs=[part(late_groups)] * len(late_type)
+        + [fields]
+        + forward_specs
+        + backward_specs
+        + [whole(viscosity.shape)],
+        out_specs=[fields] + [part(late_groups)] * len(late_type),
+        scratch_shapes=[late_scratch] * len(late_type),
         name="stress",
         **params(2 * one_product, 16 << 20),
-    )(received[1], even, forward, backward, viscosity)
-    second = pl.pallas_call(
-        functools.partial(odd_spectrum_kernel, norm),
-        out_shape=spectrum_type,
+    )(*received[1:], early_field, forward, forward, backward, backward, viscosity)
+    early = pl.pallas_call(
+        functools.partial(early_spectrum_kernel, norm),
+        out_shape=jax.ShapeDtypeStruct(received[0].shape, jnp.bfloat16),
         grid=(steps,),
-        in_specs=[field, wave(1, backward_shape)],
-        out_specs=part,
-        name="odd_spectrum",
+        in_specs=[fields] + backward_specs,
+        out_specs=part(early_groups),
+        name="early_spectrum",
         **params(one_product, 6 << 20),
-    )(difference, backward)
-    return [first, second]
-
-
-def run_place(kernel, place, pieces, out_shape, counts):
+    )(total, backward, backward)
+    return [early] + late
+
+
+def run_place(kernel, place, pieces, out_shape):
     vmem = pl.BlockSpec(memory_space=pltpu.VMEM)
     return pl.pallas_call(
-        functools.partial(kernel, counts),
+        kernel,
         out_shape=out_shape,
         in_specs=[vmem] * (1 + len(pieces)),
         out_specs=vmem,
@@ -687,13 +714,21 @@
 
 
 def wave_tables(sorted_all, point_count, groups):
-    blocks = sorted_all.shape[0]
     half_points = point_count // 2
-    orders = sorted_all.reshape(blocks, 2, groups // 2, 1, ORD).transpose(1, 0, 2, 3, 4)
-    shape = (2, blocks, groups // 2, 2, ORD)
+    late = late_share(groups)
+    early = groups // 2 - late
+    by_group = sorted_all.reshape(sorted_all.shape[0], groups, ORD)
+    orders = []
+    for p in range(2):
+        begin = 2 * late + p * early
+        first = by_group[:, begin : begin + early].reshape(-1, ORD)
+        second = by_group[:, p * late : (p + 1) * late].reshape(-1, ORD)
+        orders.append(jnp.concatenate([first, second], axis=0))
+    orders = jnp.stack(orders)
+    shape = (2, orders.shape[1], 2, ORD)
     depth = math.prod(shape[1:])
     shift = jnp.arange(2, dtype=jnp.int32)[:, None] * (point_count // 4)
-    lane_orders = jnp.broadcast_to(orders, shape).reshape(2, 1, depth)
+    lane_orders = jnp.broadcast_to(orders[:, :, None], shape).reshape(2, 1, depth)
     lane_shift = jnp.broadcast_to(shift, shape).reshape(2, 1, depth)
 
     def angle(phase):
@@ -786,7 +821,9 @@
     counter = jnp.arange(1, degrees, dtype=jnp.float32)
     logs = jnp.where(counter <= order[:, None], jnp.log(1.0 - 0.5 / counter), 0.0)
     starts = 0.5 * jnp.log((2.0 * order + 1.0) / (4.0 * math.pi)) + 0.5 * jnp.sum(logs, axis=1)
-    order_lanes = lane_fill(order)
+    order_lanes = jnp.broadcast_to(
+        jnp.stack([order, starts]).reshape(2, groups, ORD, 1), (2, groups, ORD, LANES)
+    )
 
     cycle_index = jnp.arange(half_cycles, dtype=jnp.float32)
     colatitude = math.pi * (2.0 * cycle_index + 1.0) / (2.0 * cycle_count)
@@ -804,24 +841,12 @@
     place_out = hit.T.astype(jnp.bfloat16)
 
     spectra = strain_spec.reshape(comps, slots * parts, degrees)
-    part_count = 2
-    part_groups = groups // part_count
-    part_rows = part_groups * 2 * ORD
-    sections = [slice(i * part_groups, (i + 1) * part_groups) for i in range(part_count)]
-    signs = [1.0 if i < part_count // 2 else -1.0 for i in range(part_count)]
-    start_lanes, degree_table = lane_fill(starts), degree_rows(degrees)
+    late = late_share(groups)
+    spans = [(2 * late, groups - 2 * late)] + ([(0, 2 * late)] if late else [])
     received, tables = [], []
-    for i, part in enumerate(sections):
+    for base, count in spans:
         gridded, table, kappa = run_synth(
-            first[part],
-            spectra,
-            place_in[i * part_rows : (i + 1) * part_rows],
-            order_lanes[part],
-            start_lanes[part],
-            degree_table,
-            geometry,
-            chunks,
-            signs[i],
+            first, spectra, place_in, order_lanes, geometry, chunks, base, count
         )
         tables.append((table, kappa))
         arrived = lax.all_to_all(to_blocks(gridded, cycle_local), "blk", 0, 0, tiled=True)
@@ -845,11 +870,13 @@
     ]
 
     shell_count = lax.axis_size("shell")
-    ordered, shared = [], []
-    for i, part in enumerate(sections):
+    ordered, offsets, integrated = [], [], []
+    sum_type = jax.ShapeDtypeStruct((comps, slots * parts, degrees // shell_count), jnp.float32)
+    for i in reversed(range(len(spans))):
+        base = spans[i][0]
         table, kappa = tables[i]
         coefs, weighted = run_analysis(
-            first[part],
+            first,
             radial_weight,
             from_blocks(returned[i], cycle_local),
             table,
@@ -857,24 +884,20 @@
             gather,
             weights,
             shell_count,
-            signs[i],
+            base,
         )
         ordered.append(coefs)
-        shared.append(lax.all_to_all(weighted, "shell", 0, 0, tiled=True))
+        offsets.append(base * 2 * ORD)
+        shared = lax.all_to_all(weighted, "shell", 0, 0, tiled=True)
+        kernel = functools.partial(shell_sum_kernel, offsets[-1])
+        integrated = [run_place(kernel, place_out, [shared] + integrated, sum_type)]
     stress = run_place(
-        unsort_kernel,
+        functools.partial(unsort_kernel, offsets),
         place_out,
         ordered,
         jax.ShapeDtypeStruct((comps, slots * parts, degrees), jnp.bfloat16),
-        part_rows,
     )
-    integrated = run_place(
-        shell_sum_kernel,
-        place_out,
-        shared,
-        jax.ShapeDtypeStruct((comps, slots * parts, degrees // shell_count), jnp.float32),
-        part_rows,
-    )
+    integrated = integrated[0]
     stress_spec = stress.reshape(strain_spec.shape)
     return (stress_spec, integrated.reshape(comps, slots, parts, degrees // shell_count))
 

time: 307 us -> 295 us (0.961)
  waiting for transfers between devices: 49.7 us -> 39 us
  local copies, waits for them, and re-layouts: 29.2 us -> 25.1 us
    all_to_all x2, waiting for transfers between devices: 35.7 us -> 31.1 us  [shards(): lax.all_to_all(unpack_comps(piece, comps, cycle_local), 'blk', 0, 0, tile...]
    all_to_all x2, waiting for transfers between devices: 8.32 us -> 4.7 us  [shards(): shared = lax.all_to_all(weighted, 'shell', 0, 0, tiled=True)]
    broadcast_in_dim x8 -> x3, local copies, waits for them, and re-layouts: 4.16 us -> 0.87 us  [the longest x1 0.77 us: shards(): jnp.broadcast_to(jnp.stack([order, starts]).reshape(2, groups, ORD, 1), (...]
    pallas_call x7 -> x8, Pallas kernels: 111 us -> 114 us  [the longest x2 71.7 us: run_synth(): pl.pallas_call(functools.partial(synth_kernel, comps, groups, chunks, bas...]
  transfers between devices with their start and end apart: 6 -> 6, of which waited for: 5 -> 4; matrix products, arithmetic and copies ran while one was open for 8% -> 8% of each run, Pallas kernels for 40% -> 47%
where the time goes in v4:
time: 295 us; the launch traced here: 294 us
  Pallas kernels  180 us (61%)
  waiting for transfers between devices  39 us (13%)
  starting transfers between devices  28.6 us (10%)
  local copies, waits for them, and re-layouts  25.1 us (9%)
  other arithmetic  17.5 us (6%)
    pallas_call x2, Pallas kernels, run_synth(): pl.pallas_call(functools.partial(synth_kernel, comps, groups, chunks, bas...  71.7 us
    pallas_call x2, Pallas kernels, run_analysis(): pl.pallas_call(functools.partial(analysis_kernel, comps, groups, chunks,...  55.9 us
    all_to_all x2, waiting for transfers between devices, shards(): lax.all_to_all(unpack_comps(piece, comps, cycle_local), 'blk', 0, 0, tile...  31.1 us
    pallas_call x1, Pallas kernels, run_grid(): pl.pallas_call(functools.partial(stress_kernel, norm, packs, late_groups...  13.9 us
    all_to_all x2, starting transfers between devices, shards(): lax.all_to_all(to_blocks(gridded, cycle_local), 'blk', 0, 0, tiled=True)  13.2 us
    pallas_call x3, Pallas kernels, run_place(): pl.pallas_call(kernel, out_shape=out_shape, in_specs=[vmem] * (1 + len(pi...  13 us
    pallas_call x1, Pallas kernels, wave_tables(): pl.pallas_call(wave_kernel, out_shape=(jax.ShapeDtypeStruct((2, half_poin...  10.7 us
    all_to_all x2, starting transfers between devices, shards(): shared = lax.all_to_all(weighted, 'shell', 0, 0, tiled=True)  8.12 us
  transfers between devices with their start and end apart: 6, of which 4 were waited for; matrix products, arithmetic and copies ran while one was open for 8% of the time, Pallas kernels for 47%

profile of v4, /device:TPU:0, one launch (start us, length us, event | category | flops | bytes accessed | tf_op | source)
XLA Modules:
  0.0 294.0 jit_solution(13932024923410229123)
XLA Ops:
  6.5 5.7 %reshape.629.spec_ref = bf16[6,256,1024]{2,1,0:T(8,128)(2,1)} reshape(bf16[6,1,128,2,1024]{4,3,2,1,0:T(2,128)(2,1)} %param.4) | data formatting | bytes 6291456 | tf_op jit(solution)/shard_map/reshape | solution.py:843
  14.3 25.4 %synthesis.3 = (bf16[8,6,8,16,128]{4,3,2,1,0:T(8,128)(2,1)}, bf16[64,2,512,512]{3,2,1,0:T(8,128)(2,1)}, f32[8,8,1024]{2,1,0:T(8,128)}) custom-call(s32[16]{0:T(128)} %and_select_fusion.1.first_ref, bf16[6,256,1024]{2,1,0:T(8,128)(2,1)} %reshape.629.spec_ref, bf16[256,256]{1,0:T(8,128)(2,1)} %select_convert_fusion.place_ref, ...), custom_call_target="tpu_custom_call" | custom-call | flops 6442450944 | bytes 41943040 | tf_op jit(solution)/shard_map/synthesis/pallas_call | solution.py:588
  39.7 6.6 %all-to-all-start.1 = ((bf16[8,6,8,16,128]{4,3,2,1,0:T(8,128)(2,1)}), bf16[8,6,8,16,128]{4,3,2,1,0:T(8,128)(2,1)S(1)}, u32[]{:S(2)}, u32[]{:S(2)}) async-start(bf16[8,6,8,16,128]{4,3,2,1,0:T(8,128)(2,1)} %get-tuple-element.20), calls=%async_computation.1 | async-start | bytes 3145728 | tf_op jit(solution)/shard_map/all_to_all | solution.py:852
  47.4 46.3 %synthesis.2 = (bf16[8,6,8,16,128]{4,3,2,1,0:T(8,128)(2,1)}, bf16[64,2,512,512]{3,2,1,0:T(8,128)(2,1)}, f32[8,8,1024]{2,1,0:T(8,128)}) custom-call(s32[16]{0:T(128)} %and_select_fusion.1.first_ref, bf16[6,256,1024]{2,1,0:T(8,128)(2,1)} %reshape.629.spec_ref, bf16[256,256]{1,0:T(8,128)(2,1)} %select_convert_fusion.place_ref, ...), custom_call_target="tpu_custom_call" | custom-call | flops 6442450944 | bytes 41943040 | tf_op jit(solution)/shard_map/synthesis/pallas_call | solution.py:588
  94.8 6.7 %all-to-all-start = ((bf16[8,6,8,16,128]{4,3,2,1,0:T(8,128)(2,1)}), bf16[8,6,8,16,128]{4,3,2,1,0:T(8,128)(2,1)S(1)}, u32[]{:S(2)}, u32[]{:S(2)}) async-start(bf16[8,6,8,16,128]{4,3,2,1,0:T(8,128)(2,1)} %get-tuple-element.19), calls=%async_computation | async-start | bytes 3145728 | tf_op jit(solution)/shard_map/all_to_all | solution.py:852
  108.6 10.7 %waves.1 = (bf16[2,1024,1024]{2,1,0:T(8,128)(2,1)}, bf16[2,1024,1024]{2,1,0:T(8,128)(2,1)}) custom-call(f32[2,2,8,1024]{3,2,1,0:T(8,128)} %pad_maximum_fusion.1.forward_base, f32[2,2,1,1024]{3,2,1,0:T(1,128)} %pad_maximum_fusion.2.forward_turn, f32[2,2,64,8,128]{4,3,2,1,0:T(8,128)} %pad_maximum_fusion.backward_base, ...), custom_call_target="tpu_custom_call" | custom-call | flops 8388608 | bytes 12582912 | tf_op jit(solution)/shard_map/waves/pallas_call | solution.py:750
  119.2 4.4 %fusion.6 = f32[512]{0:T(512)S(1)} fusion(f32[512]{0:T(512)S(1)} %fusion.53, s32[512]{0:T(512)S(1)} %get-tuple-element.72, s32[512]{0:T(512)S(1)} %get-tuple-element.73), kind=kLoop, calls=%fused_computation.13 | loop fusion | flops 4193792 | bytes 8192 | tf_op jit(solution)/shard_map/reduce_sum | solution.py:32
  127.0 7.8 %early_field.1.refs_1_ = f32[3,2,1024,256]{3,2,1,0:T(8,128)} custom-call(bf16[8,6,8,16,128]{4,3,2,1,0:T(8,128)(2,1)} %copy-done.3, bf16[2,1024,1024]{2,1,0:T(8,128)(2,1)} %get-tuple-element.22.even_wave_ref.odd_wave_ref.refs_2_.refs_3_, bf16[2,1024,1024]{2,1,0:T(8,128)(2,1)} %get-tuple-element.22.even_wave_ref.odd_wave_ref.refs_2_.refs_3_), custom_call_target="tpu_custom_call" | custom-call | flops 1610612736 | bytes 8388608 | tf_op jit(solution)/shard_map/early_field/pallas_call | solution.py:665
  134.8 3.1 %all-to-all-done.refs_0_ = bf16[8,6,8,16,128]{4,3,2,1,0:T(8,128)(2,1)S(1)} async-done(((bf16[8,6,8,16,128]{4,3,2,1,0:T(8,128)(2,1)}), bf16[8,6,8,16,128]{4,3,2,1,0:T(8,128)(2,1)S(1)}, u32[]{:S(2)}, u32[]{:S(2)}) %all-to-all-start) | async-done | bytes 1572896 | tf_op jit(solution)/shard_map/all_to_all | solution.py:852
  139.1 13.9 %stress.1 = (bf16[3,2,1024,256]{3,2,1,0:T(8,128)(2,1)}, bf16[8,6,8,16,128]{4,3,2,1,0:T(8,128)(2,1)}) custom-call(bf16[8,6,8,16,128]{4,3,2,1,0:T(8,128)(2,1)} %copy-done.1, f32[3,2,1024,256]{3,2,1,0:T(8,128)} %early_field.1.refs_1_, bf16[2,1024,1024]{2,1,0:T(8,128)(2,1)} %get-tuple-element.22.even_wave_ref.odd_wave_ref.refs_2_.refs_3_, ...), custom_call_target="tpu_custom_call" | custom-call | flops 3221225472 | bytes 16777216 | tf_op jit(solution)/shard_map/stress/pallas_call | solution.py:678
  152.9 3.6 %all-to-all-start.2 = ((bf16[8,6,8,16,128]{4,3,2,1,0:T(8,128)(2,1)}), bf16[8,6,8,16,128]{4,3,2,1,0:T(8,128)(2,1)S(1)}, u32[]{:S(2)}, u32[]{:S(2)}) async-start(bf16[8,6,8,16,128]{4,3,2,1,0:T(8,128)(2,1)} %get-tuple-element.24), calls=%async_computation.2 | async-start | bytes 3145728 | tf_op jit(solution)/shard_map/all_to_all | solution.py:868
  156.6 7.3 %early_spectrum.1 = bf16[8,6,8,16,128]{4,3,2,1,0:T(8,128)(2,1)} custom-call(bf16[3,2,1024,256]{3,2,1,0:T(8,128)(2,1)} %get-tuple-element.30.total_ref, bf16[2,1024,1024]{2,1,0:T(8,128)(2,1)} %get-tuple-element.23.refs_4_.refs_5_.even_back_ref.odd_back_ref, bf16[2,1024,1024]{2,1,0:T(8,128)(2,1)} %get-tuple-element.23.refs_4_.refs_5_.even_back_ref.odd_back_ref), custom_call_target="tpu_custom_call" | custom-call | flops 1610612736 | bytes 6291456 | tf_op jit(solution)/shard_map/early_spectrum/pallas_call | solution.py:692
  163.9 29.9 %all-to-all-done.2.grid_ref = bf16[8,6,8,16,128]{4,3,2,1,0:T(8,128)(2,1)S(1)} async-done(((bf16[8,6,8,16,128]{4,3,2,1,0:T(8,128)(2,1)}), bf16[8,6,8,16,128]{4,3,2,1,0:T(8,128)(2,1)S(1)}, u32[]{:S(2)}, u32[]{:S(2)}) %all-to-all-start.2) | async-done | bytes 1572896 | tf_op jit(solution)/shard_map/all_to_all | solution.py:868
  194.9 3.6 %all-to-all-start.3 = ((bf16[8,6,8,16,128]{4,3,2,1,0:T(8,128)(2,1)}), bf16[8,6,8,16,128]{4,3,2,1,0:T(8,128)(2,1)S(1)}, u32[]{:S(2)}, u32[]{:S(2)}) async-start(bf16[8,6,8,16,128]{4,3,2,1,0:T(8,128)(2,1)} %early_spectrum.1), calls=%async_computation.3 | async-start | bytes 3145728 | tf_op jit(solution)/shard_map/all_to_all | solution.py:868
  199.2 35.3 %analysis.2 = (bf16[6,128,1024]{2,1,0:T(8,128)(2,1)}, bf16[4,6,128,256]{3,2,1,0:T(8,128)(2,1)}) custom-call(s32[16]{0:T(128)} %and_select_fusion.1.first_ref, f32[1]{0:T(128)S(6)} %copy.42.radial_ref, bf16[8,6,8,16,128]{4,3,2,1,0:T(8,128)(2,1)} %copy-done.5, bf16[64,2,512,512]{3,2,1,0:T(8,128)(2,1)} %get-tuple-element.25.table_ref, ...), custom_call_target="tpu_custom_call" | custom-call | flops 6442450944 | bytes 41943040 | tf_op jit(solution)/shard_map/analysis/pallas_call | solution.py:625
  236.9 3.6 %all-to-all-start.5 = ((bf16[4,6,128,256]{3,2,1,0:T(8,128)(2,1)}), bf16[4,6,128,256]{3,2,1,0:T(8,128)(2,1)S(1)}, u32[]{:S(2)}, u32[]{:S(2)}) async-start(bf16[4,6,128,256]{3,2,1,0:T(8,128)(2,1)} %get-tuple-element.35), calls=%async_computation.5 | async-start | bytes 3145728 | tf_op jit(solution)/shard_map/all_to_all | solution.py:891
  240.4 20.7 %analysis.3 = (bf16[6,128,1024]{2,1,0:T(8,128)(2,1)}, bf16[4,6,128,256]{3,2,1,0:T(8,128)(2,1)}) custom-call(s32[16]{0:T(128)} %and_select_fusion.1.first_ref, f32[1]{0:T(128)S(6)} %copy.42.radial_ref, bf16[8,6,8,16,128]{4,3,2,1,0:T(8,128)(2,1)} %copy-done.4, bf16[64,2,512,512]{3,2,1,0:T(8,128)(2,1)} %get-tuple-element.31.table_ref, ...), custom_call_target="tpu_custom_call" | custom-call | flops 6442450944 | bytes 41943040 | tf_op jit(solution)/shard_map/analysis/pallas_call | solution.py:625
  262.3 4.6 %all-to-all-start.4 = ((bf16[4,6,128,256]{3,2,1,0:T(8,128)(2,1)}), bf16[4,6,128,256]{3,2,1,0:T(8,128)(2,1)}, u32[]{:S(2)}, u32[]{:S(2)}) async-start(bf16[4,6,128,256]{3,2,1,0:T(8,128)(2,1)} %get-tuple-element.34), calls=%async_computation.4 | async-start | bytes 3145728 | tf_op jit(solution)/shard_map/all_to_all | solution.py:891
  267.6 5.3 %natural_order.3 = bf16[6,256,1024]{2,1,0:T(8,128)(2,1)} custom-call(bf16[256,256]{1,0:T(8,128)(2,1)} %fusion.15.place_ref, bf16[6,128,1024]{2,1,0:T(8,128)(2,1)} %get-tuple-element.29.refs_0_, bf16[6,128,1024]{2,1,0:T(8,128)(2,1)} %get-tuple-element.33.refs_1_), custom_call_target="tpu_custom_call" | custom-call | flops 805306368 | bytes 8388608 | tf_op jit(solution)/shard_map/natural_order/pallas_call | solution.py:706
  272.9 5.7 %reshape.635 = bf16[6,1,128,2,1024]{4,3,2,0,1:T(2,128)(2,1)} reshape(bf16[6,256,1024]{2,1,0:T(8,128)(2,1)} %natural_order.3) | data formatting | bytes 6291456 | tf_op jit(solution)/shard_map/reshape | solution.py:901
  278.6 3.6 %natural_order.4.refs_0_ = f32[6,256,256]{2,1,0:T(8,128)} custom-call(bf16[256,256]{1,0:T(8,128)(2,1)} %fusion.15.place_ref, bf16[4,6,128,256]{3,2,1,0:T(8,128)(2,1)} %copy-done.2), custom_call_target="tpu_custom_call" | custom-call | flops 201326592 | bytes 8388608 | tf_op jit(solution)/shard_map/natural_order/pallas_call | solution.py:706
  282.2 4.7 %all-to-all-done.4.shared_ref = bf16[4,6,128,256]{3,2,1,0:T(8,128)(2,1)} async-done(((bf16[4,6,128,256]{3,2,1,0:T(8,128)(2,1)}), bf16[4,6,128,256]{3,2,1,0:T(8,128)(2,1)}, u32[]{:S(2)}, u32[]{:S(2)}) %all-to-all-start.4) | async-done | bytes 1572896 | tf_op jit(solution)/shard_map/all_to_all | solution.py:891
  286.9 4.0 %natural_order.5 = f32[6,256,256]{2,1,0:T(8,128)} custom-call(bf16[256,256]{1,0:T(8,128)(2,1)} %fusion.15.place_ref, bf16[4,6,128,256]{3,2,1,0:T(8,128)(2,1)} %all-to-all-done.4.shared_ref, f32[6,256,256]{2,1,0:T(8,128)} %natural_order.4.refs_0_), custom_call_target="tpu_custom_call" | custom-call | flops 201326592 | bytes 8388608 | tf_op jit(solution)/shard_map/natural_order/pallas_call | solution.py:706
  291.0 3.0 %reshape.636 = f32[6,128,2,256]{3,2,1,0:T(2,128)} reshape(f32[6,256,256]{2,1,0:T(8,128)} %natural_order.5) | data formatting | bytes 3145728 | tf_op jit(solution)/shard_map/reshape | solution.py:902
  (78 shorter events, 27.0 us)
Async XLA Ops:
  0.6 124.4 %copy-start = (f32[1,128,2048]{2,1,0:T(8,128)S(1)}, f32[1,128,2048]{2,1,0:T(8,128)}, u32[]{:S(2)}) copy-start(f32[1,128,2048]{2,1,0:T(8,128)} %param.6) | copy-start | bytes 3145732
  39.7 53.9 %all-to-all-start.1 = ((bf16[8,6,8,16,128]{4,3,2,1,0:T(8,128)(2,1)}), bf16[8,6,8,16,128]{4,3,2,1,0:T(8,128)(2,1)S(1)}, u32[]{:S(2)}, u32[]{:S(2)}) async-start(bf16[8,6,8,16,128]{4,3,2,1,0:T(8,128)(2,1)} %get-tuple-element.20), calls=%async_computation.1 | async-start | bytes 3145728 | tf_op jit(solution)/shard_map/all_to_all | solution.py:852
  93.7 1.1 copy-start.3
  94.8 43.1 %all-to-all-start = ((bf16[8,6,8,16,128]{4,3,2,1,0:T(8,128)(2,1)}), bf16[8,6,8,16,128]{4,3,2,1,0:T(8,128)(2,1)S(1)}, u32[]{:S(2)}, u32[]{:S(2)}) async-start(bf16[8,6,8,16,128]{4,3,2,1,0:T(8,128)(2,1)} %get-tuple-element.19), calls=%async_computation | async-start | bytes 3145728 | tf_op jit(solution)/shard_map/all_to_all | solution.py:852
  137.9 1.1 copy-start.1
  152.9 40.8 %all-to-all-start.2 = ((bf16[8,6,8,16,128]{4,3,2,1,0:T(8,128)(2,1)}), bf16[8,6,8,16,128]{4,3,2,1,0:T(8,128)(2,1)S(1)}, u32[]{:S(2)}, u32[]{:S(2)}) async-start(bf16[8,6,8,16,128]{4,3,2,1,0:T(8,128)(2,1)} %get-tuple-element.24), calls=%async_computation.2 | async-start | bytes 3145728 | tf_op jit(solution)/shard_map/all_to_all | solution.py:868
  193.8 1.1 copy-start.5
  194.9 40.8 %all-to-all-start.3 = ((bf16[8,6,8,16,128]{4,3,2,1,0:T(8,128)(2,1)}), bf16[8,6,8,16,128]{4,3,2,1,0:T(8,128)(2,1)S(1)}, u32[]{:S(2)}, u32[]{:S(2)}) async-start(bf16[8,6,8,16,128]{4,3,2,1,0:T(8,128)(2,1)} %early_spectrum.1), calls=%async_computation.3 | async-start | bytes 3145728 | tf_op jit(solution)/shard_map/all_to_all | solution.py:868
  235.7 1.1 copy-start.4
  236.9 24.3 %all-to-all-start.5 = ((bf16[4,6,128,256]{3,2,1,0:T(8,128)(2,1)}), bf16[4,6,128,256]{3,2,1,0:T(8,128)(2,1)S(1)}, u32[]{:S(2)}, u32[]{:S(2)}) async-start(bf16[4,6,128,256]{3,2,1,0:T(8,128)(2,1)} %get-tuple-element.35), calls=%async_computation.5 | async-start | bytes 3145728 | tf_op jit(solution)/shard_map/all_to_all | solution.py:891
  261.1 1.1 copy-start.2
  262.3 24.7 %all-to-all-start.4 = ((bf16[4,6,128,256]{3,2,1,0:T(8,128)(2,1)}), bf16[4,6,128,256]{3,2,1,0:T(8,128)(2,1)}, u32[]{:S(2)}, u32[]{:S(2)}) async-start(bf16[4,6,128,256]{3,2,1,0:T(8,128)(2,1)} %get-tuple-element.34), calls=%async_computation.4 | async-start | bytes 3145728 | tf_op jit(solution)/shard_map/all_to_all | solution.py:891

commit v5 on v4

--- a/solution.py
+++ b/solution.py
@@ -18,7 +18,7 @@
 LANES = 128
 TILE = 256
 SLOTS = 4
-VMEM_LIMIT = 56 * 1024 * 1024
+VMEM_LIMIT = 63 * 1024 * 1024
 
 
 def fejer_weights(cycle_count):
@@ -160,7 +160,7 @@
             wide_ref[:, half:], other[before, 1], preferred_element_type=jnp.float32
         )
 
-    def recursion(group, chunk, slot, mine):
+    def recursion(seeded, group, chunk, slot, mine):
         order = lanes_ref[0, base + group]
         begin = chunk * CHUNK
         odd_chunk = lax.rem(chunk, LANES // CHUNK)
@@ -181,7 +181,8 @@
                 two = degree_ref[1, pl.ds(begin + step, 1), :]
                 coef = jnp.concatenate([one - two * square] * lane_blocks, axis=1)
                 now = twice * last - coef * prev
-                now = jnp.where(seed_at == float(step), 1.0, now)
+                if seeded:
+                    now = jnp.where(seed_at == float(step), 1.0, now)
                 held.append(now * scale)
                 prev, last = last, now
             for p in range(2):
@@ -252,17 +253,20 @@
             wide_start = jnp.concatenate([lanes_ref[1, base + group]] * lane_blocks, axis=1)
             log_ref[...] = wide_start + wide_order * geometry_ref[1:2, :]
 
+        seeded = chunk <= first_ref[first_ref.shape[0] // 2 + base + group]
         for parity in range(2):
-
-            @pl.when(lax.rem(item, 2) == parity)
-            def _(parity=parity):
-                mine, other = (buffer_ref, second_ref) if parity == 0 else (second_ref, buffer_ref)
-                place = lax.rem(item // 2, SLOTS // 2)
-                before = lax.rem((item + SLOTS - 1) // 2, SLOTS // 2)
-                products(other, before)
-                recursion(group, chunk, place, mine)
-                for copy in table_copies(item, place, mine):
-                    copy.start()
+            mine, other = (buffer_ref, second_ref) if parity == 0 else (second_ref, buffer_ref)
+            place = lax.rem(item // 2, SLOTS // 2)
+            before = lax.rem((item + SLOTS - 1) // 2, SLOTS // 2)
+            turn = lax.rem(item, 2) == parity
+            for want in (True, False):
+
+                @pl.when(jnp.logical_and(turn, seeded if want else jnp.logical_not(seeded)))
+                def _(mine=mine, other=other, want=want):
+                    products(other, before)
+                    recursion(want, group, chunk, place, mine)
+                    for copy in table_copies(item, place, mine):
+                        copy.start()
 
         @pl.when(jnp.logical_and(before_chunk == chunks - 1, item > 0))
         def _():
@@ -816,7 +820,7 @@
     rank = lax.dynamic_index_in_dim(rank_all, block, 0, keepdims=False)
     sorted_orders = lax.dynamic_index_in_dim(sorted_all, block, 0, keepdims=False)
     by_group = sorted_orders.reshape(groups, ORD)
-    first = by_group[:, 0] // CHUNK
+    first = jnp.concatenate([by_group[:, 0], by_group[:, -1]]) // CHUNK
     order = sorted_orders.astype(jnp.float32)
     counter = jnp.arange(1, degrees, dtype=jnp.float32)
     logs = jnp.where(counter <= order[:, None], jnp.log(1.0 - 0.5 / counter), 0.0)

time: 295 us -> 290 us (0.983)
  local copies, waits for them, and re-layouts: 25.1 us -> 19.4 us
  starting transfers between devices: 28.6 us -> 33 us
  Pallas kernels: 180 us -> 176 us
    unnamed x12 -> x0, local copies, waits for them, and re-layouts: 5.71 us -> none
    pallas_call x2, Pallas kernels: 71.7 us -> 68.6 us  [run_synth(): pl.pallas_call(functools.partial(synth_kernel, comps, groups, chunks, bas...]
where the time goes in v5:
time: 290 us; the launch traced here: 289 us
  Pallas kernels  176 us (61%)
  waiting for transfers between devices  38 us (13%)
  starting transfers between devices  33 us (11%)
  local copies, waits for them, and re-layouts  19.4 us (7%)
  other arithmetic  17.5 us (6%)
  matrix products  3.25 us (1%)
    pallas_call x2, Pallas kernels, run_synth(): pl.pallas_call(functools.partial(synth_kernel, comps, groups, chunks, bas...  68.6 us
    pallas_call x2, Pallas kernels, run_analysis(): pl.pallas_call(functools.partial(analysis_kernel, comps, groups, chunks,...  55 us
    all_to_all x2, waiting for transfers between devices, shards(): lax.all_to_all(unpack_comps(piece, comps, cycle_local), 'blk', 0, 0, tile...  29.3 us
    all_to_all x2, starting transfers between devices, shards(): lax.all_to_all(to_blocks(gridded, cycle_local), 'blk', 0, 0, tiled=True)  15.5 us
    pallas_call x1, Pallas kernels, run_grid(): pl.pallas_call(functools.partial(stress_kernel, norm, packs, late_groups...  13.8 us
    pallas_call x3, Pallas kernels, run_place(): pl.pallas_call(kernel, out_shape=out_shape, in_specs=[vmem] * (1 + len(pi...  13 us
    pallas_call x1, Pallas kernels, wave_tables(): pl.pallas_call(wave_kernel, out_shape=(jax.ShapeDtypeStruct((2, half_poin...  10.7 us
    all_to_all x2, starting transfers between devices, shards(): shared = lax.all_to_all(weighted, 'shell', 0, 0, tiled=True)  8.92 us
  transfers between devices with their start and end apart: 6, of which 4 were waited for; matrix products, arithmetic and copies ran while one was open for 8% of the time, Pallas kernels for 47%

profile of v5, /device:TPU:0, one launch (start us, length us, event | category | flops | bytes accessed | tf_op | source)
XLA Modules:
  0.0 288.8 jit_solution(13904647056102898804)
XLA Ops:
  6.0 5.7 %reshape.629.spec_ref = bf16[6,256,1024]{2,1,0:T(8,128)(2,1)} reshape(bf16[6,1,128,2,1024]{4,3,2,1,0:T(2,128)(2,1)} %param.4) | data formatting | bytes 6291456 | tf_op jit(solution)/shard_map/reshape | solution.py:847
  14.3 21.6 %synthesis.3 = (bf16[8,6,8,16,128]{4,3,2,1,0:T(8,128)(2,1)}, bf16[64,2,512,512]{3,2,1,0:T(8,128)(2,1)}, f32[8,8,1024]{2,1,0:T(8,128)}) custom-call(s32[32]{0:T(128)} %and_select_fusion.1.first_ref, bf16[6,256,1024]{2,1,0:T(8,128)(2,1)} %reshape.629.spec_ref, bf16[256,256]{1,0:T(8,128)(2,1)} %select_convert_fusion.place_ref, ...), custom_call_target="tpu_custom_call" | custom-call | flops 6442450944 | bytes 41943040 | tf_op jit(solution)/shard_map/synthesis/pallas_call | solution.py:592
  36.0 10.9 %all-to-all-start.1 = ((bf16[8,6,8,16,128]{4,3,2,1,0:T(8,128)(2,1)}), bf16[8,6,8,16,128]{4,3,2,1,0:T(8,128)(2,1)}, u32[]{:S(2)}, u32[]{:S(2)}) async-start(bf16[8,6,8,16,128]{4,3,2,1,0:T(8,128)(2,1)} %get-tuple-element.20), calls=%async_computation.1 | async-start | bytes 3145728 | tf_op jit(solution)/shard_map/all_to_all | solution.py:856
  48.0 47.0 %synthesis.2 = (bf16[8,6,8,16,128]{4,3,2,1,0:T(8,128)(2,1)}, bf16[64,2,512,512]{3,2,1,0:T(8,128)(2,1)}, f32[8,8,1024]{2,1,0:T(8,128)}) custom-call(s32[32]{0:T(128)} %and_select_fusion.1.first_ref, bf16[6,256,1024]{2,1,0:T(8,128)(2,1)} %reshape.629.spec_ref, bf16[256,256]{1,0:T(8,128)(2,1)} %select_convert_fusion.place_ref, ...), custom_call_target="tpu_custom_call" | custom-call | flops 6442450944 | bytes 41943040 | tf_op jit(solution)/shard_map/synthesis/pallas_call | solution.py:592
  95.0 4.6 %all-to-all-start = ((bf16[8,6,8,16,128]{4,3,2,1,0:T(8,128)(2,1)}), bf16[8,6,8,16,128]{4,3,2,1,0:T(8,128)(2,1)}, u32[]{:S(2)}, u32[]{:S(2)}) async-start(bf16[8,6,8,16,128]{4,3,2,1,0:T(8,128)(2,1)} %get-tuple-element.19), calls=%async_computation | async-start | bytes 3145728 | tf_op jit(solution)/shard_map/all_to_all | solution.py:856
  106.6 10.7 %waves.1 = (bf16[2,1024,1024]{2,1,0:T(8,128)(2,1)}, bf16[2,1024,1024]{2,1,0:T(8,128)(2,1)}) custom-call(f32[2,2,8,1024]{3,2,1,0:T(8,128)} %pad_maximum_fusion.1.forward_base, f32[2,2,1,1024]{3,2,1,0:T(1,128)} %pad_maximum_fusion.2.forward_turn, f32[2,2,64,8,128]{4,3,2,1,0:T(8,128)} %pad_maximum_fusion.backward_base, ...), custom_call_target="tpu_custom_call" | custom-call | flops 8388608 | bytes 12582912 | tf_op jit(solution)/shard_map/waves/pallas_call | solution.py:754
  117.3 4.4 %fusion.6 = f32[512]{0:T(512)S(1)} fusion(f32[512]{0:T(512)S(1)} %fusion.53, s32[512]{0:T(512)S(1)} %get-tuple-element.74, s32[512]{0:T(512)S(1)} %get-tuple-element.75), kind=kLoop, calls=%fused_computation.13 | loop fusion | flops 4193792 | bytes 8192 | tf_op jit(solution)/shard_map/reduce_sum | solution.py:32
  123.1 3.2 %convolution_bitcast_fusion.refs_6_ = f32[2048,128]{1,0:T(8,128)} fusion(f32[1,128,2048]{2,1,0:T(8,128)} %param.6, s32[128]{0:T(128)S(1)} %broadcast_select_fusion), kind=kOutput, calls=%fused_computation | convolution fusion | flops 402669568 | bytes 2097664 | tf_op jit(solution)/shard_map/jk,ji->ki/dot_general | solution.py:866
  126.3 7.8 %early_field.1.refs_1_ = f32[3,2,1024,256]{3,2,1,0:T(8,128)} custom-call(bf16[8,6,8,16,128]{4,3,2,1,0:T(8,128)(2,1)} %all-to-all-done.1.grid_ref, bf16[2,1024,1024]{2,1,0:T(8,128)(2,1)} %get-tuple-element.22.even_wave_ref.odd_wave_ref.refs_2_.refs_3_, bf16[2,1024,1024]{2,1,0:T(8,128)(2,1)} %get-tuple-element.22.even_wave_ref.odd_wave_ref.refs_2_.refs_3_), custom_call_target="tpu_custom_call" | custom-call | flops 1610612736 | bytes 8388608 | tf_op jit(solution)/shard_map/early_field/pallas_call | solution.py:669
  136.3 13.8 %stress.1 = (bf16[3,2,1024,256]{3,2,1,0:T(8,128)(2,1)}, bf16[8,6,8,16,128]{4,3,2,1,0:T(8,128)(2,1)}) custom-call(bf16[8,6,8,16,128]{4,3,2,1,0:T(8,128)(2,1)} %all-to-all-done.refs_0_, f32[3,2,1024,256]{3,2,1,0:T(8,128)} %early_field.1.refs_1_, bf16[2,1024,1024]{2,1,0:T(8,128)(2,1)} %get-tuple-element.22.even_wave_ref.odd_wave_ref.refs_2_.refs_3_, ...), custom_call_target="tpu_custom_call" | custom-call | flops 3221225472 | bytes 16777216 | tf_op jit(solution)/shard_map/stress/pallas_call | solution.py:682
  150.1 4.3 %all-to-all-start.2 = ((bf16[8,6,8,16,128]{4,3,2,1,0:T(8,128)(2,1)}), bf16[8,6,8,16,128]{4,3,2,1,0:T(8,128)(2,1)}, u32[]{:S(2)}, u32[]{:S(2)}) async-start(bf16[8,6,8,16,128]{4,3,2,1,0:T(8,128)(2,1)} %get-tuple-element.24), calls=%async_computation.2 | async-start | bytes 3145728 | tf_op jit(solution)/shard_map/all_to_all | solution.py:872
  154.4 7.3 %early_spectrum.1 = bf16[8,6,8,16,128]{4,3,2,1,0:T(8,128)(2,1)} custom-call(bf16[3,2,1024,256]{3,2,1,0:T(8,128)(2,1)} %get-tuple-element.30.total_ref, bf16[2,1024,1024]{2,1,0:T(8,128)(2,1)} %get-tuple-element.23.refs_4_.refs_5_.even_back_ref.odd_back_ref, bf16[2,1024,1024]{2,1,0:T(8,128)(2,1)} %get-tuple-element.23.refs_4_.refs_5_.even_back_ref.odd_back_ref), custom_call_target="tpu_custom_call" | custom-call | flops 1610612736 | bytes 6291456 | tf_op jit(solution)/shard_map/early_spectrum/pallas_call | solution.py:696
  161.7 29.3 %all-to-all-done.2.grid_ref = bf16[8,6,8,16,128]{4,3,2,1,0:T(8,128)(2,1)} async-done(((bf16[8,6,8,16,128]{4,3,2,1,0:T(8,128)(2,1)}), bf16[8,6,8,16,128]{4,3,2,1,0:T(8,128)(2,1)}, u32[]{:S(2)}, u32[]{:S(2)}) %all-to-all-start.2) | async-done | bytes 1572896 | tf_op jit(solution)/shard_map/all_to_all | solution.py:872
  191.0 4.3 %all-to-all-start.3 = ((bf16[8,6,8,16,128]{4,3,2,1,0:T(8,128)(2,1)}), bf16[8,6,8,16,128]{4,3,2,1,0:T(8,128)(2,1)}, u32[]{:S(2)}, u32[]{:S(2)}) async-start(bf16[8,6,8,16,128]{4,3,2,1,0:T(8,128)(2,1)} %early_spectrum.1), calls=%async_computation.3 | async-start | bytes 3145728 | tf_op jit(solution)/shard_map/all_to_all | solution.py:872
  196.0 36.8 %analysis.2 = (bf16[6,128,1024]{2,1,0:T(8,128)(2,1)}, bf16[4,6,128,256]{3,2,1,0:T(8,128)(2,1)}) custom-call(s32[32]{0:T(128)} %and_select_fusion.1.first_ref, f32[1]{0:T(128)S(6)} %copy.42.radial_ref, bf16[8,6,8,16,128]{4,3,2,1,0:T(8,128)(2,1)} %all-to-all-done.2.grid_ref, bf16[64,2,512,512]{3,2,1,0:T(8,128)(2,1)} %get-tuple-element.25.table_ref, ...), custom_call_target="tpu_custom_call" | custom-call | flops 6442450944 | bytes 41943040 | tf_op jit(solution)/shard_map/analysis/pallas_call | solution.py:629
  232.8 4.4 %all-to-all-start.5 = ((bf16[4,6,128,256]{3,2,1,0:T(8,128)(2,1)}), bf16[4,6,128,256]{3,2,1,0:T(8,128)(2,1)}, u32[]{:S(2)}, u32[]{:S(2)}) async-start(bf16[4,6,128,256]{3,2,1,0:T(8,128)(2,1)} %get-tuple-element.35), calls=%async_computation.5 | async-start | bytes 3145728 | tf_op jit(solution)/shard_map/all_to_all | solution.py:895
  237.1 18.2 %analysis.3 = (bf16[6,128,1024]{2,1,0:T(8,128)(2,1)}, bf16[4,6,128,256]{3,2,1,0:T(8,128)(2,1)}) custom-call(s32[32]{0:T(128)} %and_select_fusion.1.first_ref, f32[1]{0:T(128)S(6)} %copy.42.radial_ref, bf16[8,6,8,16,128]{4,3,2,1,0:T(8,128)(2,1)} %all-to-all-done.3.grid_ref, bf16[64,2,512,512]{3,2,1,0:T(8,128)(2,1)} %get-tuple-element.31.table_ref, ...), custom_call_target="tpu_custom_call" | custom-call | flops 6442450944 | bytes 41943040 | tf_op jit(solution)/shard_map/analysis/pallas_call | solution.py:629
  257.3 4.6 %all-to-all-start.4 = ((bf16[4,6,128,256]{3,2,1,0:T(8,128)(2,1)}), bf16[4,6,128,256]{3,2,1,0:T(8,128)(2,1)}, u32[]{:S(2)}, u32[]{:S(2)}) async-start(bf16[4,6,128,256]{3,2,1,0:T(8,128)(2,1)} %get-tuple-element.34), calls=%async_computation.4 | async-start | bytes 3145728 | tf_op jit(solution)/shard_map/all_to_all | solution.py:895
  262.6 5.3 %natural_order.3 = bf16[6,256,1024]{2,1,0:T(8,128)(2,1)} custom-call(bf16[256,256]{1,0:T(8,128)(2,1)} %fusion.15.place_ref, bf16[6,128,1024]{2,1,0:T(8,128)(2,1)} %get-tuple-element.29.refs_0_, bf16[6,128,1024]{2,1,0:T(8,128)(2,1)} %get-tuple-element.33.refs_1_), custom_call_target="tpu_custom_call" | custom-call | flops 805306368 | bytes 8388608 | tf_op jit(solution)/shard_map/natural_order/pallas_call | solution.py:710
  267.9 5.7 %reshape.635 = bf16[6,1,128,2,1024]{4,3,2,0,1:T(2,128)(2,1)} reshape(bf16[6,256,1024]{2,1,0:T(8,128)(2,1)} %natural_order.3) | data formatting | bytes 6291456 | tf_op jit(solution)/shard_map/reshape | solution.py:905
  273.6 3.6 %natural_order.4.refs_0_ = f32[6,256,256]{2,1,0:T(8,128)} custom-call(bf16[256,256]{1,0:T(8,128)(2,1)} %fusion.15.place_ref, bf16[4,6,128,256]{3,2,1,0:T(8,128)(2,1)} %all-to-all-done.5.shared_ref), custom_call_target="tpu_custom_call" | custom-call | flops 201326592 | bytes 8388608 | tf_op jit(solution)/shard_map/natural_order/pallas_call | solution.py:710
  277.2 4.6 %all-to-all-done.4.shared_ref = bf16[4,6,128,256]{3,2,1,0:T(8,128)(2,1)} async-done(((bf16[4,6,128,256]{3,2,1,0:T(8,128)(2,1)}), bf16[4,6,128,256]{3,2,1,0:T(8,128)(2,1)}, u32[]{:S(2)}, u32[]{:S(2)}) %all-to-all-start.4) | async-done | bytes 1572896 | tf_op jit(solution)/shard_map/all_to_all | solution.py:895
  281.8 4.0 %natural_order.5 = f32[6,256,256]{2,1,0:T(8,128)} custom-call(bf16[256,256]{1,0:T(8,128)(2,1)} %fusion.15.place_ref, bf16[4,6,128,256]{3,2,1,0:T(8,128)(2,1)} %all-to-all-done.4.shared_ref, f32[6,256,256]{2,1,0:T(8,128)} %natural_order.4.refs_0_), custom_call_target="tpu_custom_call" | custom-call | flops 201326592 | bytes 8388608 | tf_op jit(solution)/shard_map/natural_order/pallas_call | solution.py:710
  285.8 3.0 %reshape.636 = f32[6,128,2,256]{3,2,1,0:T(2,128)} reshape(f32[6,256,256]{2,1,0:T(8,128)} %natural_order.5) | data formatting | bytes 3145728 | tf_op jit(solution)/shard_map/reshape | solution.py:906
  (66 shorter events, 22.2 us)
Async XLA Ops:
  36.0 59.0 %all-to-all-start.1 = ((bf16[8,6,8,16,128]{4,3,2,1,0:T(8,128)(2,1)}), bf16[8,6,8,16,128]{4,3,2,1,0:T(8,128)(2,1)}, u32[]{:S(2)}, u32[]{:S(2)}) async-start(bf16[8,6,8,16,128]{4,3,2,1,0:T(8,128)(2,1)} %get-tuple-element.20), calls=%async_computation.1 | async-start | bytes 3145728 | tf_op jit(solution)/shard_map/all_to_all | solution.py:856
  95.0 41.3 %all-to-all-start = ((bf16[8,6,8,16,128]{4,3,2,1,0:T(8,128)(2,1)}), bf16[8,6,8,16,128]{4,3,2,1,0:T(8,128)(2,1)}, u32[]{:S(2)}, u32[]{:S(2)}) async-start(bf16[8,6,8,16,128]{4,3,2,1,0:T(8,128)(2,1)} %get-tuple-element.19), calls=%async_computation | async-start | bytes 3145728 | tf_op jit(solution)/shard_map/all_to_all | solution.py:856
  150.1 40.9 %all-to-all-start.2 = ((bf16[8,6,8,16,128]{4,3,2,1,0:T(8,128)(2,1)}), bf16[8,6,8,16,128]{4,3,2,1,0:T(8,128)(2,1)}, u32[]{:S(2)}, u32[]{:S(2)}) async-start(bf16[8,6,8,16,128]{4,3,2,1,0:T(8,128)(2,1)} %get-tuple-element.24), calls=%async_computation.2 | async-start | bytes 3145728 | tf_op jit(solution)/shard_map/all_to_all | solution.py:872
  191.0 41.7 %all-to-all-start.3 = ((bf16[8,6,8,16,128]{4,3,2,1,0:T(8,128)(2,1)}), bf16[8,6,8,16,128]{4,3,2,1,0:T(8,128)(2,1)}, u32[]{:S(2)}, u32[]{:S(2)}) async-start(bf16[8,6,8,16,128]{4,3,2,1,0:T(8,128)(2,1)} %early_spectrum.1), calls=%async_computation.3 | async-start | bytes 3145728 | tf_op jit(solution)/shard_map/all_to_all | solution.py:872
  232.8 24.5 %all-to-all-start.5 = ((bf16[4,6,128,256]{3,2,1,0:T(8,128)(2,1)}), bf16[4,6,128,256]{3,2,1,0:T(8,128)(2,1)}, u32[]{:S(2)}, u32[]{:S(2)}) async-start(bf16[4,6,128,256]{3,2,1,0:T(8,128)(2,1)} %get-tuple-element.35), calls=%async_computation.5 | async-start | bytes 3145728 | tf_op jit(solution)/shard_map/all_to_all | solution.py:895
  257.3 24.5 %all-to-all-start.4 = ((bf16[4,6,128,256]{3,2,1,0:T(8,128)(2,1)}), bf16[4,6,128,256]{3,2,1,0:T(8,128)(2,1)}, u32[]{:S(2)}, u32[]{:S(2)}) async-start(bf16[4,6,128,256]{3,2,1,0:T(8,128)(2,1)} %get-tuple-element.34), calls=%async_computation.4 | async-start | bytes 3145728 | tf_op jit(solution)/shard_map/all_to_all | solution.py:895

commit v6 on v5

--- a/solution.py
+++ b/solution.py
@@ -16,7 +16,7 @@
 CHUNK = 128
 BLOCK = 16
 LANES = 128
-TILE = 256
+TILE = 512
 SLOTS = 4
 VMEM_LIMIT = 63 * 1024 * 1024
 

time: 290 us -> 288 us (level)
  Pallas kernels: 176 us -> 173 us
  transfers between devices with their start and end apart: 6 -> 6, of which waited for: 4 -> 4; matrix products, arithmetic and copies ran while one was open for 8% -> 8% of each run, Pallas kernels for 47% -> 46%
where the time goes in v6:
time: 288 us; the launch traced here: 287 us
  Pallas kernels  173 us (60%)
  waiting for transfers between devices  38.5 us (13%)
  starting transfers between devices  34.2 us (12%)
  local copies, waits for them, and re-layouts  19.4 us (7%)
  other arithmetic  17.5 us (6%)
  matrix products  3.25 us (1%)
    pallas_call x2, Pallas kernels, run_synth(): pl.pallas_call(functools.partial(synth_kernel, comps, groups, chunks, bas...  69.5 us
    pallas_call x2, Pallas kernels, run_analysis(): pl.pallas_call(functools.partial(analysis_kernel, comps, groups, chunks,...  55.5 us
    all_to_all x2, waiting for transfers between devices, shards(): lax.all_to_all(unpack_comps(piece, comps, cycle_local), 'blk', 0, 0, tile...  31.1 us
    all_to_all x2, starting transfers between devices, shards(): lax.all_to_all(to_blocks(gridded, cycle_local), 'blk', 0, 0, tiled=True)  16.7 us
    pallas_call x3, Pallas kernels, run_place(): pl.pallas_call(kernel, out_shape=out_shape, in_specs=[vmem] * (1 + len(pi...  13 us
    pallas_call x1, Pallas kernels, run_grid(): pl.pallas_call(functools.partial(stress_kernel, norm, packs, late_groups...  10.9 us
    pallas_call x1, Pallas kernels, wave_tables(): pl.pallas_call(wave_kernel, out_shape=(jax.ShapeDtypeStruct((2, half_poin...  10.7 us
    all_to_all x2, starting transfers between devices, shards(): shared = lax.all_to_all(weighted, 'shell', 0, 0, tiled=True)  8.92 us
  transfers between devices with their start and end apart: 6, of which 4 were waited for; matrix products, arithmetic and copies ran while one was open for 8% of the time, Pallas kernels for 46%

profile of v6, /device:TPU:0, one launch (start us, length us, event | category | flops | bytes accessed | tf_op | source)
XLA Modules:
  0.0 287.4 jit_solution(10884078734724196139)
XLA Ops:
  6.0 5.7 %reshape.629.spec_ref = bf16[6,256,1024]{2,1,0:T(8,128)(2,1)} reshape(bf16[6,1,128,2,1024]{4,3,2,1,0:T(2,128)(2,1)} %param.4) | data formatting | bytes 6291456 | tf_op jit(solution)/shard_map/reshape | solution.py:847
  14.3 24.5 %synthesis.3 = (bf16[8,6,8,16,128]{4,3,2,1,0:T(8,128)(2,1)}, bf16[64,2,512,512]{3,2,1,0:T(8,128)(2,1)}, f32[8,8,1024]{2,1,0:T(8,128)}) custom-call(s32[32]{0:T(128)} %and_select_fusion.1.first_ref, bf16[6,256,1024]{2,1,0:T(8,128)(2,1)} %reshape.629.spec_ref, bf16[256,256]{1,0:T(8,128)(2,1)} %select_convert_fusion.place_ref, ...), custom_call_target="tpu_custom_call" | custom-call | flops 6442450944 | bytes 41943040 | tf_op jit(solution)/shard_map/synthesis/pallas_call | solution.py:592
  38.8 10.1 %all-to-all-start.1 = ((bf16[8,6,8,16,128]{4,3,2,1,0:T(8,128)(2,1)}), bf16[8,6,8,16,128]{4,3,2,1,0:T(8,128)(2,1)}, u32[]{:S(2)}, u32[]{:S(2)}) async-start(bf16[8,6,8,16,128]{4,3,2,1,0:T(8,128)(2,1)} %get-tuple-element.20), calls=%async_computation.1 | async-start | bytes 3145728 | tf_op jit(solution)/shard_map/all_to_all | solution.py:856
  50.0 45.1 %synthesis.2 = (bf16[8,6,8,16,128]{4,3,2,1,0:T(8,128)(2,1)}, bf16[64,2,512,512]{3,2,1,0:T(8,128)(2,1)}, f32[8,8,1024]{2,1,0:T(8,128)}) custom-call(s32[32]{0:T(128)} %and_select_fusion.1.first_ref, bf16[6,256,1024]{2,1,0:T(8,128)(2,1)} %reshape.629.spec_ref, bf16[256,256]{1,0:T(8,128)(2,1)} %select_convert_fusion.place_ref, ...), custom_call_target="tpu_custom_call" | custom-call | flops 6442450944 | bytes 41943040 | tf_op jit(solution)/shard_map/synthesis/pallas_call | solution.py:592
  95.1 6.6 %all-to-all-start = ((bf16[8,6,8,16,128]{4,3,2,1,0:T(8,128)(2,1)}), bf16[8,6,8,16,128]{4,3,2,1,0:T(8,128)(2,1)}, u32[]{:S(2)}, u32[]{:S(2)}) async-start(bf16[8,6,8,16,128]{4,3,2,1,0:T(8,128)(2,1)} %get-tuple-element.19), calls=%async_computation | async-start | bytes 3145728 | tf_op jit(solution)/shard_map/all_to_all | solution.py:856
  108.7 10.7 %waves.1 = (bf16[2,1024,1024]{2,1,0:T(8,128)(2,1)}, bf16[2,1024,1024]{2,1,0:T(8,128)(2,1)}) custom-call(f32[2,2,8,1024]{3,2,1,0:T(8,128)} %pad_maximum_fusion.1.forward_base, f32[2,2,1,1024]{3,2,1,0:T(1,128)} %pad_maximum_fusion.2.forward_turn, f32[2,2,64,8,128]{4,3,2,1,0:T(8,128)} %pad_maximum_fusion.backward_base, ...), custom_call_target="tpu_custom_call" | custom-call | flops 8388608 | bytes 12582912 | tf_op jit(solution)/shard_map/waves/pallas_call | solution.py:754
  119.4 4.4 %fusion.6 = f32[512]{0:T(512)S(1)} fusion(f32[512]{0:T(512)S(1)} %fusion.53, s32[512]{0:T(512)S(1)} %get-tuple-element.74, s32[512]{0:T(512)S(1)} %get-tuple-element.75), kind=kLoop, calls=%fused_computation.13 | loop fusion | flops 4193792 | bytes 8192 | tf_op jit(solution)/shard_map/reduce_sum | solution.py:32
  125.2 3.2 %convolution_bitcast_fusion.refs_6_ = f32[2048,128]{1,0:T(8,128)} fusion(f32[1,128,2048]{2,1,0:T(8,128)} %param.6, s32[128]{0:T(128)S(1)} %broadcast_select_fusion), kind=kOutput, calls=%fused_computation | convolution fusion | flops 402669568 | bytes 2097664 | tf_op jit(solution)/shard_map/jk,ji->ki/dot_general | solution.py:866
  128.4 7.1 %early_field.1.refs_1_ = f32[3,2,1024,256]{3,2,1,0:T(8,128)} custom-call(bf16[8,6,8,16,128]{4,3,2,1,0:T(8,128)(2,1)} %all-to-all-done.1.grid_ref, bf16[2,1024,1024]{2,1,0:T(8,128)(2,1)} %get-tuple-element.22.even_wave_ref.odd_wave_ref.refs_2_.refs_3_, bf16[2,1024,1024]{2,1,0:T(8,128)(2,1)} %get-tuple-element.22.even_wave_ref.odd_wave_ref.refs_2_.refs_3_), custom_call_target="tpu_custom_call" | custom-call | flops 1610612736 | bytes 8388608 | tf_op jit(solution)/shard_map/early_field/pallas_call | solution.py:669
  138.2 10.9 %stress.1 = (bf16[3,2,1024,256]{3,2,1,0:T(8,128)(2,1)}, bf16[8,6,8,16,128]{4,3,2,1,0:T(8,128)(2,1)}) custom-call(bf16[8,6,8,16,128]{4,3,2,1,0:T(8,128)(2,1)} %all-to-all-done.refs_0_, f32[3,2,1024,256]{3,2,1,0:T(8,128)} %early_field.1.refs_1_, bf16[2,1024,1024]{2,1,0:T(8,128)(2,1)} %get-tuple-element.22.even_wave_ref.odd_wave_ref.refs_2_.refs_3_, ...), custom_call_target="tpu_custom_call" | custom-call | flops 3221225472 | bytes 16777216 | tf_op jit(solution)/shard_map/stress/pallas_call | solution.py:682
  149.1 4.3 %all-to-all-start.2 = ((bf16[8,6,8,16,128]{4,3,2,1,0:T(8,128)(2,1)}), bf16[8,6,8,16,128]{4,3,2,1,0:T(8,128)(2,1)}, u32[]{:S(2)}, u32[]{:S(2)}) async-start(bf16[8,6,8,16,128]{4,3,2,1,0:T(8,128)(2,1)} %get-tuple-element.24), calls=%async_computation.2 | async-start | bytes 3145728 | tf_op jit(solution)/shard_map/all_to_all | solution.py:872
  153.4 6.3 %early_spectrum.1 = bf16[8,6,8,16,128]{4,3,2,1,0:T(8,128)(2,1)} custom-call(bf16[3,2,1024,256]{3,2,1,0:T(8,128)(2,1)} %get-tuple-element.30.total_ref, bf16[2,1024,1024]{2,1,0:T(8,128)(2,1)} %get-tuple-element.23.refs_4_.refs_5_.even_back_ref.odd_back_ref, bf16[2,1024,1024]{2,1,0:T(8,128)(2,1)} %get-tuple-element.23.refs_4_.refs_5_.even_back_ref.odd_back_ref), custom_call_target="tpu_custom_call" | custom-call | flops 1610612736 | bytes 6291456 | tf_op jit(solution)/shard_map/early_spectrum/pallas_call | solution.py:696
  159.7 30.3 %all-to-all-done.2.grid_ref = bf16[8,6,8,16,128]{4,3,2,1,0:T(8,128)(2,1)} async-done(((bf16[8,6,8,16,128]{4,3,2,1,0:T(8,128)(2,1)}), bf16[8,6,8,16,128]{4,3,2,1,0:T(8,128)(2,1)}, u32[]{:S(2)}, u32[]{:S(2)}) %all-to-all-start.2) | async-done | bytes 1572896 | tf_op jit(solution)/shard_map/all_to_all | solution.py:872
  190.1 4.3 %all-to-all-start.3 = ((bf16[8,6,8,16,128]{4,3,2,1,0:T(8,128)(2,1)}), bf16[8,6,8,16,128]{4,3,2,1,0:T(8,128)(2,1)}, u32[]{:S(2)}, u32[]{:S(2)}) async-start(bf16[8,6,8,16,128]{4,3,2,1,0:T(8,128)(2,1)} %early_spectrum.1), calls=%async_computation.3 | async-start | bytes 3145728 | tf_op jit(solution)/shard_map/all_to_all | solution.py:872
  195.0 35.2 %analysis.2 = (bf16[6,128,1024]{2,1,0:T(8,128)(2,1)}, bf16[4,6,128,256]{3,2,1,0:T(8,128)(2,1)}) custom-call(s32[32]{0:T(128)} %and_select_fusion.1.first_ref, f32[1]{0:T(128)S(6)} %copy.42.radial_ref, bf16[8,6,8,16,128]{4,3,2,1,0:T(8,128)(2,1)} %all-to-all-done.2.grid_ref, bf16[64,2,512,512]{3,2,1,0:T(8,128)(2,1)} %get-tuple-element.25.table_ref, ...), custom_call_target="tpu_custom_call" | custom-call | flops 6442450944 | bytes 41943040 | tf_op jit(solution)/shard_map/analysis/pallas_call | solution.py:629
  231.0 4.3 %all-to-all-start.5 = ((bf16[4,6,128,256]{3,2,1,0:T(8,128)(2,1)}), bf16[4,6,128,256]{3,2,1,0:T(8,128)(2,1)}, u32[]{:S(2)}, u32[]{:S(2)}) async-start(bf16[4,6,128,256]{3,2,1,0:T(8,128)(2,1)} %get-tuple-element.35), calls=%async_computation.5 | async-start | bytes 3145728 | tf_op jit(solution)/shard_map/all_to_all | solution.py:895
  235.4 20.2 %analysis.3 = (bf16[6,128,1024]{2,1,0:T(8,128)(2,1)}, bf16[4,6,128,256]{3,2,1,0:T(8,128)(2,1)}) custom-call(s32[32]{0:T(128)} %and_select_fusion.1.first_ref, f32[1]{0:T(128)S(6)} %copy.42.radial_ref, bf16[8,6,8,16,128]{4,3,2,1,0:T(8,128)(2,1)} %all-to-all-done.3.grid_ref, bf16[64,2,512,512]{3,2,1,0:T(8,128)(2,1)} %get-tuple-element.31.table_ref, ...), custom_call_target="tpu_custom_call" | custom-call | flops 6442450944 | bytes 41943040 | tf_op jit(solution)/shard_map/analysis/pallas_call | solution.py:629
  255.6 4.6 %all-to-all-start.4 = ((bf16[4,6,128,256]{3,2,1,0:T(8,128)(2,1)}), bf16[4,6,128,256]{3,2,1,0:T(8,128)(2,1)}, u32[]{:S(2)}, u32[]{:S(2)}) async-start(bf16[4,6,128,256]{3,2,1,0:T(8,128)(2,1)} %get-tuple-element.34), calls=%async_computation.4 | async-start | bytes 3145728 | tf_op jit(solution)/shard_map/all_to_all | solution.py:895
  260.9 5.3 %natural_order.3 = bf16[6,256,1024]{2,1,0:T(8,128)(2,1)} custom-call(bf16[256,256]{1,0:T(8,128)(2,1)} %fusion.15.place_ref, bf16[6,128,1024]{2,1,0:T(8,128)(2,1)} %get-tuple-element.29.refs_0_, bf16[6,128,1024]{2,1,0:T(8,128)(2,1)} %get-tuple-element.33.refs_1_), custom_call_target="tpu_custom_call" | custom-call | flops 805306368 | bytes 8388608 | tf_op jit(solution)/shard_map/natural_order/pallas_call | solution.py:710
  266.3 5.7 %reshape.635 = bf16[6,1,128,2,1024]{4,3,2,0,1:T(2,128)(2,1)} reshape(bf16[6,256,1024]{2,1,0:T(8,128)(2,1)} %natural_order.3) | data formatting | bytes 6291456 | tf_op jit(solution)/shard_map/reshape | solution.py:905
  272.0 3.6 %natural_order.4.refs_0_ = f32[6,256,256]{2,1,0:T(8,128)} custom-call(bf16[256,256]{1,0:T(8,128)(2,1)} %fusion.15.place_ref, bf16[4,6,128,256]{3,2,1,0:T(8,128)(2,1)} %all-to-all-done.5.shared_ref), custom_call_target="tpu_custom_call" | custom-call | flops 201326592 | bytes 8388608 | tf_op jit(solution)/shard_map/natural_order/pallas_call | solution.py:710
  275.6 4.7 %all-to-all-done.4.shared_ref = bf16[4,6,128,256]{3,2,1,0:T(8,128)(2,1)} async-done(((bf16[4,6,128,256]{3,2,1,0:T(8,128)(2,1)}), bf16[4,6,128,256]{3,2,1,0:T(8,128)(2,1)}, u32[]{:S(2)}, u32[]{:S(2)}) %all-to-all-start.4) | async-done | bytes 1572896 | tf_op jit(solution)/shard_map/all_to_all | solution.py:895
  280.3 4.0 %natural_order.5 = f32[6,256,256]{2,1,0:T(8,128)} custom-call(bf16[256,256]{1,0:T(8,128)(2,1)} %fusion.15.place_ref, bf16[4,6,128,256]{3,2,1,0:T(8,128)(2,1)} %all-to-all-done.4.shared_ref, f32[6,256,256]{2,1,0:T(8,128)} %natural_order.4.refs_0_), custom_call_target="tpu_custom_call" | custom-call | flops 201326592 | bytes 8388608 | tf_op jit(solution)/shard_map/natural_order/pallas_call | solution.py:710
  284.4 3.0 %reshape.636 = f32[6,128,2,256]{3,2,1,0:T(2,128)} reshape(f32[6,256,256]{2,1,0:T(8,128)} %natural_order.5) | data formatting | bytes 3145728 | tf_op jit(solution)/shard_map/reshape | solution.py:906
  (66 shorter events, 21.5 us)
Async XLA Ops:
  38.8 56.3 %all-to-all-start.1 = ((bf16[8,6,8,16,128]{4,3,2,1,0:T(8,128)(2,1)}), bf16[8,6,8,16,128]{4,3,2,1,0:T(8,128)(2,1)}, u32[]{:S(2)}, u32[]{:S(2)}) async-start(bf16[8,6,8,16,128]{4,3,2,1,0:T(8,128)(2,1)} %get-tuple-element.20), calls=%async_computation.1 | async-start | bytes 3145728 | tf_op jit(solution)/shard_map/all_to_all | solution.py:856
  95.1 43.1 %all-to-all-start = ((bf16[8,6,8,16,128]{4,3,2,1,0:T(8,128)(2,1)}), bf16[8,6,8,16,128]{4,3,2,1,0:T(8,128)(2,1)}, u32[]{:S(2)}, u32[]{:S(2)}) async-start(bf16[8,6,8,16,128]{4,3,2,1,0:T(8,128)(2,1)} %get-tuple-element.19), calls=%async_computation | async-start | bytes 3145728 | tf_op jit(solution)/shard_map/all_to_all | solution.py:856
  149.1 40.9 %all-to-all-start.2 = ((bf16[8,6,8,16,128]{4,3,2,1,0:T(8,128)(2,1)}), bf16[8,6,8,16,128]{4,3,2,1,0:T(8,128)(2,1)}, u32[]{:S(2)}, u32[]{:S(2)}) async-start(bf16[8,6,8,16,128]{4,3,2,1,0:T(8,128)(2,1)} %get-tuple-element.24), calls=%async_computation.2 | async-start | bytes 3145728 | tf_op jit(solution)/shard_map/all_to_all | solution.py:872
  190.1 40.9 %all-to-all-start.3 = ((bf16[8,6,8,16,128]{4,3,2,1,0:T(8,128)(2,1)}), bf16[8,6,8,16,128]{4,3,2,1,0:T(8,128)(2,1)}, u32[]{:S(2)}, u32[]{:S(2)}) async-start(bf16[8,6,8,16,128]{4,3,2,1,0:T(8,128)(2,1)} %early_spectrum.1), calls=%async_computation.3 | async-start | bytes 3145728 | tf_op jit(solution)/shard_map/all_to_all | solution.py:872
  231.0 24.6 %all-to-all-start.5 = ((bf16[4,6,128,256]{3,2,1,0:T(8,128)(2,1)}), bf16[4,6,128,256]{3,2,1,0:T(8,128)(2,1)}, u32[]{:S(2)}, u32[]{:S(2)}) async-start(bf16[4,6,128,256]{3,2,1,0:T(8,128)(2,1)} %get-tuple-element.35), calls=%async_computation.5 | async-start | bytes 3145728 | tf_op jit(solution)/shard_map/all_to_all | solution.py:895
  255.6 24.7 %all-to-all-start.4 = ((bf16[4,6,128,256]{3,2,1,0:T(8,128)(2,1)}), bf16[4,6,128,256]{3,2,1,0:T(8,128)(2,1)}, u32[]{:S(2)}, u32[]{:S(2)}) async-start(bf16[4,6,128,256]{3,2,1,0:T(8,128)(2,1)} %get-tuple-element.34), calls=%async_computation.4 | async-start | bytes 3145728 | tf_op jit(solution)/shard_map/all_to_all | solution.py:895
